TPU v7x, 128 devices: a whole 4x4x4 slice. The times are simulated.
128 devices in a mesh: col: 4 (over z), sec: 32 (over y, x, core).
Axes of the slice: x: 4, y: 4, z: 4, core: 2. Of those that a mesh axis runs over, the one named last changes fastest.
Arguments:
- site_tensor: float32 [512, 32, 1536], P('col', 'sec')
- left_env: float32 [32, 5, 512, 512], P('sec'), as said below
- right_env: float32 [32, 5, 512, 512], P('sec', None, None, 'col'), as said below
- bond_env: float32 [32, 5, 512, 512], P('sec'), as said below
- sector_sizes: int32 [32], P('sec'), may hold values from 1 to 512, as said below
Outputs:
- evolved_site: float32 [512, 32, 1536], P('col', 'sec')
- evolved_bond: float32 [512, 32, 512], P('col', 'sec')
Inputs may be any that keep to these rules, and one draw needn't show every extreme that they name: `sector_sizes`: the sizes sum to 8192. Every tensor and environment block is zero outside the live states of its sectors. For a in 0, 1, 4 the blocks left_env[t, a] are symmetric, and left_env[t, 3] is the transpose of left_env[t - 1, 2] (zero for t = 0). `right_env`: same structure as left_env. `bond_env`: same structure as left_env.
All inputs are finite; a program needn't handle non-finite values.
Results may differ from a plain program's by a relative error of at most 0.0003.
Values sent between devices are 32-bit elements; how exact they have to be, the bound alone decides.
No kernel may reach another device: no remote copies, remote signals or barrier semaphores. Data moves between devices by JAX's collectives and lax.ppermute only.
A program may use at most 192 MiB of HBM per device.

v0:
```python
import math

import jax
import jax.numpy as jnp
from jax import lax
from jax.sharding import PartitionSpec as P

KRYLOV = 4


HIGH_PREC = lax.Precision.HIGHEST
SECTOR_SHIFT = (0, 0, 1, -1, 0)
ROOT_TWO = math.sqrt(2.0)
ANISOTROPY = 0.5
TIME_STEP = 0.1
ONE_SITE_TERMS = (
    (0, 0, 0, 0, 1.0),
    (0, 0, 1, 1, 1.0),
    (0, 0, 2, 2, 1.0),
    (1, 0, 0, 0, 1.0),
    (1, 0, 2, 2, -1.0),
    (2, 0, 0, 1, ROOT_TWO),
    (2, 0, 1, 2, ROOT_TWO),
    (3, 0, 1, 0, ROOT_TWO),
    (3, 0, 2, 1, ROOT_TWO),
    (4, 0, 0, 0, ANISOTROPY),
    (4, 0, 2, 2, ANISOTROPY),
    (4, 1, 0, 0, 1.0),
    (4, 1, 2, 2, -1.0),
    (4, 2, 1, 0, ROOT_TWO / 2),
    (4, 2, 2, 1, ROOT_TWO / 2),
    (4, 3, 0, 1, ROOT_TWO / 2),
    (4, 3, 1, 2, ROOT_TWO / 2),
    (4, 4, 0, 0, 1.0),
    (4, 4, 1, 1, 1.0),
    (4, 4, 2, 2, 1.0),
)
ZERO_SITE_TERMS = (
    (0, 0, 0, 0, 1.0),
    (1, 1, 0, 0, 1.0),
    (2, 2, 0, 0, 1.0),
    (3, 3, 0, 0, 1.0),
    (4, 4, 0, 0, 1.0),
)


def with_halo(block, sides, width):
    for axis, dim in sides:
        count = lax.axis_size(axis)
        forward = [(i, i + 1) for i in range(count - 1)]
        backward = [(target, source) for source, target in forward]
        low = lax.ppermute(
            lax.slice_in_dim(block, block.shape[dim] - width, None, axis=dim), axis, forward
        )
        high = lax.ppermute(lax.slice_in_dim(block, 0, width, axis=dim), axis, backward)
        block = jnp.concatenate([low, block, high], axis=dim)
    return block


def small_exp(matrix):
    dimension = matrix.shape[0]
    identity = jnp.eye(dimension, dtype=jnp.float32)
    scaled = matrix / 16.0
    result = identity
    for degree in range(8, 0, -1):
        result = identity + jnp.dot(scaled, result, precision=HIGH_PREC) / degree
    for squaring in range(4):
        result = jnp.dot(result, result, precision=HIGH_PREC)
    return result


def tridiagonal(alpha_list, beta_list):
    diagonal_part = jnp.diag(jnp.stack(alpha_list))
    upper_part = jnp.diag(jnp.stack(beta_list), 1)
    return diagonal_part + upper_part + upper_part.T


def apply_left(fetch_block, left_of, term_list, spin_count, wanted):
    columns = []
    for spin_out in range(spin_count):
        summed = None
        for a, b, spin_row, spin_in, factor in term_list:
            if spin_row == spin_out and b in wanted:
                product = factor * jnp.einsum(
                    "rtk,tlk->rtl",
                    fetch_block(b, spin_in),
                    left_of(a, spin_out),
                    precision=HIGH_PREC,
                )
                summed = product if summed is None else summed + product
        if summed is None:
            summed = jnp.zeros_like(fetch_block(0, spin_out))
        columns.append(summed)
    return jnp.concatenate(columns, axis=2)


def apply_ham(vector, spin_count, left_of, term_list, right_env):
    col_rows = vector.shape[0]
    sectors_here = vector.shape[1]
    block_size = vector.shape[2] // spin_count
    widened = with_halo(vector, (("sec", 1),), 1)

    def source(which_b, spin_in):
        lowest = 1 + SECTOR_SHIFT[which_b]
        return widened[
            :, lowest : lowest + sectors_here, spin_in * block_size : (spin_in + 1) * block_size
        ]

    stacked = jnp.stack(
        [apply_left(source, left_of, term_list, spin_count, (b,)) for b in range(5)]
    )
    panel = lax.slice_in_dim(right_env, 0, lax.axis_size("col") * col_rows, axis=2)
    return lax.psum_scatter(
        jnp.einsum("tbrc,bctx->rtx", panel, stacked, precision=HIGH_PREC),
        "col",
        scatter_dimension=0,
        tiled=True,
    )


def evolve(start, apply_fn, sign):
    first_sum = lax.psum(jnp.sum(start * start), ("col", "sec"))
    norm_zero = jnp.sqrt(first_sum)
    krylov_basis = [start / norm_zero]
    alpha_list = []
    beta_list = []
    for krylov_step in range(KRYLOV):
        image = apply_fn(krylov_basis[krylov_step])
        if krylov_step > 0:
            image = image - beta_list[krylov_step - 1] * krylov_basis[krylov_step - 1]
        alpha_now = lax.psum(jnp.sum(krylov_basis[krylov_step] * image), ("col", "sec"))
        alpha_list.append(alpha_now)
        if krylov_step + 1 < KRYLOV:
            image = image - alpha_now * krylov_basis[krylov_step]
            beta_now = jnp.sqrt(lax.psum(jnp.sum(image * image), ("col", "sec")))
            beta_list.append(beta_now)
            krylov_basis.append(image / beta_now)
    weights = small_exp(sign * TIME_STEP * tridiagonal(alpha_list, beta_list))[:, 0]
    result = weights[0] * krylov_basis[0]
    for krylov_step in range(1, KRYLOV):
        result = result + weights[krylov_step] * krylov_basis[krylov_step]
    return norm_zero * result


def body(site_tensor, left_env, right_env, bond_env, sector_sizes):
    col_rows = site_tensor.shape[0]
    sectors_here = site_tensor.shape[1]
    block_size = left_env.shape[2]
    left_wide = with_halo(left_env, (("sec", 0),), 1)

    def site_left(a, spin_out):
        return left_wide[spin_out : spin_out + sectors_here, a]

    def bond_left(a, spin_out):
        return bond_env[:, a]

    evolved_site = evolve(
        site_tensor, lambda vector: apply_ham(vector, 3, site_left, ONE_SITE_TERMS, right_env), -1.0
    )
    gathered = lax.all_gather(evolved_site, "col", axis=0, tiled=True)
    gram_matrix = jnp.einsum("rtx,stx->trs", gathered, gathered, precision=HIGH_PREC)
    live_mask = (jnp.arange(block_size)[None, :] < sector_sizes[:, None]).astype(jnp.float32)
    gram_matrix = (
        gram_matrix + (1.0 - live_mask)[:, :, None] * jnp.eye(block_size, dtype=jnp.float32)[None]
    )
    factor_lower = jnp.linalg.cholesky(gram_matrix)
    offset = lax.axis_index("col") * col_rows
    row_block = lax.dynamic_slice_in_dim(factor_lower, offset, col_rows, 1)
    live_rows = lax.dynamic_slice_in_dim(live_mask, offset, col_rows, 1)
    masked = row_block * live_rows[:, :, None] * live_mask[:, None, :]
    bond_start = jnp.transpose(masked, (1, 0, 2)) / math.sqrt(3.0 * block_size)
    evolved_bond = evolve(
        bond_start, lambda vector: apply_ham(vector, 1, bond_left, ZERO_SITE_TERMS, right_env), 1.0
    )
    return (evolved_site, evolved_bond)


def solution(mesh):
    in_specs = (
        P("col", "sec", None),
        P("sec", None, None, None),
        P("sec", None, None, "col"),
        P("sec", None, None, None),
        P("sec"),
    )
    out_specs = (P("col", "sec", None), P("col", "sec", None))
    return jax.shard_map(body, mesh=mesh, in_specs=in_specs, out_specs=out_specs, check_vma=False)
```

profile of v0, /device:TPU:1, one launch (start us, length us, event | category | flops | bytes accessed | tf_op | source)
XLA Modules:
  0.0 1875.2 jit_solution(12397167343773336727)
XLA Ops:
  17.7 116.4 %psum.112 = f32[]{:T(128)} all-reduce(f32[]{:T(128)} %multiply_reduce_fusion.7), channel_id=1, replica_groups=mesh['col'=4,'sec'=32] {'col','sec'}, use_global_device_ids=true, to_apply=%region_1.0 | all-reduce | flops 1 | bytes 8 | tf_op jit(solution)/shard_map/psum | solution.py:122
  194.6 39.7 %reduce-scatter.9.cloned.1.call-done = f32[128,1,1536]{0,2,1:T(8,128)} async-done(((f32[512,1,1536]{0,2,1:T(8,128)}), f32[128,1,1536]{0,2,1:T(8,128)}) %reduce-scatter.9.cloned.1.call-update) | async-done | bytes 786448 | tf_op jit(solution)/shard_map/reduce_scatter | solution.py:113
  236.2 64.5 %psum.113 = f32[]{:T(128)} all-reduce(f32[]{:T(128)} %multiply_reduce_fusion.6), channel_id=1, replica_groups=mesh['col'=4,'sec'=32] {'col','sec'}, use_global_device_ids=true, to_apply=%region_4.0 | all-reduce | flops 1 | bytes 8 | tf_op jit(solution)/shard_map/psum | solution.py:131
  303.3 64.1 %psum.114 = f32[]{:T(128)} all-reduce(f32[]{:T(128)} %multiply_reduce_fusion.5), channel_id=1, replica_groups=mesh['col'=4,'sec'=32] {'col','sec'}, use_global_device_ids=true, to_apply=%region_6.0 | all-reduce | flops 1 | bytes 8 | tf_op jit(solution)/shard_map/psum | solution.py:135
  427.0 37.8 %reduce-scatter.11.cloned.1.call-done = f32[128,1,1536]{0,2,1:T(8,128)} async-done(((f32[512,1,1536]{0,2,1:T(8,128)}), f32[128,1,1536]{0,2,1:T(8,128)}) %reduce-scatter.11.cloned.1.call-update) | async-done | bytes 786448 | tf_op jit(solution)/shard_map/reduce_scatter | solution.py:113
  466.7 64.5 %psum.115 = f32[]{:T(128)} all-reduce(f32[]{:T(128)} %multiply_reduce_fusion.4), channel_id=1, replica_groups=mesh['col'=4,'sec'=32] {'col','sec'}, use_global_device_ids=true, to_apply=%region_9.0 | all-reduce | flops 1 | bytes 8 | tf_op jit(solution)/shard_map/psum | solution.py:131
  534.8 64.1 %psum.116 = f32[]{:T(128)} all-reduce(f32[]{:T(128)} %get-tuple-element.10), channel_id=1, replica_groups=mesh['col'=4,'sec'=32] {'col','sec'}, use_global_device_ids=true, to_apply=%region_11.0 | all-reduce | flops 1 | bytes 8 | tf_op jit(solution)/shard_map/psum | solution.py:135
  657.7 37.8 %reduce-scatter.13.cloned.1.call-done = f32[128,1,1536]{0,2,1:T(8,128)} async-done(((f32[512,1,1536]{0,2,1:T(8,128)}), f32[128,1,1536]{0,2,1:T(8,128)}) %reduce-scatter.13.cloned.1.call-update) | async-done | bytes 786448 | tf_op jit(solution)/shard_map/reduce_scatter | solution.py:113
  697.7 64.5 %psum.117 = f32[]{:T(128)} all-reduce(f32[]{:T(128)} %multiply_reduce_fusion.2), channel_id=1, replica_groups=mesh['col'=4,'sec'=32] {'col','sec'}, use_global_device_ids=true, to_apply=%region_14.0 | all-reduce | flops 1 | bytes 8 | tf_op jit(solution)/shard_map/psum | solution.py:131
  765.8 64.1 %psum.118 = f32[]{:T(128)} all-reduce(f32[]{:T(128)} %get-tuple-element.8), channel_id=1, replica_groups=mesh['col'=4,'sec'=32] {'col','sec'}, use_global_device_ids=true, to_apply=%region_16.0 | all-reduce | flops 1 | bytes 8 | tf_op jit(solution)/shard_map/psum | solution.py:135
  888.9 37.7 %reduce-scatter.15.cloned.1.call-done = f32[128,1,1536]{0,2,1:T(8,128)} async-done(((f32[512,1,1536]{0,2,1:T(8,128)}), f32[128,1,1536]{0,2,1:T(8,128)}) %reduce-scatter.15.cloned.1.call-update) | async-done | bytes 786448 | tf_op jit(solution)/shard_map/reduce_scatter | solution.py:113
  929.1 64.5 %psum.119 = f32[1]{0:T(128)} all-reduce(f32[1]{0:T(128)} %bitcast.216), channel_id=1, replica_groups=mesh['col'=4,'sec'=32] {'col','sec'}, use_global_device_ids=true, to_apply=%region_19.0 | all-reduce | flops 1 | bytes 8 | tf_op jit(solution)/shard_map/psum | solution.py:131
  1004.9 39.2 %all-gather.2.cloned.1.call-done = f32[512,1,1536]{0,2,1:T(8,128)} async-done(((f32[128,1,1536]{0,2,1:T(8,128)}), f32[512,1,1536]{0,2,1:T(8,128)}) %all-gather.2.cloned.1.call-update) | async-done | bytes 3145744 | tf_op jit(solution)/shard_map/all_gather | solution.py:160
  1143.9 65.6 %psum.120 = f32[]{:T(128)} all-reduce(f32[]{:T(128)} %multiply_reduce_fusion.15), channel_id=1, replica_groups=mesh['col'=4,'sec'=32] {'col','sec'}, use_global_device_ids=true, to_apply=%region_29.30 | all-reduce | flops 1 | bytes 8 | tf_op jit(solution)/shard_map/psum | solution.py:122
  1232.0 23.2 %reduce-scatter.17.cloned.1.call-done = f32[128,1,512]{2,0,1:T(8,128)} async-done(((f32[512,1,512]{2,0,1:T(8,128)}), f32[128,1,512]{2,0,1:T(8,128)}) %reduce-scatter.17.cloned.1.call-update) | async-done | bytes 262160 | tf_op jit(solution)/shard_map/reduce_scatter | solution.py:113
  1256.9 65.9 %psum.121 = f32[]{:T(128)} all-reduce(f32[]{:T(128)} %multiply_reduce_fusion.14), channel_id=1, replica_groups=mesh['col'=4,'sec'=32] {'col','sec'}, use_global_device_ids=true, to_apply=%region_32.33 | all-reduce | flops 1 | bytes 8 | tf_op jit(solution)/shard_map/psum | solution.py:131
  1325.2 62.6 %psum.122 = f32[]{:T(128)} all-reduce(f32[]{:T(128)} %multiply_reduce_fusion.13), channel_id=1, replica_groups=mesh['col'=4,'sec'=32] {'col','sec'}, use_global_device_ids=true, to_apply=%region_34.35 | all-reduce | flops 1 | bytes 8 | tf_op jit(solution)/shard_map/psum | solution.py:135
  1412.3 22.8 %reduce-scatter.19.cloned.1.call-done = f32[128,1,512]{2,0,1:T(8,128)} async-done(((f32[512,1,512]{2,0,1:T(8,128)}), f32[128,1,512]{2,0,1:T(8,128)}) %reduce-scatter.19.cloned.1.call-update) | async-done | bytes 262160 | tf_op jit(solution)/shard_map/reduce_scatter | solution.py:113
  1436.9 66.0 %psum.123 = f32[]{:T(128)} all-reduce(f32[]{:T(128)} %multiply_reduce_fusion.12), channel_id=1, replica_groups=mesh['col'=4,'sec'=32] {'col','sec'}, use_global_device_ids=true, to_apply=%region_37.38 | all-reduce | flops 1 | bytes 8 | tf_op jit(solution)/shard_map/psum | solution.py:131
  1505.3 62.5 %psum.124 = f32[]{:T(128)} all-reduce(f32[]{:T(128)} %get-tuple-element.6), channel_id=1, replica_groups=mesh['col'=4,'sec'=32] {'col','sec'}, use_global_device_ids=true, to_apply=%region_39.40 | all-reduce | flops 1 | bytes 8 | tf_op jit(solution)/shard_map/psum | solution.py:135
  1590.7 22.1 %reduce-scatter.21.cloned.1.call-done = f32[128,1,512]{2,0,1:T(8,128)} async-done(((f32[512,1,512]{2,0,1:T(8,128)}), f32[128,1,512]{2,0,1:T(8,128)}) %reduce-scatter.21.cloned.1.call-update) | async-done | bytes 262160 | tf_op jit(solution)/shard_map/reduce_scatter | solution.py:113
  1614.4 66.6 %psum.125 = f32[]{:T(128)} all-reduce(f32[]{:T(128)} %multiply_reduce_fusion.10), channel_id=1, replica_groups=mesh['col'=4,'sec'=32] {'col','sec'}, use_global_device_ids=true, to_apply=%region_42.43 | all-reduce | flops 1 | bytes 8 | tf_op jit(solution)/shard_map/psum | solution.py:131
  1683.3 62.6 %psum.126 = f32[]{:T(128)} all-reduce(f32[]{:T(128)} %get-tuple-element.4), channel_id=1, replica_groups=mesh['col'=4,'sec'=32] {'col','sec'}, use_global_device_ids=true, to_apply=%region_44.45 | all-reduce | flops 1 | bytes 8 | tf_op jit(solution)/shard_map/psum | solution.py:135
  1793.3 65.9 %psum.127 = f32[1]{0:T(128)} all-reduce(f32[1]{0:T(128)} %bitcast.365), channel_id=1, replica_groups=mesh['col'=4,'sec'=32] {'col','sec'}, use_global_device_ids=true, to_apply=%region_47.48 | all-reduce | flops 1 | bytes 8 | tf_op jit(solution)/shard_map/psum | solution.py:131
  (279 shorter events, 505.9 us)
Async XLA Ops:
  7.2 227.1 %reduce-scatter.9.cloned.1.call-start = ((), (), s32[]{:S(2)}) async-start(), calls=%async_computation.8 | async-start | bytes 3932160 | tf_op jit(solution)/shard_map/reduce_scatter | solution.py:113
  7.2 146.8 %collective-permute-start = (f32[1,5,512,512]{3,2,1,0:T(8,128)}, f32[1,5,512,512]{3,2,1,0:T(8,128)}, u32[]{:S(2)}, u32[]{:S(2)}) collective-permute-start(f32[1,5,512,512]{3,2,1,0:T(8,128)} %param.6), channel_id=1, source_target_pairs={{0,1},{1,2},{2,3},{3,4},{4,5},{5,6},{6,7},{7,8},{8,9},{9,10},{10,1... | collective-permute-start | bytes 15728648 | tf_op jit(solution)/shard_map/ppermute | solution.py:52
  11.9 149.6 %collective-permute-start.1 = (f32[1,5,512,512]{3,2,1,0:T(8,128)}, f32[1,5,512,512]{3,2,1,0:T(8,128)}, u32[]{:S(2)}, u32[]{:S(2)}) collective-permute-start(f32[1,5,512,512]{3,2,1,0:T(8,128)} %param.6), channel_id=1, source_target_pairs={{1,0},{2,1},{3,2},{4,3},{5,4},{6,5},{7,6},{8,7},{9,8},{10,9},{11,1... | collective-permute-start | bytes 15728648 | tf_op jit(solution)/shard_map/ppermute | solution.py:55
  137.0 14.0 collective-permute-start.3
  139.4 13.3 collective-permute-start.2
  194.5 270.2 %reduce-scatter.11.cloned.1.call-start = ((), (), s32[]{:S(2)}) async-start(), calls=%async_computation.9 | async-start | bytes 3932160 | tf_op jit(solution)/shard_map/reduce_scatter | solution.py:113
  375.2 32.7 %collective-permute-start.5 = (f32[128,1,1536]{0,2,1:T(8,128)S(1)}, f32[128,1,1536]{0,2,1:T(8,128)S(1)}, u32[]{:S(2)}, u32[]{:S(2)}) collective-permute-start(f32[128,1,1536]{0,2,1:T(8,128)S(1)} %broadcast_divide_fusion.2), channel_id=1, source_target_pairs={{0,1},{1,2},{2,3},{3,4},{4,5},{5,6},{6,7},{7,8},{8,9},{9,10},{10,1... | collective-permute-start | bytes 2359304 | tf_op jit(solution)/shard_map/ppermute | solution.py:52
  377.4 26.4 %collective-permute-start.4 = (f32[128,1,1536]{0,2,1:T(8,128)S(1)}, f32[128,1,1536]{0,2,1:T(8,128)S(1)}, u32[]{:S(2)}, u32[]{:S(2)}) collective-permute-start(f32[128,1,1536]{0,2,1:T(8,128)S(1)} %broadcast_divide_fusion.2), channel_id=1, source_target_pairs={{1,0},{2,1},{3,2},{4,3},{5,4},{6,5},{7,6},{8,7},{9,8},{10,9},{11,1... | collective-permute-start | bytes 2359304 | tf_op jit(solution)/shard_map/ppermute | solution.py:55
  426.9 268.6 %reduce-scatter.13.cloned.1.call-start = ((), (), s32[]{:S(2)}) async-start(), calls=%async_computation.10 | async-start | bytes 3932160 | tf_op jit(solution)/shard_map/reduce_scatter | solution.py:113
  605.9 32.7 %collective-permute-start.7 = (f32[128,1,1536]{0,2,1:T(8,128)S(1)}, f32[128,1,1536]{0,2,1:T(8,128)S(1)}, u32[]{:S(2)}, u32[]{:S(2)}) collective-permute-start(f32[128,1,1536]{0,2,1:T(8,128)S(1)} %broadcast_divide_fusion.1), channel_id=1, source_target_pairs={{0,1},{1,2},{2,3},{3,4},{4,5},{5,6},{6,7},{7,8},{8,9},{9,10},{10,1... | collective-permute-start | bytes 2359304 | tf_op jit(solution)/shard_map/ppermute | solution.py:52
  608.1 26.4 %collective-permute-start.6 = (f32[128,1,1536]{0,2,1:T(8,128)S(1)}, f32[128,1,1536]{0,2,1:T(8,128)S(1)}, u32[]{:S(2)}, u32[]{:S(2)}) collective-permute-start(f32[128,1,1536]{0,2,1:T(8,128)S(1)} %broadcast_divide_fusion.1), channel_id=1, source_target_pairs={{1,0},{2,1},{3,2},{4,3},{5,4},{6,5},{7,6},{8,7},{9,8},{10,9},{11,1... | collective-permute-start | bytes 2359304 | tf_op jit(solution)/shard_map/ppermute | solution.py:55
  657.6 269.0 %reduce-scatter.15.cloned.1.call-start = ((), (), s32[]{:S(2)}) async-start(), calls=%async_computation.11 | async-start | bytes 3932160 | tf_op jit(solution)/shard_map/reduce_scatter | solution.py:113
  836.9 32.7 %collective-permute-start.9 = (f32[128,1,1536]{0,2,1:T(8,128)S(1)}, f32[128,1,1536]{0,2,1:T(8,128)S(1)}, u32[]{:S(2)}, u32[]{:S(2)}) collective-permute-start(f32[128,1,1536]{0,2,1:T(8,128)S(1)} %broadcast_divide_fusion), channel_id=1, source_target_pairs={{0,1},{1,2},{2,3},{3,4},{4,5},{5,6},{6,7},{7,8},{8,9},{9,10},{10,1... | collective-permute-start | bytes 2359304 | tf_op jit(solution)/shard_map/ppermute | solution.py:52
  839.1 26.4 %collective-permute-start.8 = (f32[128,1,1536]{0,2,1:T(8,128)S(1)}, f32[128,1,1536]{0,2,1:T(8,128)S(1)}, u32[]{:S(2)}, u32[]{:S(2)}) collective-permute-start(f32[128,1,1536]{0,2,1:T(8,128)S(1)} %broadcast_divide_fusion), channel_id=1, source_target_pairs={{1,0},{2,1},{3,2},{4,3},{5,4},{6,5},{7,6},{8,7},{9,8},{10,9},{11,1... | collective-permute-start | bytes 2359304 | tf_op jit(solution)/shard_map/ppermute | solution.py:55
  888.8 155.3 %all-gather.2.cloned.1.call-start = ((), (), s32[]{:S(2)}) async-start(), calls=%async_computation.12 | async-start | bytes 3932160 | tf_op jit(solution)/shard_map/all_gather | solution.py:160
  1004.2 251.0 %reduce-scatter.17.cloned.1.call-start = ((), (), s32[]{:S(2)}) async-start(), calls=%async_computation.13 | async-start | bytes 1310720 | tf_op jit(solution)/shard_map/reduce_scatter | solution.py:113
  1210.3 13.1 collective-permute-start.11
  1232.0 203.2 %reduce-scatter.19.cloned.1.call-start = ((), (), s32[]{:S(2)}) async-start(), calls=%async_computation.14 | async-start | bytes 1310720 | tf_op jit(solution)/shard_map/reduce_scatter | solution.py:113
  1390.2 13.6 collective-permute-start.13
  1393.7 7.7 collective-permute-start.12
  1412.3 200.5 %reduce-scatter.21.cloned.1.call-start = ((), (), s32[]{:S(2)}) async-start(), calls=%async_computation.15 | async-start | bytes 1310720 | tf_op jit(solution)/shard_map/reduce_scatter | solution.py:113
  1568.5 13.6 collective-permute-start.15
  1590.6 200.9 %reduce-scatter.23.cloned.1.call-start = ((), (), s32[]{:S(2)}) async-start(), calls=%async_computation.16 | async-start | bytes 1310720 | tf_op jit(solution)/shard_map/reduce_scatter | solution.py:113
  1746.6 13.6 collective-permute-start.17
  (12 other events, 331.1 us)
Sparse Core Ops, SparseCore 0:
  194.7 39.5 reduce-scatter.8
  427.0 37.7 reduce-scatter.10
  657.7 37.7 reduce-scatter.12
  888.9 37.7 reduce-scatter.14
  1004.3 39.7 all-gather.1
  1232.1 23.0 reduce-scatter.16
  1412.4 22.6 reduce-scatter.18
  1590.8 21.9 reduce-scatter.20
  1768.8 22.7 reduce-scatter.22
where the time goes:
time: 1880 us
  blocking collectives  1080 us (57%)
  matrix products  286 us (15%)
  waiting for transfers between devices  283 us (15%)
  other arithmetic  138 us (7%)
  starting transfers between devices  49.2 us (3%)
  between operations  24.4 us (1%)
    psum x8, blocking collectives, evolve(): lax.psum(jnp.sum(krylov_basis[krylov_step] * image), ('col', 'sec'))  523 us
    psum x6, blocking collectives, evolve(): beta_now = jnp.sqrt(lax.psum(jnp.sum(image * image), ('col', 'sec')))  380 us
    reduce_scatter x8, waiting for transfers between devices, apply_ham(): lax.psum_scatter(jnp.einsum('tbrc,bctx->rtx', panel, stacked, precision=H...  241 us
    dot_general x84, matrix products, apply_left(): jnp.einsum('rtk,tlk->rtl', fetch_block(b, spin_in), left_of(a, spin_out),...  193 us
    psum x2, blocking collectives, evolve(): first_sum = lax.psum(jnp.sum(start * start), ('col', 'sec'))  182 us
    another operation x14, other arithmetic, body(): factor_lower = jnp.linalg.cholesky(gram_matrix)  78.9 us
    dot_general x8, matrix products, apply_ham(): jnp.einsum('tbrc,bctx->rtx', panel, stacked, precision=HIGH_PREC)  75.3 us
    all_gather x1, waiting for transfers between devices, body(): gathered = lax.all_gather(evolved_site, 'col', axis=0, tiled=True)  39.2 us
  transfers between devices with their start and end apart: 27, of which 14 were waited for; matrix products, arithmetic and copies ran while one was open for 7% of the time, Pallas kernels for 0%

commit v1 on v0

v1 whole, which is shorter than its diff:
```python
import math

import jax
import jax.numpy as jnp
from jax import lax
from jax.sharding import PartitionSpec as P

KRYLOV = 4
HIGHEST = lax.Precision.HIGHEST
HIGH = lax.Precision.HIGH
ROOT_TWO = math.sqrt(2.0)
ANISOTROPY = 0.5
TIME_STEP = 0.1


def small_exp(matrix):
    dimension = matrix.shape[0]
    identity = jnp.eye(dimension, dtype=jnp.float32)
    scaled = matrix / 16.0

    def mul(left, right):
        return jnp.sum(left[:, :, None] * right[None, :, :], axis=1)

    result = identity
    for degree in range(8, 0, -1):
        result = identity + mul(scaled, result) / degree
    for squaring in range(4):
        result = mul(result, result)
    return result


def tridiagonal(alpha_list, beta_list):
    diagonal_part = jnp.diag(jnp.stack(alpha_list))
    upper_part = jnp.diag(jnp.stack(beta_list), 1)
    return diagonal_part + upper_part + upper_part.T


def sector_perms(mesh_shape):
    ny, nx, nc = mesh_shape

    def perm(move):
        pairs = []
        for y in range(ny):
            for x in range(nx):
                for k in range(nc):
                    y2, x2, k2 = move(y, x, k)
                    source = (y * nx + x) * nc + k
                    target = ((y2 % ny) * nx + x2 % nx) * nc + k2 % nc
                    pairs.append((source, target))
        return pairs

    stages = [[perm(lambda y, x, k: (y, x, k + 1))]]
    stages.append([perm(lambda y, x, k, d=d: (y, x + d, k)) for d in range(1, nx)])
    stages.append([perm(lambda y, x, k, d=d: (y + d, x, k)) for d in range(1, ny)])
    return stages


STAGES = sector_perms((4, 4, 2))


def sum_over_sectors(values):
    packed = jnp.stack(values)
    for stage in STAGES:
        received = [lax.ppermute(packed, "sec", pairs) for pairs in stage]
        for part in received:
            packed = packed + part
    return [packed[i] for i in range(len(values))]


def to_next(block):
    count = lax.axis_size("sec")
    return lax.ppermute(block, "sec", [(i, i + 1) for i in range(count - 1)])


def to_previous(block):
    count = lax.axis_size("sec")
    return lax.ppermute(block, "sec", [(i + 1, i) for i in range(count - 1)])


def gather_col(block, axis):
    return lax.all_gather(block, "col", axis=axis, tiled=True)


def mm(left, right):
    return jnp.dot(left, right, precision=HIGH)


def evolve(start, apply_fn, sign, scale_of):
    raw = apply_fn(start)
    norm_zero = scale_of()
    inverse = 1.0 / norm_zero
    u_list = [start * inverse]
    y_list = [raw * inverse]
    gammas = [jnp.float32(1.0)]
    alphas = []
    betas = []
    for step in range(KRYLOV):
        u_now, y_now = u_list[-1], y_list[-1]
        partial = [jnp.sum(u_now * u_now), jnp.sum(u_now * y_now)]
        ahead = apply_fn(y_now) if step + 1 < KRYLOV else None
        norm_sq, cross = sum_over_sectors(partial)
        if step > 0:
            beta = jnp.sqrt(norm_sq)
            betas.append(beta)
            gammas.append(1.0 / beta)
            alphas.append(cross / norm_sq)
        else:
            alphas.append(cross)
        if step + 1 < KRYLOV:
            gamma = gammas[-1]
            u_next = gamma * (y_now - alphas[-1] * u_now)
            y_next = gamma * (ahead - alphas[-1] * y_now)
            if step > 0:
                back = betas[-1] * gammas[-2]
                u_next = u_next - back * u_list[-2]
                y_next = y_next - back * y_list[-2]
            u_list.append(u_next)
            y_list.append(y_next)
    weights = small_exp(sign * TIME_STEP * tridiagonal(alphas, betas))[:, 0]
    result = (norm_zero * weights[0]) * u_list[0]
    for step in range(1, KRYLOV):
        result = result + (norm_zero * weights[step] * gammas[step]) * u_list[step]
    return result


def body(site_tensor, left_env, right_env, bond_env, sector_sizes):
    col_rows = site_tensor.shape[0]
    block_size = left_env.shape[2]
    size = block_size
    sector = lax.axis_index("sec")
    last = lax.axis_size("sec") - 1

    left = left_env[0]
    site_full = gather_col(site_tensor[:, 0], 0)
    right = gather_col(right_env[0], 2)

    send_up = jnp.stack([left[0] + left[1] + ANISOTROPY * left[4], left[4]])
    send_down = jnp.stack([left[0] - left[1] + ANISOTROPY * left[4], left[4]])
    below = to_next(send_up)
    above = to_previous(send_down)
    raise_here = jnp.where(sector < last, ROOT_TWO * left[2], 0.0)
    lower_here = jnp.where(sector > 0, ROOT_TWO * left[3], 0.0)
    right_plus = right[4] + right[1]
    right_minus = right[4] - right[1]
    half = ROOT_TWO / 2
    up_matrix = half * right[2].T
    down_matrix = half * right[3].T

    def apply_site(vector):
        x0, x1, x2 = (vector[:, s * size : (s + 1) * size] for s in range(3))
        z1 = mm(x1, left[4])
        z0 = mm(x0, below[1])
        z2 = mm(x2, above[1])
        from_above = to_previous(mm(down_matrix, jnp.concatenate([z0, z1], axis=1)))
        from_below = to_next(mm(up_matrix, jnp.concatenate([z1, z2], axis=1)))
        p0 = mm(x0, below[0]) + mm(x1, lower_here)
        p1 = mm(x1, left[0]) + mm(x0, lower_here.T) + mm(x2, raise_here.T)
        p2 = mm(x2, above[0]) + mm(x1, raise_here)
        y0 = mm(right[0], p0) + mm(right_plus, z0)
        y1 = mm(right[0], p1) + mm(right[4], z1)
        y2 = mm(right[0], p2) + mm(right_minus, z2)
        y0 = y0 + from_below[:, :size]
        y1 = y1 + from_below[:, size:] + from_above[:, :size]
        y2 = y2 + from_above[:, size:]
        return jnp.concatenate([y0, y1, y2], axis=1)

    def site_norm():
        (norm_sq,) = sum_over_sectors([jnp.sum(site_full * site_full)])
        return jnp.sqrt(norm_sq)

    evolved = evolve(site_full, apply_site, -1.0, site_norm)
    gram = lax.dot_general(evolved, evolved, (((1,), (1,)), ((), ())), precision=HIGHEST)
    live = (jnp.arange(size) < sector_sizes[0]).astype(jnp.float32)
    gram = gram + (1.0 - live)[:, None] * jnp.eye(size, dtype=jnp.float32)
    factor = jnp.linalg.cholesky(gram[None])[0]
    start = factor * live[:, None] * live[None, :] / math.sqrt(3.0 * block_size)

    bond = bond_env[0]
    down_bond = ROOT_TWO * bond[3]
    up_bond = ROOT_TWO * bond[2]

    def apply_bond(vector):
        from_above = to_previous(mm(down_matrix, mm(vector, down_bond)))
        from_below = to_next(mm(up_matrix, mm(vector, up_bond)))
        y = mm(right[0], mm(vector, bond[0]))
        y = y + mm(right[1], mm(vector, bond[1]))
        y = y + mm(right[4], mm(vector, bond[4]))
        return y + from_above + from_below

    def bond_norm():
        (norm_sq,) = sum_over_sectors([jnp.sum(start * start)])
        return jnp.sqrt(norm_sq)

    evolved_bond = evolve(start, apply_bond, 1.0, bond_norm)

    offset = lax.axis_index("col") * col_rows
    out_site = lax.dynamic_slice_in_dim(evolved, offset, col_rows, 0)[:, None, :]
    out_bond = lax.dynamic_slice_in_dim(evolved_bond, offset, col_rows, 0)[:, None, :]
    return (out_site, out_bond)


def solution(mesh):
    in_specs = (
        P("col", "sec", None),
        P("sec", None, None, None),
        P("sec", None, None, "col"),
        P("sec", None, None, None),
        P("sec"),
    )
    out_specs = (P("col", "sec", None), P("col", "sec", None))
    return jax.shard_map(body, mesh=mesh, in_specs=in_specs, out_specs=out_specs, check_vma=False)
```

time: 1880 us -> 770 us (0.41)
  blocking collectives: 1080 us -> 0 us
  waiting for transfers between devices: 283 us -> 134 us
  starting transfers between devices: 49.2 us -> 167 us
  matrix products: 286 us -> 256 us
  between operations: 24.4 us -> 46.8 us
    psum x16 -> x0, blocking collectives: 1080 us -> none  [the longest x8 523 us: evolve(): lax.psum(jnp.sum(krylov_basis[krylov_step] * image), ('col', 'sec'))]
    reduce_scatter x8 -> x0, waiting for transfers between devices: 241 us -> none  [apply_ham(): lax.psum_scatter(jnp.einsum('tbrc,bctx->rtx', panel, stacked, precision=H...]
    ppermute x18 -> x88, starting transfers between devices: 48.9 us -> 167 us  [the longest x70 113 us: sum_over_sectors(): received = [lax.ppermute(packed, 'sec', pairs) for pairs in stage]]
    ppermute x18 -> x88, waiting for transfers between devices: 3.22 us -> 62.1 us  [the longest x70 62.1 us: sum_over_sectors(): received = [lax.ppermute(packed, 'sec', pairs) for pairs in stage]]
    all_gather x1 -> x2, waiting for transfers between devices: 39.2 us -> 70.8 us  [gather_col(): return lax.all_gather(block, 'col', axis=axis, tiled=True)]
    dot_general x117 -> x113, matrix products: 281 us -> 251 us  [the longest x112 245 us: mm(): return jnp.dot(left, right, precision=HIGH)]
    add x0 -> x44, other arithmetic: none -> 21.6 us  [the longest x24 10.7 us: sum_over_sectors(): packed = packed + part]
    another operation x18 -> x24, other arithmetic: 79.1 us -> 92.7 us  [the longest x15 79.6 us: body(): factor = jnp.linalg.cholesky(gram[None])[0]]
  transfers between devices with their start and end apart: 27 -> 90, of which waited for: 14 -> 44; matrix products, arithmetic and copies ran while one was open for 7% -> 25% of each run, Pallas kernels for 0% -> 0%
where the time goes in v1:
time: 770 us; the launch traced here: 757 us
  matrix products  256 us (33%)
  starting transfers between devices  167 us (22%)
  other arithmetic  137 us (18%)
  waiting for transfers between devices  134 us (17%)
  between operations  46.8 us (6%)
  local copies, waits for them, and re-layouts  15.9 us (2%)
    dot_general x112, matrix products, mm(): return jnp.dot(left, right, precision=HIGH)  245 us
    ppermute x70, starting transfers between devices, sum_over_sectors(): received = [lax.ppermute(packed, 'sec', pairs) for pairs in stage]  113 us
    another operation x15, other arithmetic, body(): factor = jnp.linalg.cholesky(gram[None])[0]  79.6 us
    all_gather x2, waiting for transfers between devices, gather_col(): return lax.all_gather(block, 'col', axis=axis, tiled=True)  70.8 us
    ppermute x70, waiting for transfers between devices, sum_over_sectors(): received = [lax.ppermute(packed, 'sec', pairs) for pairs in stage]  62.1 us
    ppermute x9, starting transfers between devices, to_next(): return lax.ppermute(block, 'sec', [(i, i + 1) for i in range(count - 1)])  31.8 us
    ppermute x9, starting transfers between devices, to_previous(): return lax.ppermute(block, 'sec', [(i + 1, i) for i in range(count - 1)])  22 us
  transfers between devices with their start and end apart: 90, of which 44 were waited for; matrix products, arithmetic and copies ran while one was open for 25% of the time, Pallas kernels for 0%

profile of v1, /device:TPU:1, one launch (start us, length us, event | category | flops | bytes accessed | tf_op | source)
XLA Modules:
  0.0 756.8 jit_solution(5933168237492048613)
XLA Ops:
  17.1 4.5 collective-permute-start.7
  24.2 31.9 %all-gather.5.cloned.1.call-done = f32[512,1,1536]{0,2,1:T(8,128)} async-done(((f32[128,1,1536]{0,2,1:T(8,128)}), f32[512,1,1536]{0,2,1:T(8,128)}) %all-gather.5.cloned.1.call-update) | async-done | bytes 3145744 | tf_op jit(solution)/shard_map/all_gather | solution.py:81
  80.9 38.9 %all-gather.7.cloned.1.call-done = f32[1,5,512,512]{3,2,1,0:T(8,128)} async-done(((f32[1,5,512,128]{3,2,1,0:T(8,128)}), f32[1,5,512,512]{3,2,1,0:T(8,128)}) %all-gather.7.cloned.1.call-update) | async-done | bytes 5242896 | tf_op jit(solution)/shard_map/all_gather | solution.py:81
  119.8 5.2 fusion.10
  128.6 4.5 fusion.6
  143.2 16.1 %collective-permute-start.1 = (f32[1]{0:T(128)}, f32[1]{0:T(128)}, u32[]{:S(2)}, u32[]{:S(2)}) collective-permute-start(f32[1]{0:T(128)} %add.683), channel_id=1, source_target_pairs={{0,2},{1,3},{2,4},{3,5},{4,6},{5,7},{6,0},{7,1},{8,10},{9,11},{10,... | collective-permute-start | bytes 20 | tf_op jit(solution)/shard_map/ppermute | solution.py:64
  235.1 4.9 collective-permute-done.13
  418.2 5.4 multiply_add_fusion
  423.6 5.2 convolution_add_fusion.34
  430.4 11.7 %custom-call.31 = f32[1,128,128]{2,1,0:T(8,128)S(1)} custom-call(f32[1,128,128]{2,1,0:T(8,128)S(1)} %cholesky.267), custom_call_target="Cholesky" | custom-call | tf_op jit(solution)/shard_map/jit(cholesky)/cholesky | solution.py:175
  442.3 10.0 %custom-call.32 = f32[1,1,128,128]{2,3,1,0:T(8,128)S(1)} custom-call(f32[1,1,128,128]{3,2,1,0:T(8,128)S(1)} %get-tuple-element.45), custom_call_target="InvertDiagBlocksLowerTriangular" | custom-call | tf_op jit(solution)/shard_map/jit(cholesky)/cholesky | solution.py:175
  454.8 11.7 %custom-call.33 = f32[1,128,128]{2,1,0:T(8,128)S(1)} custom-call(f32[1,128,128]{2,1,0:T(8,128)S(1)} %cholesky.271), custom_call_target="Cholesky" | custom-call | tf_op jit(solution)/shard_map/jit(cholesky)/cholesky | solution.py:175
  466.5 9.8 %custom-call.34 = f32[1,1,128,128]{2,3,1,0:T(8,128)S(1)} custom-call(f32[1,1,128,128]{3,2,1,0:T(8,128)S(1)} %get-tuple-element.42), custom_call_target="InvertDiagBlocksLowerTriangular" | custom-call | tf_op jit(solution)/shard_map/jit(cholesky)/cholesky | solution.py:175
  477.9 12.1 %custom-call.35 = f32[1,128,128]{2,1,0:T(8,128)S(1)} custom-call(f32[1,128,128]{2,1,0:T(8,128)S(1)} %cholesky.276), custom_call_target="Cholesky" | custom-call | tf_op jit(solution)/shard_map/jit(cholesky)/cholesky | solution.py:175
  490.0 9.8 %custom-call.36 = f32[1,1,128,128]{2,3,1,0:T(8,128)S(1)} custom-call(f32[1,1,128,128]{3,2,1,0:T(8,128)S(1)} %get-tuple-element.39), custom_call_target="InvertDiagBlocksLowerTriangular" | custom-call | tf_op jit(solution)/shard_map/jit(cholesky)/cholesky | solution.py:175
  501.3 11.7 %custom-call.37 = f32[1,128,128]{2,1,0:T(8,128)S(1)} custom-call(f32[1,128,128]{2,1,0:T(8,128)S(1)} %fusion.69), custom_call_target="Cholesky" | custom-call | tf_op jit(solution)/shard_map/jit(cholesky)/cholesky | solution.py:175
  533.6 5.7 collective-permute-start.53
  575.8 4.7 multiply_reduce_fusion.14
  587.1 5.0 collective-permute-start.54
  605.6 4.6 collective-permute-done.56
  626.9 5.6 collective-permute-start.63
  662.6 6.7 multiply_reduce_fusion.10
  676.8 5.3 collective-permute-start.72
  718.4 7.2 collective-permute-start.81
  (542 shorter events, 471.8 us)
Async XLA Ops:
  7.2 49.0 %all-gather.5.cloned.1.call-start = ((), (), s32[]{:S(2)}) async-start(), calls=%async_computation | async-start | bytes 3932160 | tf_op jit(solution)/shard_map/all_gather | solution.py:81
  10.3 109.5 %all-gather.7.cloned.1.call-start = ((), (), s32[]{:S(2)}) async-start(), calls=%async_computation.1 | async-start | bytes 6553600 | tf_op jit(solution)/shard_map/all_gather | solution.py:81
  17.1 50.8 %collective-permute-start.7 = (f32[2,512,512]{2,1,0:T(8,128)}, f32[2,512,512]{2,1,0:T(8,128)}, u32[]{:S(2)}, u32[]{:S(2)}) collective-permute-start(f32[2,512,512]{2,1,0:T(8,128)} %get-tuple-element.34), channel_id=1, source_target_pairs={{0,1},{1,2},{2,3},{3,4},{4,5},{5,6},{6,7},{7,8},{8,9},{9,10},{10,1... | collective-permute-start | bytes 6291464 | tf_op jit(solution)/shard_map/ppermute | solution.py:72
  21.6 49.7 %collective-permute-start.8 = (f32[2,512,512]{2,1,0:T(8,128)}, f32[2,512,512]{2,1,0:T(8,128)}, u32[]{:S(2)}, u32[]{:S(2)}) collective-permute-start(f32[2,512,512]{2,1,0:T(8,128)} %get-tuple-element.35), channel_id=1, source_target_pairs={{1,0},{2,1},{3,2},{4,3},{5,4},{6,5},{7,6},{8,7},{9,8},{10,9},{11,1... | collective-permute-start | bytes 6291464 | tf_op jit(solution)/shard_map/ppermute | solution.py:77
  59.6 82.3 %collective-permute-start = (f32[1]{0:T(128)}, f32[1]{0:T(128)}, u32[]{:S(2)}, u32[]{:S(2)}) collective-permute-start(f32[1]{0:T(128)} %bitcast.1), channel_id=1, source_target_pairs={{0,1},{1,0},{2,3},{3,2},{4,5},{5,4},{6,7},{7,6},{8,9},{9,8},{10,11... | collective-permute-start | bytes 20 | tf_op jit(solution)/shard_map/ppermute | solution.py:64
  124.9 60.0 %collective-permute-start.10 = (f32[512,1024]{0,1:T(8,128)}, f32[512,1024]{0,1:T(8,128)}, u32[]{:S(2)}, u32[]{:S(2)}) collective-permute-start(f32[512,1024]{0,1:T(8,128)} %fusion.10), channel_id=1, source_target_pairs={{1,0},{2,1},{3,2},{4,3},{5,4},{6,5},{7,6},{8,7},{9,8},{10,9},{11,1... | collective-permute-start | bytes 6291464 | tf_op jit(solution)/shard_map/ppermute | solution.py:77
  133.1 54.4 %collective-permute-start.9 = (f32[512,1024]{0,1:T(8,128)}, f32[512,1024]{0,1:T(8,128)}, u32[]{:S(2)}, u32[]{:S(2)}) collective-permute-start(f32[512,1024]{0,1:T(8,128)} %fusion.6), channel_id=1, source_target_pairs={{0,1},{1,2},{2,3},{3,4},{4,5},{5,6},{6,7},{7,8},{8,9},{9,10},{10,1... | collective-permute-start | bytes 6291464 | tf_op jit(solution)/shard_map/ppermute | solution.py:72
  143.2 21.2 %collective-permute-start.1 = (f32[1]{0:T(128)}, f32[1]{0:T(128)}, u32[]{:S(2)}, u32[]{:S(2)}) collective-permute-start(f32[1]{0:T(128)} %add.683), channel_id=1, source_target_pairs={{0,2},{1,3},{2,4},{3,5},{4,6},{5,7},{6,0},{7,1},{8,10},{9,11},{10,... | collective-permute-start | bytes 20 | tf_op jit(solution)/shard_map/ppermute | solution.py:64
  200.3 28.4 %collective-permute-start.11 = (f32[2]{0:T(128)S(1)}, f32[2]{0:T(128)S(1)}, u32[]{:S(2)}, u32[]{:S(2)}) collective-permute-start(f32[2]{0:T(128)S(1)} %pad_maximum_fusion.2), channel_id=1, source_target_pairs={{0,1},{1,0},{2,3},{3,2},{4,5},{5,4},{6,7},{7,6},{8,9},{9,8},{10,11... | collective-permute-start | bytes 32 | tf_op jit(solution)/shard_map/ppermute | solution.py:64
  204.5 43.5 %collective-permute-start.19 = (f32[512,1024]{0,1:T(8,128)S(1)}, f32[512,1024]{0,1:T(8,128)S(1)}, u32[]{:S(2)}, u32[]{:S(2)}) collective-permute-start(f32[512,1024]{0,1:T(8,128)S(1)} %fusion.18), channel_id=1, source_target_pairs={{1,0},{2,1},{3,2},{4,3},{5,4},{6,5},{7,6},{8,7},{9,8},{10,9},{11,1... | collective-permute-start | bytes 6291464 | tf_op jit(solution)/shard_map/ppermute | solution.py:77
  211.1 38.1 %collective-permute-start.18 = (f32[512,1024]{0,1:T(8,128)S(1)}, f32[512,1024]{0,1:T(8,128)S(1)}, u32[]{:S(2)}, u32[]{:S(2)}) collective-permute-start(f32[512,1024]{0,1:T(8,128)S(1)} %fusion.14), channel_id=1, source_target_pairs={{0,1},{1,2},{2,3},{3,4},{4,5},{5,6},{6,7},{7,8},{8,9},{9,10},{10,1... | collective-permute-start | bytes 6291464 | tf_op jit(solution)/shard_map/ppermute | solution.py:72
  260.5 33.8 %collective-permute-start.20 = (f32[2]{0:T(128)S(1)}, f32[2]{0:T(128)S(1)}, u32[]{:S(2)}, u32[]{:S(2)}) collective-permute-start(f32[2]{0:T(128)S(1)} %pad_maximum_fusion.3), channel_id=1, source_target_pairs={{0,1},{1,0},{2,3},{3,2},{4,5},{5,4},{6,7},{7,6},{8,9},{9,8},{10,11... | collective-permute-start | bytes 32 | tf_op jit(solution)/shard_map/ppermute | solution.py:64
  265.9 44.4 %collective-permute-start.28 = (f32[512,1024]{0,1:T(8,128)}, f32[512,1024]{0,1:T(8,128)}, u32[]{:S(2)}, u32[]{:S(2)}) collective-permute-start(f32[512,1024]{0,1:T(8,128)} %fusion.26), channel_id=1, source_target_pairs={{1,0},{2,1},{3,2},{4,3},{5,4},{6,5},{7,6},{8,7},{9,8},{10,9},{11,1... | collective-permute-start | bytes 6291464 | tf_op jit(solution)/shard_map/ppermute | solution.py:77
  274.0 39.5 %collective-permute-start.27 = (f32[512,1024]{0,1:T(8,128)}, f32[512,1024]{0,1:T(8,128)}, u32[]{:S(2)}, u32[]{:S(2)}) collective-permute-start(f32[512,1024]{0,1:T(8,128)} %fusion.22), channel_id=1, source_target_pairs={{0,1},{1,2},{2,3},{3,4},{4,5},{5,6},{6,7},{7,8},{8,9},{9,10},{10,1... | collective-permute-start | bytes 6291464 | tf_op jit(solution)/shard_map/ppermute | solution.py:72
  329.8 35.2 %collective-permute-start.29 = (f32[2]{0:T(128)S(1)}, f32[2]{0:T(128)S(1)}, u32[]{:S(2)}, u32[]{:S(2)}) collective-permute-start(f32[2]{0:T(128)S(1)} %pad_maximum_fusion.4), channel_id=1, source_target_pairs={{0,1},{1,0},{2,3},{3,2},{4,5},{5,4},{6,7},{7,6},{8,9},{9,8},{10,11... | collective-permute-start | bytes 32 | tf_op jit(solution)/shard_map/ppermute | solution.py:64
  337.6 47.2 %collective-permute-start.37 = (f32[512,1024]{0,1:T(8,128)}, f32[512,1024]{0,1:T(8,128)}, u32[]{:S(2)}, u32[]{:S(2)}) collective-permute-start(f32[512,1024]{0,1:T(8,128)} %fusion.34), channel_id=1, source_target_pairs={{1,0},{2,1},{3,2},{4,3},{5,4},{6,5},{7,6},{8,7},{9,8},{10,9},{11,1... | collective-permute-start | bytes 6291464 | tf_op jit(solution)/shard_map/ppermute | solution.py:77
  345.0 43.3 %collective-permute-start.36 = (f32[512,1024]{0,1:T(8,128)}, f32[512,1024]{0,1:T(8,128)}, u32[]{:S(2)}, u32[]{:S(2)}) collective-permute-start(f32[512,1024]{0,1:T(8,128)} %fusion.30), channel_id=1, source_target_pairs={{0,1},{1,2},{2,3},{3,4},{4,5},{5,6},{6,7},{7,8},{8,9},{9,10},{10,1... | collective-permute-start | bytes 6291464 | tf_op jit(solution)/shard_map/ppermute | solution.py:72
  533.6 42.2 %collective-permute-start.53 = (f32[512,512]{1,0:T(8,128)}, f32[512,512]{1,0:T(8,128)}, u32[]{:S(2)}, u32[]{:S(2)}) collective-permute-start(f32[512,512]{1,0:T(8,128)} %fusion.249), channel_id=1, source_target_pairs={{0,1},{1,2},{2,3},{3,4},{4,5},{5,6},{6,7},{7,8},{8,9},{9,10},{10,1... | collective-permute-start | bytes 3145736 | tf_op jit(solution)/shard_map/ppermute | solution.py:72
  542.6 33.2 %collective-permute-start.52 = (f32[512,512]{1,0:T(8,128)}, f32[512,512]{1,0:T(8,128)}, u32[]{:S(2)}, u32[]{:S(2)}) collective-permute-start(f32[512,512]{1,0:T(8,128)} %fusion.261), channel_id=1, source_target_pairs={{1,0},{2,1},{3,2},{4,3},{5,4},{6,5},{7,6},{8,7},{9,8},{10,9},{11,1... | collective-permute-start | bytes 3145736 | tf_op jit(solution)/shard_map/ppermute | solution.py:77
  593.2 24.7 %collective-permute-start.62 = (f32[512,512]{1,0:T(8,128)S(1)}, f32[512,512]{1,0:T(8,128)S(1)}, u32[]{:S(2)}, u32[]{:S(2)}) collective-permute-start(f32[512,512]{1,0:T(8,128)S(1)} %fusion.247), channel_id=1, source_target_pairs={{0,1},{1,2},{2,3},{3,4},{4,5},{5,6},{6,7},{7,8},{8,9},{9,10},{10,1... | collective-permute-start | bytes 3145736 | tf_op jit(solution)/shard_map/ppermute | solution.py:72
  634.6 27.9 %collective-permute-start.71 = (f32[512,512]{1,0:T(8,128)}, f32[512,512]{1,0:T(8,128)}, u32[]{:S(2)}, u32[]{:S(2)}) collective-permute-start(f32[512,512]{1,0:T(8,128)} %fusion.245), channel_id=1, source_target_pairs={{0,1},{1,2},{2,3},{3,4},{4,5},{5,6},{6,7},{7,8},{8,9},{9,10},{10,1... | collective-permute-start | bytes 3145736 | tf_op jit(solution)/shard_map/ppermute | solution.py:72
  639.4 23.2 %collective-permute-start.70 = (f32[512,512]{1,0:T(8,128)}, f32[512,512]{1,0:T(8,128)}, u32[]{:S(2)}, u32[]{:S(2)}) collective-permute-start(f32[512,512]{1,0:T(8,128)} %fusion.257), channel_id=1, source_target_pairs={{1,0},{2,1},{3,2},{4,3},{5,4},{6,5},{7,6},{8,7},{9,8},{10,9},{11,1... | collective-permute-start | bytes 3145736 | tf_op jit(solution)/shard_map/ppermute | solution.py:77
  684.2 28.5 %collective-permute-start.80 = (f32[512,512]{1,0:T(8,128)}, f32[512,512]{1,0:T(8,128)}, u32[]{:S(2)}, u32[]{:S(2)}) collective-permute-start(f32[512,512]{1,0:T(8,128)} %fusion.243), channel_id=1, source_target_pairs={{0,1},{1,2},{2,3},{3,4},{4,5},{5,6},{6,7},{7,8},{8,9},{9,10},{10,1... | collective-permute-start | bytes 3145736 | tf_op jit(solution)/shard_map/ppermute | solution.py:72
  688.8 23.9 %collective-permute-start.79 = (f32[512,512]{1,0:T(8,128)}, f32[512,512]{1,0:T(8,128)}, u32[]{:S(2)}, u32[]{:S(2)}) collective-permute-start(f32[512,512]{1,0:T(8,128)} %fusion.255), channel_id=1, source_target_pairs={{1,0},{2,1},{3,2},{4,3},{5,4},{6,5},{7,6},{8,7},{9,8},{10,9},{11,1... | collective-permute-start | bytes 3145736 | tf_op jit(solution)/shard_map/ppermute | solution.py:77
  (130 other events, 1250.1 us)
Sparse Core Ops, SparseCore 0:
  10.4 45.7 all-gather.4
  57.8 61.9 all-gather.6

commit v2 on v1

v2 whole, which is shorter than its diff:
```python
import functools
import math

import jax
import jax.numpy as jnp
from jax import lax
from jax.experimental import pallas as pl
from jax.experimental.pallas import tpu as pltpu
from jax.sharding import PartitionSpec as P

KRYLOV = 4
HIGHEST = lax.Precision.HIGHEST
HIGH = lax.Precision.HIGH
ROOT_TWO = math.sqrt(2.0)
ANISOTROPY = 0.5
TIME_STEP = 0.1
VMEM_LIMIT = 48 * 1024 * 1024
ROWS = 16


def to_next(block):
    count = lax.axis_size("sec")
    return lax.ppermute(block, "sec", [(i, i + 1) for i in range(count - 1)])


def to_previous(block):
    count = lax.axis_size("sec")
    return lax.ppermute(block, "sec", [(i + 1, i) for i in range(count - 1)])


def gather_col(block, axis):
    return lax.all_gather(block, "col", axis=axis, tiled=True)


def mm(left, right):
    return jnp.dot(left, right, precision=HIGH)


def params():
    return pltpu.CompilerParams(vmem_limit_bytes=VMEM_LIMIT)


def exchange(rows, axis):
    count = lax.axis_size(axis) if isinstance(axis, str) else lax.axis_size(axis[0]) * lax.axis_size(axis[1])
    sent = jnp.broadcast_to(rows[None], (count,) + rows.shape)
    return lax.all_to_all(sent, axis, 0, 0)


def sum_over_col(rows):
    count = lax.axis_size("col")
    parts = [
        lax.ppermute(rows, "col", [(i, (i + step) % count) for i in range(count)])
        for step in range(1, count)
    ]
    for part in parts:
        rows = rows + part
    return rows


def dot_rows_kernel(a_ref, out_ref):
    a = a_ref[...]
    out_ref[...] = jnp.full(out_ref.shape, jnp.sum(a * a))


def norm_rows(block):
    return pl.pallas_call(
        dot_rows_kernel,
        out_shape=jax.ShapeDtypeStruct((8, 128), jnp.float32),
        compiler_params=params(),
    )(block)


def inverse_norm_kernel(parts_ref, out_ref):
    out_ref[...] = 1.0 / jnp.sqrt(jnp.sum(parts_ref[...], axis=0))


def inverse_norm(parts):
    return pl.pallas_call(
        inverse_norm_kernel,
        out_shape=jax.ShapeDtypeStruct((8, 128), jnp.float32),
        compiler_params=params(),
    )(parts)


def first_combine_kernel(spins, nloc, *refs):
    scale_ref, x_ref = refs[0], refs[1]
    part_refs = refs[2 : 2 + nloc]
    y_ref, sums_ref = refs[2 + nloc], refs[3 + nloc]
    nu = scale_ref[0:1, 0:1]
    size = y_ref.shape[2]
    cross = jnp.float32(0.0)
    square = jnp.float32(0.0)
    index = 0
    for s in range(spins):
        total = None
        for part in spin_parts(spins, s):
            value = part_refs[index][...]
            index += 1
            total = value if total is None else total + value
        y = total * nu
        y_ref[s] = y
        cross += jnp.sum(x_ref[:, s * size : (s + 1) * size] * nu * y)
        square += jnp.sum(y * y)

    @pl.when(pl.program_id(0) == 0)
    def _():
        sums_ref[...] = jnp.zeros_like(sums_ref)

    row = lax.broadcasted_iota(jnp.int32, sums_ref.shape, 0)
    sums_ref[...] += jnp.where(row == 0, cross, jnp.where(row == 1, square, 0.0))


def spin_parts(spins, s):
    if spins == 1:
        return range(3)
    return range((2, 3, 2)[s])


def first_combine(x, nu, parts, spins):
    size = x.shape[0]
    step = 128
    spec = pl.BlockSpec((step, size), lambda i: (i, 0))
    return pl.pallas_call(
        functools.partial(first_combine_kernel, spins, len(parts)),
        grid=(size // step,),
        in_specs=[
            pl.BlockSpec((8, 128), lambda i: (0, 0)),
            pl.BlockSpec((step, spins * size), lambda i: (i, 0)),
        ]
        + [spec] * len(parts),
        out_specs=[
            pl.BlockSpec((spins, step, size), lambda i: (0, i, 0)),
            pl.BlockSpec((8, 128), lambda i: (0, 0)),
        ],
        out_shape=[
            jax.ShapeDtypeStruct((spins, size, size), jnp.float32),
            jax.ShapeDtypeStruct((8, 128), jnp.float32),
        ],
        compiler_params=params(),
    )(nu, x, *parts)


def shift_kernel(nu_ref, parts_ref, out_ref):
    total = jnp.sum(parts_ref[...], axis=0)
    row = lax.broadcasted_iota(jnp.int32, out_ref.shape, 0)
    sigma = total[0:1]
    tau = 1.0 / jnp.sqrt(total[1:2])
    out_ref[...] = jnp.where(row == 0, sigma, jnp.where(row == 1, tau, nu_ref[...]))


def shift_rows(nu, parts):
    return pl.pallas_call(
        shift_kernel,
        out_shape=jax.ShapeDtypeStruct((8, 128), jnp.float32),
        compiler_params=params(),
    )(nu, parts)


def combine_kernel(second, spins, count, *refs):
    scale_ref = refs[0]
    sigma, tau, nu = scale_ref[0:1, 0:1], scale_ref[1:2, 0:1], scale_ref[2:3, 0:1]
    w_ref = refs[1]
    x_ref = refs[2] if second else None
    base = 3 if second else 2
    part_refs = refs[base : base + count]
    out_ref = refs[base + count]
    size = out_ref.shape[2]
    index = 0
    for s in range(spins):
        total = None
        for part in spin_parts(spins, s):
            value = part_refs[index][...]
            index += 1
            total = value if total is None else total + value
        if second:
            x = x_ref[:, s * size : (s + 1) * size]
            inner = w_ref[s] - sigma * (nu * x)
            out_ref[s] = tau * tau * ((total - sigma * w_ref[s]) - sigma * inner)
        else:
            out_ref[s] = tau * (total - sigma * w_ref[s])


def combine(scales, w, x, parts, spins):
    size = w.shape[1]
    step = 128
    spec = pl.BlockSpec((step, size), lambda i: (i, 0))
    state = pl.BlockSpec((spins, step, size), lambda i: (0, i, 0))
    second = x is not None
    arrays = [scales, w] + ([x] if second else []) + list(parts)
    specs = [pl.BlockSpec((8, 128), lambda i: (0, 0)), state]
    if second:
        specs.append(pl.BlockSpec((step, spins * size), lambda i: (i, 0)))
    return pl.pallas_call(
        functools.partial(combine_kernel, second, spins, len(parts)),
        grid=(size // step,),
        in_specs=specs + [spec] * len(parts),
        out_specs=state,
        out_shape=jax.ShapeDtypeStruct((spins, size, size), jnp.float32),
        compiler_params=params(),
    )(*arrays)


PAIRS = [(i, j) for j in range(5) for i in range(j + 1) if (i, j) != (4, 4)]


def gram_kernel(spins, count, *refs):
    scale_ref, x_ref, y_ref, w2_ref, w3_ref = refs[:5]
    part_refs = refs[5 : 5 + count]
    out_ref = refs[5 + count]
    sigma, tau, nu = scale_ref[0:1, 0:1], scale_ref[1:2, 0:1], scale_ref[2:3, 0:1]
    sums = [jnp.zeros((1, 128), jnp.float32)] * len(PAIRS)
    index = 0
    for s in range(spins):
        total = None
        for part in spin_parts(spins, s):
            value = part_refs[index][...]
            index += 1
            total = value if total is None else total + value
        w = [nu * x_ref[:, s], None, w2_ref[:, s], w3_ref[:, s], None]
        w[1] = tau * (y_ref[:, s] - sigma * w[0])
        w[4] = tau * (total - sigma * w[3])
        for p, (i, j) in enumerate(PAIRS):
            sums[p] = sums[p] + jnp.sum(w[i] * w[j], axis=0, keepdims=True)
    for p in range(len(PAIRS)):
        out_ref[p : p + 1, :] = jnp.broadcast_to(jnp.sum(sums[p], axis=1, keepdims=True), (1, 128))
    for p in range(len(PAIRS), ROWS):
        out_ref[p : p + 1, :] = jnp.zeros((1, 128), jnp.float32)


def gram_rows(scales, quarters, parts, spins):
    return pl.pallas_call(
        functools.partial(gram_kernel, spins, len(parts)),
        out_shape=jax.ShapeDtypeStruct((ROWS, 128), jnp.float32),
        compiler_params=params(),
    )(scales, *quarters, *parts)


def weights_kernel(step_size, scale_ref, sums_ref, out_ref):
    sigma, tau, nu = scale_ref[0:1], scale_ref[1:2], scale_ref[2:3]
    gram = {}
    for p, (i, j) in enumerate(PAIRS):
        gram[(i, j)] = sums_ref[p : p + 1, :]
    low = {}
    inverse = []
    for j in range(4):
        pivot = gram[(j, j)]
        for k in range(j):
            pivot = pivot - low[(j, k)] * low[(j, k)]
        low[(j, j)] = jnp.sqrt(pivot)
        inverse.append(1.0 / low[(j, j)])
        for i in range(j + 1, 5):
            value = gram[(j, i)]
            for k in range(j):
                value = value - low[(i, k)] * low[(j, k)]
            low[(i, j)] = value * inverse[j]
    stretch = 1.0 / tau
    beta = [low[(j + 1, j + 1)] * inverse[j] * stretch for j in range(3)]
    alpha = []
    for j in range(4):
        value = low[(j + 1, j)] * stretch
        if j > 0:
            value = value - low[(j, j - 1)] * beta[j - 1]
        alpha.append(sigma + value * inverse[j])
    factor = step_size / 16.0
    diag = [factor * a for a in alpha]
    off = [factor * b for b in beta]
    one = jnp.ones_like(sigma)
    zero = jnp.zeros_like(sigma)
    result = {(i, j): one if i == j else zero for i in range(4) for j in range(i, 4)}

    def entry(table, i, j):
        return table[(min(i, j), max(i, j))]

    for degree in range(8, 0, -1):
        fresh = {}
        for i in range(4):
            for j in range(i, 4):
                value = diag[i] * entry(result, i, j)
                if i > 0:
                    value = value + off[i - 1] * entry(result, i - 1, j)
                if i < 3:
                    value = value + off[i] * entry(result, i + 1, j)
                value = value * (1.0 / degree)
                fresh[(i, j)] = one + value if i == j else value
        result = fresh
    for squaring in range(4):
        fresh = {}
        for i in range(4):
            for j in range(i, 4):
                if squaring == 3 and i > 0:
                    continue
                value = entry(result, i, 0) * entry(result, 0, j)
                for k in range(1, 4):
                    value = value + entry(result, i, k) * entry(result, k, j)
                fresh[(i, j)] = value
        result = fresh
    column = [result[(0, j)] for j in range(4)]
    size = jnp.sqrt(sum(c * c for c in column))
    c = [None] * 4
    for i in range(3, -1, -1):
        value = column[i]
        for j in range(i + 1, 4):
            value = value - low[(j, i)] * c[j]
        c[i] = value * inverse[i]
    norm = low[(0, 0)] / nu
    c = [norm * v for v in c]
    rows = [(c[0] - c[1] * tau * sigma) * nu, c[1] * tau, c[2], c[3], 1.0 / (norm * size)]
    for p, value in enumerate(rows):
        out_ref[p : p + 1, :] = value
    for p in range(len(rows), 8):
        out_ref[p : p + 1, :] = zero


def basis_weights(scales, sums, step_size):
    return pl.pallas_call(
        functools.partial(weights_kernel, step_size),
        out_shape=jax.ShapeDtypeStruct((8, 128), jnp.float32),
        compiler_params=params(),
    )(scales, sums)


def result_kernel(spins, weight_ref, x_ref, y_ref, w2_ref, w3_ref, out_ref):
    size = out_ref.shape[2]
    for s in range(spins):
        value = weight_ref[0:1, 0:1] * x_ref[:, s * size : (s + 1) * size]
        value = value + weight_ref[1:2, 0:1] * y_ref[s]
        value = value + weight_ref[2:3, 0:1] * w2_ref[s]
        out_ref[s] = value + weight_ref[3:4, 0:1] * w3_ref[s]


def weighted(weights, x, y, w2, w3, spins):
    size = x.shape[0]
    step = 128
    state = pl.BlockSpec((spins, step, size), lambda i: (0, i, 0))
    return pl.pallas_call(
        functools.partial(result_kernel, spins),
        grid=(size // step,),
        in_specs=[
            pl.BlockSpec((8, 128), lambda i: (0, 0)),
            pl.BlockSpec((step, spins * size), lambda i: (i, 0)),
        ]
        + [state] * 3,
        out_specs=state,
        out_shape=jax.ShapeDtypeStruct((spins, size, size), jnp.float32),
        compiler_params=params(),
    )(weights, x, y, w2, w3)


def quarter_state(state, offset, width):
    return jnp.swapaxes(lax.dynamic_slice_in_dim(state, offset, width, 2), 0, 1)


def evolve(x, nu, apply_full, apply_quarter, step_size, spins, offset, width):
    size = x.shape[0]
    blocks = [x[:, s * size : (s + 1) * size] for s in range(spins)]
    parts, _ = apply_full(blocks, None)
    y, sums = first_combine(x, nu, parts, spins)
    parts, totals = apply_full([y[s] for s in range(spins)], sums)
    scales = shift_rows(nu, totals)
    w2 = combine(scales, y, x, parts, spins)
    parts, _ = apply_full([w2[s] for s in range(spins)], None)
    w3 = combine(scales, w2, None, parts, spins)
    parts = apply_quarter([w3[s] for s in range(spins)])
    x_quarter = lax.dynamic_slice_in_dim(x.reshape(size, spins, size), offset, width, 2)
    quarters = [x_quarter] + [quarter_state(w, offset, width) for w in (y, w2, w3)]
    rows = gram_rows(scales, quarters, parts, spins)
    total = sum_over_col(jnp.sum(exchange(rows, "sec"), axis=0))
    weights = basis_weights(scales, total, step_size)
    return weighted(weights, x, y, w2, w3, spins), weights


def body(site_tensor, left_env, right_env, bond_env, sector_sizes):
    col_rows = site_tensor.shape[0]
    size = left_env.shape[2]
    sector = lax.axis_index("sec")
    last = lax.axis_size("sec") - 1
    offset = lax.axis_index("col") * col_rows

    left = left_env[0]
    site_block = site_tensor[:, 0]
    site_full = gather_col(site_block, 0)
    right = gather_col(right_env[0], 2)
    site_nu = inverse_norm(exchange(norm_rows(site_block), ("col", "sec")))

    below_sum = to_next(left[0] + left[1] + ANISOTROPY * left[4])
    below_four = to_next(left[4])
    above_sum = to_previous(left[0] - left[1] + ANISOTROPY * left[4])
    above_four = to_previous(left[4])
    raise_here = jnp.where(sector < last, ROOT_TWO * left[2], 0.0)
    lower_here = jnp.where(sector > 0, ROOT_TWO * left[3], 0.0)
    right_plus = right[4] + right[1]
    right_minus = right[4] - right[1]
    half = ROOT_TWO / 2
    up_matrix = half * right[2].T
    down_matrix = half * right[3].T

    lefts = dict(
        bs=below_sum, b4=below_four, us=above_sum, u4=above_four, h4=left[4], h0=left[0],
        low=lower_here, lowt=lower_here.T, rai=raise_here, rait=raise_here.T,
    )
    lefts_quarter = {k: lax.dynamic_slice_in_dim(v, offset, col_rows, 1) for k, v in lefts.items()}

    def apply_site(env, blocks, sums):
        x0, x1, x2 = blocks
        z1 = mm(x1, env["h4"])
        send_down1 = mm(down_matrix, z1)
        send_up1 = mm(up_matrix, z1)
        above1 = to_previous(send_down1)
        below1 = to_next(send_up1)
        z0 = mm(x0, env["b4"])
        above0 = to_previous(mm(down_matrix, z0))
        z2 = mm(x2, env["u4"])
        send_up2 = mm(up_matrix, z2)
        below2 = to_next(send_up2)
        totals = None
        if sums is not None:
            sums, _ = lax.optimization_barrier((sums, send_up2))
            totals = exchange(sums, "sec")
        p0 = mm(x0, env["bs"]) + mm(x1, env["low"])
        p1 = mm(x1, env["h0"]) + mm(x0, env["lowt"]) + mm(x2, env["rait"])
        p2 = mm(x2, env["us"]) + mm(x1, env["rai"])
        y0 = mm(right[0], p0) + mm(right_plus, z0)
        y1 = mm(right[0], p1) + mm(right[4], z1)
        y2 = mm(right[0], p2) + mm(right_minus, z2)
        return [y0, below1, y1, below2, above0, y2, above1], totals

    evolved, weights = evolve(
        site_full,
        site_nu,
        lambda blocks, sums: apply_site(lefts, blocks, sums),
        lambda blocks: apply_site(lefts_quarter, blocks, None)[0],
        -TIME_STEP,
        3,
        offset,
        col_rows,
    )
    gram = None
    for s in range(3):
        term = lax.dot_general(
            evolved[s], evolved[s], (((1,), (1,)), ((), ())), precision=HIGHEST
        )
        gram = term if gram is None else gram + term
    live = (jnp.arange(size) < sector_sizes[0]).astype(jnp.float32)
    gram = gram + (1.0 - live)[:, None] * jnp.eye(size, dtype=jnp.float32)
    factor = jnp.linalg.cholesky(gram[None])[0]
    bond_scale = math.sqrt(3.0 * size)
    start = factor * live[:, None] * live[None, :] / bond_scale
    bond_nu = jnp.broadcast_to(weights[4:5] * bond_scale, (8, 128))

    bond = bond_env[0]
    bonds = dict(dn=ROOT_TWO * bond[3], up=ROOT_TWO * bond[2], b0=bond[0], b1=bond[1], b4=bond[4])
    bonds_quarter = {k: lax.dynamic_slice_in_dim(v, offset, col_rows, 1) for k, v in bonds.items()}

    def apply_bond(env, blocks, sums):
        (x,) = blocks
        from_above = to_previous(mm(down_matrix, mm(x, env["dn"])))
        send_up = mm(up_matrix, mm(x, env["up"]))
        from_below = to_next(send_up)
        totals = None
        if sums is not None:
            sums, _ = lax.optimization_barrier((sums, send_up))
            totals = exchange(sums, "sec")
        y = mm(right[0], mm(x, env["b0"]))
        y = y + mm(right[1], mm(x, env["b1"]))
        y = y + mm(right[4], mm(x, env["b4"]))
        return [y, from_above, from_below], totals

    evolved_bond, _ = evolve(
        start,
        bond_nu,
        lambda blocks, sums: apply_bond(bonds, blocks, sums),
        lambda blocks: apply_bond(bonds_quarter, blocks, None)[0],
        TIME_STEP,
        1,
        offset,
        col_rows,
    )

    out_site = jnp.swapaxes(lax.dynamic_slice_in_dim(evolved, offset, col_rows, 1), 0, 1)
    out_site = out_site.reshape(col_rows, 1, 3 * size)
    out_bond = lax.dynamic_slice_in_dim(evolved_bond[0], offset, col_rows, 0)[:, None, :]
    return (out_site, out_bond)


def solution(mesh):
    in_specs = (
        P("col", "sec", None),
        P("sec", None, None, None),
        P("sec", None, None, "col"),
        P("sec", None, None, None),
        P("sec"),
    )
    out_specs = (P("col", "sec", None), P("col", "sec", None))
    return jax.shard_map(body, mesh=mesh, in_specs=in_specs, out_specs=out_specs, check_vma=False)
```

time: 770 us -> 653 us (0.85)
  waiting for transfers between devices: 134 us -> 72.1 us
  Pallas kernels: 0 us -> 49 us
  other arithmetic: 137 us -> 92.6 us
  starting transfers between devices: 167 us -> 131 us
  matrix products: 256 us -> 227 us
  between operations: 46.8 us -> 19.5 us
  blocking collectives: 0 us -> 19.1 us
  local copies, waits for them, and re-layouts: 15.9 us -> 33.9 us
    ppermute x70 -> x6, starting transfers between devices: 113 us -> 8.18 us  [sum_over_col(): lax.ppermute(rows, 'col', [(i, (i + step) % count) for i in range(count)])]
    ppermute x70 -> x6, waiting for transfers between devices: 62.1 us -> 1.24 us  [sum_over_col(): lax.ppermute(rows, 'col', [(i, (i + step) % count) for i in range(count)])]
    pallas_call x0 -> x16, Pallas kernels: none -> 49 us  [the longest x2 18.8 us: gram_rows(): pl.pallas_call(functools.partial(gram_kernel, spins, len(parts)), out_sha...]
    all_to_all x0 -> x4, starting transfers between devices: none -> 44.4 us  [exchange(): return lax.all_to_all(sent, axis, 0, 0)]
    all_gather x2, waiting for transfers between devices: 70.8 us -> 32.8 us  [gather_col(): return lax.all_gather(block, 'col', axis=axis, tiled=True)]
    dot_general x112 -> x120, matrix products: 245 us -> 220 us  [mm(): return jnp.dot(left, right, precision=HIGH)]
    ppermute x9 -> x14, waiting for transfers between devices: 0.02 us -> 21.7 us  [to_previous(): return lax.ppermute(block, 'sec', [(i + 1, i) for i in range(count - 1)])]
    reduce_sum x31 -> x2, other arithmetic: 21 us -> 0.07 us  [evolve(): total = sum_over_col(jnp.sum(exchange(rows, 'sec'), axis=0))]
  transfers between devices with their start and end apart: 90 -> 40, of which waited for: 44 -> 13; matrix products, arithmetic and copies ran while one was open for 25% -> 26% of each run, Pallas kernels for 0% -> 0%
where the time goes in v2:
time: 653 us; the launch traced here: 645 us
  matrix products  227 us (35%)
  starting transfers between devices  131 us (20%)
  other arithmetic  92.6 us (14%)
  waiting for transfers between devices  72.1 us (11%)
  Pallas kernels  49 us (8%)
  local copies, waits for them, and re-layouts  33.9 us (5%)
  between operations  19.5 us (3%)
  blocking collectives  19.1 us (3%)
    dot_general x120, matrix products, mm(): return jnp.dot(left, right, precision=HIGH)  220 us
    another operation x14, other arithmetic, body(): factor = jnp.linalg.cholesky(gram[None])[0]  78.9 us
    ppermute x14, starting transfers between devices, to_next(): return lax.ppermute(block, 'sec', [(i, i + 1) for i in range(count - 1)])  47.8 us
    all_to_all x4, starting transfers between devices, exchange(): return lax.all_to_all(sent, axis, 0, 0)  44.4 us
    all_gather x2, waiting for transfers between devices, gather_col(): return lax.all_gather(block, 'col', axis=axis, tiled=True)  32.8 us
    ppermute x14, starting transfers between devices, to_previous(): return lax.ppermute(block, 'sec', [(i + 1, i) for i in range(count - 1)])  30.9 us
    ppermute x14, waiting for transfers between devices, to_previous(): return lax.ppermute(block, 'sec', [(i + 1, i) for i in range(count - 1)])  21.7 us
    all_to_all x1, blocking collectives, exchange(): return lax.all_to_all(sent, axis, 0, 0)  19.1 us
  transfers between devices with their start and end apart: 40, of which 13 were waited for; matrix products, arithmetic and copies ran while one was open for 26% of the time, Pallas kernels for 0%

profile of v2, /device:TPU:1, one launch (start us, length us, event | category | flops | bytes accessed | tf_op | source)
XLA Modules:
  0.0 645.1 jit_solution(4486695239529616786)
XLA Ops:
  12.4 11.5 %all-to-all-start = ((f32[128,8,128]{2,1,0:T(8,128)}), f32[128,8,128]{2,1,0:T(8,128)S(1)}, u32[]{:S(2)}, u32[]{:S(2)}) async-start(f32[128,8,128]{2,1,0:T(8,128)} %broadcast_in_dim.29), calls=%async_computation | async-start | bytes 1048576 | tf_op jit(solution)/shard_map/all_to_all | solution.py:46
  43.9 14.9 %all-gather.5.cloned.1.call-done = f32[512,1,1536]{2,0,1:T(8,128)} async-done(((f32[128,1,1536]{2,0,1:T(8,128)}), f32[512,1,1536]{2,0,1:T(8,128)}) %all-gather.5.cloned.1.call-update) | async-done | bytes 3145744 | tf_op jit(solution)/shard_map/all_gather | solution.py:32
  102.5 17.9 %all-gather.7.cloned.1.call-done = f32[1,5,512,512]{3,2,1,0:T(8,128)} async-done(((f32[1,5,512,128]{3,2,1,0:T(8,128)}), f32[1,5,512,512]{3,2,1,0:T(8,128)}) %all-gather.7.cloned.1.call-update) | async-done | bytes 5242896 | tf_op jit(solution)/shard_map/all_gather | solution.py:32
  150.9 7.2 %collective-permute-done.7.refs_8_ = f32[512,512]{1,0:T(8,128)} collective-permute-done((f32[512,512]{1,0:T(8,128)S(1)}, f32[512,512]{1,0:T(8,128)}, u32[]{:S(2)}, u32[]{:S(2)}) %collective-permute-start.7) | collective-permute-done | bytes 1048608 | tf_op jit(solution)/shard_map/ppermute | solution.py:28
  158.1 5.8 shard_map.70
  210.0 10.6 %all-to-all-start.1 = ((f32[32,8,128]{2,1,0:T(8,128)}), f32[32,8,128]{2,1,0:T(8,128)S(1)}, u32[]{:S(2)}, u32[]{:S(2)}) async-start(f32[32,8,128]{2,1,0:T(8,128)} %broadcast_in_dim.31), calls=%async_computation.1 | async-start | bytes 262144 | tf_op jit(solution)/shard_map/all_to_all | solution.py:46
  235.4 7.3 %shard_map.72.refs_1_.w2_ref = f32[3,512,512]{2,1,0:T(8,128)} custom-call(f32[8,128]{1,0:T(8,128)S(1)} %shard_map.71.refs_0_.scale_ref, f32[3,512,512]{2,1,0:T(8,128)} %get-tuple-element.9.refs_1_.y_ref, f32[512,1536]{1,0:T(8,128)} %bitcast.541, f32[512,512]{1,0:T(8,128)S(1)} %convolution_add_fusion.19.refs_3_, f32[512,512]{1,0:T(8,128)} %collective-permute-done.8.refs_4_, ...), custom_call_target="tpu_custom_call" | custom-call | tf_op jit(solution)/shard_map/pallas_call | solution.py:193
  289.5 5.1 shard_map.73.w3_ref
  328.2 14.2 %shard_map.74 = f32[16,128]{1,0:T(8,128)S(1)} custom-call(f32[8,128]{1,0:T(8,128)S(1)} %shard_map.71.refs_0_.scale_ref, f32[512,3,128]{2,1,0:T(4,128)S(1)} %copy.159.refs_1_, f32[512,3,128]{2,1,0:T(4,128)S(1)} %dynamic-slice_bitcast_fusion.refs_2_, f32[512,3,128]{2,1,0:T(4,128)S(1)} %bitcast.522, f32[512,3,128]{2,1,0:T(4,128)S(1)} %bitcast.523, ...), custom_call_target="tpu_custom_call" | custom-call | tf_op jit(solution)/shard_map/pallas_call | solution.py:231
  343.1 12.5 %all-to-all-start.2 = ((f32[32,16,128]{2,1,0:T(8,128)}), f32[32,16,128]{2,1,0:T(8,128)S(1)}, u32[]{:S(2)}, u32[]{:S(2)}) async-start(f32[32,16,128]{2,1,0:T(8,128)} %broadcast_in_dim.32), calls=%async_computation.2 | async-start | bytes 524288 | tf_op jit(solution)/shard_map/all_to_all | solution.py:46
  355.7 4.9 slice_multiply_fusion.2
  370.3 5.9 shard_map.76
  382.5 11.7 %custom-call.31 = f32[1,128,128]{2,1,0:T(8,128)S(1)} custom-call(f32[1,128,128]{2,1,0:T(8,128)S(1)} %cholesky.267), custom_call_target="Cholesky" | custom-call | tf_op jit(solution)/shard_map/jit(cholesky)/cholesky | solution.py:445
  394.4 10.0 %custom-call.32 = f32[1,1,128,128]{2,3,1,0:T(8,128)S(1)} custom-call(f32[1,1,128,128]{3,2,1,0:T(8,128)S(1)} %get-tuple-element.43), custom_call_target="InvertDiagBlocksLowerTriangular" | custom-call | tf_op jit(solution)/shard_map/jit(cholesky)/cholesky | solution.py:445
  405.0 11.7 %custom-call.33 = f32[1,128,128]{2,1,0:T(8,128)S(1)} custom-call(f32[1,128,128]{2,1,0:T(8,128)S(1)} %cholesky.271), custom_call_target="Cholesky" | custom-call | tf_op jit(solution)/shard_map/jit(cholesky)/cholesky | solution.py:445
  416.8 9.8 %custom-call.34 = f32[1,1,128,128]{2,3,1,0:T(8,128)S(1)} custom-call(f32[1,1,128,128]{3,2,1,0:T(8,128)S(1)} %get-tuple-element.40), custom_call_target="InvertDiagBlocksLowerTriangular" | custom-call | tf_op jit(solution)/shard_map/jit(cholesky)/cholesky | solution.py:445
  427.3 11.7 %custom-call.35 = f32[1,128,128]{2,1,0:T(8,128)S(1)} custom-call(f32[1,128,128]{2,1,0:T(8,128)S(1)} %cholesky.276), custom_call_target="Cholesky" | custom-call | tf_op jit(solution)/shard_map/jit(cholesky)/cholesky | solution.py:445
  439.7 10.2 %custom-call.36 = f32[1,1,128,128]{2,3,1,0:T(8,128)S(1)} custom-call(f32[1,1,128,128]{3,2,1,0:T(8,128)S(1)} %get-tuple-element.37), custom_call_target="InvertDiagBlocksLowerTriangular" | custom-call | tf_op jit(solution)/shard_map/jit(cholesky)/cholesky | solution.py:445
  450.4 11.7 %custom-call.37 = f32[1,128,128]{2,1,0:T(8,128)S(1)} custom-call(f32[1,128,128]{2,1,0:T(8,128)S(1)} %fusion.19), custom_call_target="Cholesky" | custom-call | tf_op jit(solution)/shard_map/jit(cholesky)/cholesky | solution.py:445
  492.5 5.6 collective-permute-done.23.refs_3_
  524.0 9.7 %all-to-all-start.3 = ((f32[32,8,128]{2,1,0:T(8,128)}), f32[32,8,128]{2,1,0:T(8,128)S(1)}, u32[]{:S(2)}, u32[]{:S(2)}) async-start(f32[32,8,128]{2,1,0:T(8,128)} %broadcast_in_dim.65), calls=%async_computation.3 | async-start | bytes 262144 | tf_op jit(solution)/shard_map/all_to_all | solution.py:46
  571.9 6.0 collective-permute-done.27.refs_3_
  600.0 4.7 shard_map.81
  604.7 19.1 %all_to_all.25 = f32[32,16,128]{2,1,0:T(8,128)S(1)} all-to-all(f32[32,16,128]{2,1,0:T(8,128)S(1)} %broadcast_in_dim.66), channel_id=1, replica_groups=mesh['col'=4,'sec'=32] {'sec'}, dimensions={0} | all-to-all | bytes 524288 | tf_op jit(solution)/shard_map/all_to_all | solution.py:46
  (354 shorter events, 385.8 us)
Async XLA Ops:
  7.2 51.6 %all-gather.5.cloned.1.call-start = ((), (), s32[]{:S(2)}) async-start(), calls=%async_computation.5 | async-start | bytes 3932160 | tf_op jit(solution)/shard_map/all_gather | solution.py:32
  9.3 111.1 %all-gather.7.cloned.1.call-start = ((), (), s32[]{:S(2)}) async-start(), calls=%async_computation.6 | async-start | bytes 6553600 | tf_op jit(solution)/shard_map/all_gather | solution.py:32
  12.4 31.4 %all-to-all-start = ((f32[128,8,128]{2,1,0:T(8,128)}), f32[128,8,128]{2,1,0:T(8,128)S(1)}, u32[]{:S(2)}, u32[]{:S(2)}) async-start(f32[128,8,128]{2,1,0:T(8,128)} %broadcast_in_dim.29), calls=%async_computation | async-start | bytes 1048576 | tf_op jit(solution)/shard_map/all_to_all | solution.py:46
  28.3 49.9 %collective-permute-start.3 = (f32[512,512]{1,0:T(8,128)}, f32[512,512]{1,0:T(8,128)}, u32[]{:S(2)}, u32[]{:S(2)}) collective-permute-start(f32[512,512]{1,0:T(8,128)} %get-tuple-element.24), channel_id=1, source_target_pairs={{1,0},{2,1},{3,2},{4,3},{5,4},{6,5},{7,6},{8,7},{9,8},{10,9},{11,1... | collective-permute-start | bytes 3145736 | tf_op jit(solution)/shard_map/ppermute | solution.py:28
  31.2 50.2 %collective-permute-start.1 = (f32[512,512]{1,0:T(8,128)}, f32[512,512]{1,0:T(8,128)}, u32[]{:S(2)}, u32[]{:S(2)}) collective-permute-start(f32[512,512]{1,0:T(8,128)} %get-tuple-element.24), channel_id=1, source_target_pairs={{0,1},{1,2},{2,3},{3,4},{4,5},{5,6},{6,7},{7,8},{8,9},{9,10},{10,1... | collective-permute-start | bytes 3145736 | tf_op jit(solution)/shard_map/ppermute | solution.py:23
  37.5 56.8 %collective-permute-start.6 = (f32[512,512]{1,0:T(8,128)}, f32[512,512]{1,0:T(8,128)}, u32[]{:S(2)}, u32[]{:S(2)}) collective-permute-start(f32[512,512]{1,0:T(8,128)} %get-tuple-element.30), channel_id=1, source_target_pairs={{1,0},{2,1},{3,2},{4,3},{5,4},{6,5},{7,6},{8,7},{9,8},{10,9},{11,1... | collective-permute-start | bytes 3145736 | tf_op jit(solution)/shard_map/ppermute | solution.py:28
  40.1 58.3 %collective-permute-start = (f32[512,512]{1,0:T(8,128)}, f32[512,512]{1,0:T(8,128)}, u32[]{:S(2)}, u32[]{:S(2)}) collective-permute-start(f32[512,512]{1,0:T(8,128)} %get-tuple-element.31), channel_id=1, source_target_pairs={{0,1},{1,2},{2,3},{3,4},{4,5},{5,6},{6,7},{7,8},{8,9},{9,10},{10,1... | collective-permute-start | bytes 3145736 | tf_op jit(solution)/shard_map/ppermute | solution.py:23
  123.4 24.6 %collective-permute-start.4 = (f32[512,512]{1,0:T(8,128)S(1)}, f32[512,512]{1,0:T(8,128)S(1)}, u32[]{:S(2)}, u32[]{:S(2)}) collective-permute-start(f32[512,512]{1,0:T(8,128)S(1)} %fusion.245), channel_id=1, source_target_pairs={{0,1},{1,2},{2,3},{3,4},{4,5},{5,6},{6,7},{7,8},{8,9},{9,10},{10,1... | collective-permute-start | bytes 3145736 | tf_op jit(solution)/shard_map/ppermute | solution.py:23
  138.5 19.6 %collective-permute-start.7 = (f32[512,512]{1,0:T(8,128)S(1)}, f32[512,512]{1,0:T(8,128)}, u32[]{:S(2)}, u32[]{:S(2)}) collective-permute-start(f32[512,512]{1,0:T(8,128)S(1)} %fusion.269), channel_id=1, source_target_pairs={{1,0},{2,1},{3,2},{4,3},{5,4},{6,5},{7,6},{8,7},{9,8},{10,9},{11,1... | collective-permute-start | bytes 3145736 | tf_op jit(solution)/shard_map/ppermute | solution.py:28
  185.6 48.5 %collective-permute-start.10 = (f32[512,512]{1,0:T(8,128)}, f32[512,512]{1,0:T(8,128)}, u32[]{:S(2)}, u32[]{:S(2)}) collective-permute-start(f32[512,512]{1,0:T(8,128)} %fusion.267), channel_id=1, source_target_pairs={{1,0},{2,1},{3,2},{4,3},{5,4},{6,5},{7,6},{8,7},{9,8},{10,9},{11,1... | collective-permute-start | bytes 3145736 | tf_op jit(solution)/shard_map/ppermute | solution.py:28
  189.6 44.6 %collective-permute-start.11 = (f32[512,512]{1,0:T(8,128)}, f32[512,512]{1,0:T(8,128)}, u32[]{:S(2)}, u32[]{:S(2)}) collective-permute-start(f32[512,512]{1,0:T(8,128)} %fusion.265), channel_id=1, source_target_pairs={{1,0},{2,1},{3,2},{4,3},{5,4},{6,5},{7,6},{8,7},{9,8},{10,9},{11,1... | collective-permute-start | bytes 3145736 | tf_op jit(solution)/shard_map/ppermute | solution.py:28
  193.7 40.4 %collective-permute-start.8 = (f32[512,512]{1,0:T(8,128)}, f32[512,512]{1,0:T(8,128)}, u32[]{:S(2)}, u32[]{:S(2)}) collective-permute-start(f32[512,512]{1,0:T(8,128)} %fusion.241), channel_id=1, source_target_pairs={{0,1},{1,2},{2,3},{3,4},{4,5},{5,6},{6,7},{7,8},{8,9},{9,10},{10,1... | collective-permute-start | bytes 3145736 | tf_op jit(solution)/shard_map/ppermute | solution.py:23
  207.0 27.2 %collective-permute-start.9 = (f32[512,512]{1,0:T(8,128)}, f32[512,512]{1,0:T(8,128)}, u32[]{:S(2)}, u32[]{:S(2)}) collective-permute-start(f32[512,512]{1,0:T(8,128)} %fusion.243), channel_id=1, source_target_pairs={{0,1},{1,2},{2,3},{3,4},{4,5},{5,6},{6,7},{7,8},{8,9},{9,10},{10,1... | collective-permute-start | bytes 3145736 | tf_op jit(solution)/shard_map/ppermute | solution.py:23
  210.0 24.0 %all-to-all-start.1 = ((f32[32,8,128]{2,1,0:T(8,128)}), f32[32,8,128]{2,1,0:T(8,128)S(1)}, u32[]{:S(2)}, u32[]{:S(2)}) async-start(f32[32,8,128]{2,1,0:T(8,128)} %broadcast_in_dim.31), calls=%async_computation.1 | async-start | bytes 262144 | tf_op jit(solution)/shard_map/all_to_all | solution.py:46
  255.2 31.4 %collective-permute-start.13 = (f32[512,512]{1,0:T(8,128)S(1)}, f32[512,512]{1,0:T(8,128)S(1)}, u32[]{:S(2)}, u32[]{:S(2)}) collective-permute-start(f32[512,512]{1,0:T(8,128)S(1)} %fusion.237), channel_id=1, source_target_pairs={{0,1},{1,2},{2,3},{3,4},{4,5},{5,6},{6,7},{7,8},{8,9},{9,10},{10,1... | collective-permute-start | bytes 3145736 | tf_op jit(solution)/shard_map/ppermute | solution.py:23
  262.1 24.6 %collective-permute-start.14 = (f32[512,512]{1,0:T(8,128)S(1)}, f32[512,512]{1,0:T(8,128)S(1)}, u32[]{:S(2)}, u32[]{:S(2)}) collective-permute-start(f32[512,512]{1,0:T(8,128)S(1)} %fusion.263), channel_id=1, source_target_pairs={{1,0},{2,1},{3,2},{4,3},{5,4},{6,5},{7,6},{8,7},{9,8},{10,9},{11,1... | collective-permute-start | bytes 3145736 | tf_op jit(solution)/shard_map/ppermute | solution.py:28
  265.1 21.6 %collective-permute-start.12 = (f32[512,512]{1,0:T(8,128)S(1)}, f32[512,512]{1,0:T(8,128)S(1)}, u32[]{:S(2)}, u32[]{:S(2)}) collective-permute-start(f32[512,512]{1,0:T(8,128)S(1)} %fusion.239), channel_id=1, source_target_pairs={{0,1},{1,2},{2,3},{3,4},{4,5},{5,6},{6,7},{7,8},{8,9},{9,10},{10,1... | collective-permute-start | bytes 3145736 | tf_op jit(solution)/shard_map/ppermute | solution.py:23
  269.8 19.8 %collective-permute-start.15 = (f32[512,512]{1,0:T(8,128)S(1)}, f32[512,512]{1,0:T(8,128)}, u32[]{:S(2)}, u32[]{:S(2)}) collective-permute-start(f32[512,512]{1,0:T(8,128)S(1)} %fusion.261), channel_id=1, source_target_pairs={{1,0},{2,1},{3,2},{4,3},{5,4},{6,5},{7,6},{8,7},{9,8},{10,9},{11,1... | collective-permute-start | bytes 3145736 | tf_op jit(solution)/shard_map/ppermute | solution.py:28
  304.3 23.9 %collective-permute-start.17 = (f32[512,128]{1,0:T(8,128)S(1)}, f32[512,128]{1,0:T(8,128)S(1)}, u32[]{:S(2)}, u32[]{:S(2)}) collective-permute-start(f32[512,128]{1,0:T(8,128)S(1)} %fusion.233), channel_id=1, source_target_pairs={{0,1},{1,2},{2,3},{3,4},{4,5},{5,6},{6,7},{7,8},{8,9},{9,10},{10,1... | collective-permute-start | bytes 786440 | tf_op jit(solution)/shard_map/ppermute | solution.py:23
  308.7 19.5 %collective-permute-start.19 = (f32[512,128]{1,0:T(8,128)S(1)}, f32[512,128]{1,0:T(8,128)S(1)}, u32[]{:S(2)}, u32[]{:S(2)}) collective-permute-start(f32[512,128]{1,0:T(8,128)S(1)} %fusion.257), channel_id=1, source_target_pairs={{1,0},{2,1},{3,2},{4,3},{5,4},{6,5},{7,6},{8,7},{9,8},{10,9},{11,1... | collective-permute-start | bytes 786440 | tf_op jit(solution)/shard_map/ppermute | solution.py:28
  343.1 21.5 %all-to-all-start.2 = ((f32[32,16,128]{2,1,0:T(8,128)}), f32[32,16,128]{2,1,0:T(8,128)S(1)}, u32[]{:S(2)}, u32[]{:S(2)}) async-start(f32[32,16,128]{2,1,0:T(8,128)} %broadcast_in_dim.32), calls=%async_computation.2 | async-start | bytes 524288 | tf_op jit(solution)/shard_map/all_to_all | solution.py:46
  515.5 29.6 %collective-permute-start.25 = (f32[512,512]{1,0:T(8,128)}, f32[512,512]{1,0:T(8,128)}, u32[]{:S(2)}, u32[]{:S(2)}) collective-permute-start(f32[512,512]{1,0:T(8,128)} %fusion.253), channel_id=1, source_target_pairs={{1,0},{2,1},{3,2},{4,3},{5,4},{6,5},{7,6},{8,7},{9,8},{10,9},{11,1... | collective-permute-start | bytes 3145736 | tf_op jit(solution)/shard_map/ppermute | solution.py:28
  519.7 25.4 %collective-permute-start.26 = (f32[512,512]{1,0:T(8,128)}, f32[512,512]{1,0:T(8,128)}, u32[]{:S(2)}, u32[]{:S(2)}) collective-permute-start(f32[512,512]{1,0:T(8,128)} %fusion.229), channel_id=1, source_target_pairs={{0,1},{1,2},{2,3},{3,4},{4,5},{5,6},{6,7},{7,8},{8,9},{9,10},{10,1... | collective-permute-start | bytes 3145736 | tf_op jit(solution)/shard_map/ppermute | solution.py:23
  524.0 21.0 %all-to-all-start.3 = ((f32[32,8,128]{2,1,0:T(8,128)}), f32[32,8,128]{2,1,0:T(8,128)S(1)}, u32[]{:S(2)}, u32[]{:S(2)}) async-start(f32[32,8,128]{2,1,0:T(8,128)} %broadcast_in_dim.65), calls=%async_computation.3 | async-start | bytes 262144 | tf_op jit(solution)/shard_map/all_to_all | solution.py:46
  (61 other events, 927.6 us)
Sparse Core Ops, SparseCore 0:
  10.2 48.5 all-gather.4
  60.4 59.8 all-gather.6

commit v3 on v2

v3 whole, which is shorter than its diff:
```python
import functools
import math

import jax
import jax.numpy as jnp
from jax import lax
from jax.experimental import pallas as pl
from jax.experimental.pallas import tpu as pltpu
from jax.sharding import PartitionSpec as P

KRYLOV = 4
HIGHEST = lax.Precision.HIGHEST
HIGH = lax.Precision.HIGH
ROOT_TWO = math.sqrt(2.0)
ANISOTROPY = 0.5
TIME_STEP = 0.1
VMEM_LIMIT = 48 * 1024 * 1024


def to_next(block):
    count = lax.axis_size("sec")
    return lax.ppermute(block, "sec", [(i, i + 1) for i in range(count - 1)])


def to_previous(block):
    count = lax.axis_size("sec")
    return lax.ppermute(block, "sec", [(i + 1, i) for i in range(count - 1)])


def gather_col(block, axis):
    return lax.all_gather(block, "col", axis=axis, tiled=True)


def mm(left, right):
    return jnp.dot(left, right, precision=HIGH)


def params():
    return pltpu.CompilerParams(vmem_limit_bytes=VMEM_LIMIT)


def exchange(rows, axis):
    count = lax.axis_size(axis) if isinstance(axis, str) else lax.axis_size(axis[0]) * lax.axis_size(axis[1])
    sent = jnp.broadcast_to(rows[None], (count,) + rows.shape)
    return lax.all_to_all(sent, axis, 0, 0)


def row_of(values, shape):
    lane = lax.broadcasted_iota(jnp.int32, shape, 1)
    row = lax.broadcasted_iota(jnp.int32, shape, 0)
    out = jnp.zeros(shape, jnp.float32)
    for p, value in enumerate(values):
        out = jnp.where((lane == p) & (row == 0), value, out)
    return out


def spin_parts(spins, s):
    if spins == 1:
        return range(3)
    return range((2, 3, 2)[s])


def add_parts(spins, part_refs):
    totals = []
    index = 0
    for s in range(spins):
        total = None
        for part in spin_parts(spins, s):
            value = part_refs[index][...]
            index += 1
            total = value if total is None else total + value
        totals.append(total)
    return totals


SCALARS = jax.ShapeDtypeStruct((8, 128), jnp.float32)


def scalar_spec():
    return pl.BlockSpec((8, 128), lambda *i: (0, 0))


def norm_kernel(a_ref, out_ref):
    a = a_ref[...]
    out_ref[...] = row_of([jnp.sum(a * a)], out_ref.shape)


def norm_row(block):
    return pl.pallas_call(norm_kernel, out_shape=SCALARS, compiler_params=params())(block)


def inverse_norm_kernel(parts_ref, out_ref):
    total = jnp.sum(parts_ref[...], axis=0)
    out_ref[...] = jnp.broadcast_to(1.0 / jnp.sqrt(total[0:1, 0:1]), out_ref.shape)


def inverse_norm(parts):
    return pl.pallas_call(inverse_norm_kernel, out_shape=SCALARS, compiler_params=params())(parts)


def x_specs(spins, step, size):
    return [pl.BlockSpec((step, size), functools.partial(lambda s, i: (i, s), s)) for s in range(spins)]


def first_combine_kernel(spins, count, *refs):
    scale_ref, x_refs = refs[0], refs[1 : 1 + spins]
    part_refs = refs[1 + spins : 1 + spins + count]
    y_refs, sums_ref = refs[1 + spins + count : -1], refs[-1]
    nu = scale_ref[2:3, 0:1]
    cross = jnp.float32(0.0)
    square = jnp.float32(0.0)
    for s, total in enumerate(add_parts(spins, part_refs)):
        y = total * nu
        y_refs[s][...] = y
        cross += jnp.sum(x_refs[s][...] * nu * y)
        square += jnp.sum(y * y)

    @pl.when(pl.program_id(0) == 0)
    def _():
        sums_ref[...] = jnp.zeros_like(sums_ref)

    sums_ref[...] += row_of([cross, square], sums_ref.shape)


def first_combine(x, nu, parts, spins):
    size = x.shape[0]
    step = 128
    spec = pl.BlockSpec((step, size), lambda i: (i, 0))
    *y, sums = pl.pallas_call(
        functools.partial(first_combine_kernel, spins, len(parts)),
        grid=(size // step,),
        in_specs=[scalar_spec()] + x_specs(spins, step, size) + [spec] * len(parts),
        out_specs=[spec] * spins + [scalar_spec()],
        out_shape=[jax.ShapeDtypeStruct((size, size), jnp.float32)] * spins + [SCALARS],
        compiler_params=params(),
    )(nu, *([x] * spins), *parts)
    return y, sums


def shift_kernel(nu_ref, parts_ref, out_ref):
    total = jnp.sum(parts_ref[...], axis=0)
    row = lax.broadcasted_iota(jnp.int32, out_ref.shape, 0)
    sigma = total[0:1, 0:1]
    tau = 1.0 / jnp.sqrt(total[0:1, 1:2])
    out_ref[...] = jnp.where(row == 0, sigma, jnp.where(row == 1, tau, nu_ref[...]))


def shift_rows(nu, parts):
    return pl.pallas_call(shift_kernel, out_shape=SCALARS, compiler_params=params())(nu, parts)


def combine_kernel(second, spins, count, *refs):
    scale_ref = refs[0]
    sigma, tau, nu = scale_ref[0:1, 0:1], scale_ref[1:2, 0:1], scale_ref[2:3, 0:1]
    w_refs = refs[1 : 1 + spins]
    base = 1 + spins
    if second:
        x_refs = refs[base : base + spins]
        base += spins
    part_refs = refs[base : base + count]
    out_refs = refs[base + count :]
    for s, total in enumerate(add_parts(spins, part_refs)):
        w = w_refs[s][...]
        if second:
            inner = w - sigma * (nu * x_refs[s][...])
            out_refs[s][...] = tau * tau * ((total - sigma * w) - sigma * inner)
        else:
            out_refs[s][...] = tau * (total - sigma * w)


def combine(scales, w, x, parts, spins):
    size = w[0].shape[1]
    step = 128
    spec = pl.BlockSpec((step, size), lambda i: (i, 0))
    second = x is not None
    return pl.pallas_call(
        functools.partial(combine_kernel, second, spins, len(parts)),
        grid=(size // step,),
        in_specs=[scalar_spec()]
        + [spec] * spins
        + (x_specs(spins, step, size) if second else [])
        + [spec] * len(parts),
        out_specs=[spec] * spins,
        out_shape=[jax.ShapeDtypeStruct((size, size), jnp.float32)] * spins,
        compiler_params=params(),
    )(scales, *w, *([x] * spins if second else []), *parts)


PAIRS = [(i, j) for j in range(5) for i in range(j + 1) if (i, j) != (4, 4)]


def gram_kernel(spins, count, place_ref, *refs):
    scale_ref = refs[0]
    bases = [refs[1 + k * spins : 1 + (k + 1) * spins] for k in range(4)]
    part_refs = refs[1 + 4 * spins : 1 + 4 * spins + count]
    out_ref = refs[-1]
    sigma, tau, nu = scale_ref[0:1, 0:1], scale_ref[1:2, 0:1], scale_ref[2:3, 0:1]
    sums = [jnp.zeros((8, 128), jnp.float32)] * len(PAIRS)
    chunk = 64
    size = part_refs[0].shape[0]
    for start in range(0, size, chunk):
        index = 0
        for s in range(spins):
            total = None
            for part in spin_parts(spins, s):
                value = part_refs[index][start : start + chunk, :]
                index += 1
                total = value if total is None else total + value
            x, y, w2, w3 = (bases[k][s][start : start + chunk, :] for k in range(4))
            w = [nu * x, None, w2, w3, None]
            w[1] = tau * (y - sigma * w[0])
            w[4] = tau * (total - sigma * w[3])
            for p, (i, j) in enumerate(PAIRS):
                product = (w[i] * w[j]).reshape(chunk // 8, 8, 128)
                sums[p] = sums[p] + jnp.sum(product, axis=0)
    out_ref[...] = row_of([jnp.sum(value) for value in sums], out_ref.shape)


def gram_row(place, scales, x, states, parts, spins):
    size = x.shape[0]
    width = parts[0].shape[1]
    per = size // width

    x_quarter = [
        pl.BlockSpec((size, width), functools.partial(lambda s, i, p: (0, s * per + p[0]), s))
        for s in range(spins)
    ]
    quarter = pl.BlockSpec((size, width), lambda i, p: (0, p[0]))
    whole = pl.BlockSpec((size, width), lambda i, p: (0, 0))
    flat = [w for state in states for w in state]
    return pl.pallas_call(
        functools.partial(gram_kernel, spins, len(parts)),
        grid_spec=pltpu.PrefetchScalarGridSpec(
            num_scalar_prefetch=1,
            grid=(1,),
            in_specs=[scalar_spec()] + x_quarter + [quarter] * len(flat) + [whole] * len(parts),
            out_specs=scalar_spec(),
        ),
        out_shape=SCALARS,
        compiler_params=params(),
    )(place, scales, *([x] * spins), *flat, *parts)


def weights_kernel(step_size, scale_ref, sums_ref, out_ref):
    sigma, tau, nu = scale_ref[0:1], scale_ref[1:2], scale_ref[2:3]
    total = jnp.sum(sums_ref[...], axis=0)[0:1]
    gram = {}
    for p, (i, j) in enumerate(PAIRS):
        gram[(i, j)] = jnp.broadcast_to(total[:, p : p + 1], (1, 128))
    low = {}
    inverse = []
    for j in range(4):
        pivot = gram[(j, j)]
        for k in range(j):
            pivot = pivot - low[(j, k)] * low[(j, k)]
        low[(j, j)] = jnp.sqrt(pivot)
        inverse.append(1.0 / low[(j, j)])
        for i in range(j + 1, 5):
            value = gram[(j, i)]
            for k in range(j):
                value = value - low[(i, k)] * low[(j, k)]
            low[(i, j)] = value * inverse[j]
    stretch = 1.0 / tau
    beta = [low[(j + 1, j + 1)] * inverse[j] * stretch for j in range(3)]
    alpha = []
    for j in range(4):
        value = low[(j + 1, j)] * stretch
        if j > 0:
            value = value - low[(j, j - 1)] * beta[j - 1]
        alpha.append(sigma + value * inverse[j])
    factor = step_size / 16.0
    diag = [factor * a for a in alpha]
    off = [factor * b for b in beta]
    one = jnp.ones_like(sigma)
    zero = jnp.zeros_like(sigma)
    result = {(i, j): one if i == j else zero for i in range(4) for j in range(i, 4)}

    def entry(table, i, j):
        return table[(min(i, j), max(i, j))]

    for degree in range(8, 0, -1):
        fresh = {}
        for i in range(4):
            for j in range(i, 4):
                value = diag[i] * entry(result, i, j)
                if i > 0:
                    value = value + off[i - 1] * entry(result, i - 1, j)
                if i < 3:
                    value = value + off[i] * entry(result, i + 1, j)
                value = value * (1.0 / degree)
                fresh[(i, j)] = one + value if i == j else value
        result = fresh
    for squaring in range(4):
        fresh = {}
        for i in range(4):
            for j in range(i, 4):
                if squaring == 3 and i > 0:
                    continue
                value = entry(result, i, 0) * entry(result, 0, j)
                for k in range(1, 4):
                    value = value + entry(result, i, k) * entry(result, k, j)
                fresh[(i, j)] = value
        result = fresh
    column = [result[(0, j)] for j in range(4)]
    size = jnp.sqrt(sum(c * c for c in column))
    c = [None] * 4
    for i in range(3, -1, -1):
        value = column[i]
        for j in range(i + 1, 4):
            value = value - low[(j, i)] * c[j]
        c[i] = value * inverse[i]
    norm = low[(0, 0)] / nu
    c = [norm * v for v in c]
    rows = [(c[0] - c[1] * tau * sigma) * nu, c[1] * tau, c[2], c[3], 1.0 / (norm * size)]
    for p, value in enumerate(rows):
        out_ref[p : p + 1, :] = value
    for p in range(len(rows), 8):
        out_ref[p : p + 1, :] = zero


def basis_weights(scales, sums, step_size):
    return pl.pallas_call(
        functools.partial(weights_kernel, step_size),
        out_shape=SCALARS,
        compiler_params=params(),
    )(scales, sums)


def result_kernel(spins, *refs):
    weight_ref = refs[0]
    bases = [refs[1 + k * spins : 1 + (k + 1) * spins] for k in range(4)]
    out_refs = refs[1 + 4 * spins :]
    for s in range(spins):
        value = weight_ref[0:1, 0:1] * bases[0][s][...]
        for k in range(1, 4):
            value = value + weight_ref[k : k + 1, 0:1] * bases[k][s][...]
        out_refs[s][...] = value


def weighted(weights, x, states, spins):
    size = x.shape[0]
    step = 128
    spec = pl.BlockSpec((step, size), lambda i: (i, 0))
    flat = [w for state in states for w in state]
    return pl.pallas_call(
        functools.partial(result_kernel, spins),
        grid=(size // step,),
        in_specs=[scalar_spec()] + x_specs(spins, step, size) + [spec] * len(flat),
        out_specs=[spec] * spins,
        out_shape=[jax.ShapeDtypeStruct((size, size), jnp.float32)] * spins,
        compiler_params=params(),
    )(weights, *([x] * spins), *flat)


def output_kernel(spins, place_ref, *refs):
    weight_ref = refs[0]
    bases = [refs[1 + k * spins : 1 + (k + 1) * spins] for k in range(4)]
    out_ref = refs[1 + 4 * spins]
    size = bases[0][0].shape[1]
    for s in range(spins):
        value = weight_ref[0:1, 0:1] * bases[0][s][...]
        for k in range(1, 4):
            value = value + weight_ref[k : k + 1, 0:1] * bases[k][s][...]
        out_ref[:, s * size : (s + 1) * size] = value


def output_rows(place, weights, x, states, spins, rows):
    size = x.shape[0]
    x_rows = [
        pl.BlockSpec((rows, size), functools.partial(lambda s, i, p: (p[0], s), s))
        for s in range(spins)
    ]
    spec = pl.BlockSpec((rows, size), lambda i, p: (p[0], 0))
    flat = [w for state in states for w in state]
    return pl.pallas_call(
        functools.partial(output_kernel, spins),
        grid_spec=pltpu.PrefetchScalarGridSpec(
            num_scalar_prefetch=1,
            grid=(1,),
            in_specs=[scalar_spec()] + x_rows + [spec] * len(flat),
            out_specs=pl.BlockSpec((rows, spins * size), lambda i, p: (0, 0)),
        ),
        out_shape=jax.ShapeDtypeStruct((rows, spins * size), jnp.float32),
        compiler_params=params(),
    )(place, weights, *([x] * spins), *flat)


def evolve(place, x, nu, apply_full, apply_quarter, step_size, spins):
    size = x.shape[0]
    parts, _ = apply_full([x[:, s * size : (s + 1) * size] for s in range(spins)], None)
    y, sums = first_combine(x, nu, parts, spins)
    parts, totals = apply_full(y, sums)
    scales = shift_rows(nu, totals)
    w2 = combine(scales, y, x, parts, spins)
    parts, _ = apply_full(w2, None)
    w3 = combine(scales, w2, None, parts, spins)
    parts = apply_quarter(w3)
    states = [y, w2, w3]
    row = gram_row(place, scales, x, states, parts, spins)
    weights = basis_weights(scales, exchange(row, ("col", "sec")), step_size)
    return states, weights


def body(site_tensor, left_env, right_env, bond_env, sector_sizes):
    col_rows = site_tensor.shape[0]
    size = left_env.shape[2]
    sector = lax.axis_index("sec")
    last = lax.axis_size("sec") - 1
    col = lax.axis_index("col")
    place = col.reshape(1).astype(jnp.int32)

    def quarter_of(*matrices):
        picked = [lax.dynamic_slice_in_dim(m, col * col_rows, col_rows, 1) for m in matrices]
        return jnp.concatenate(picked, axis=1)

    def cut(matrix):
        return [matrix[:, i : i + col_rows] for i in range(0, matrix.shape[1], col_rows)]

    def join(*blocks):
        return jnp.concatenate(blocks, axis=1)

    left = left_env[0]
    site_block = site_tensor[:, 0]
    site_full = gather_col(site_block, 0)
    right = gather_col(right_env[0], 2)
    site_nu = inverse_norm(exchange(norm_row(site_block), ("col", "sec")))

    below_sum = to_next(left[0] + left[1] + ANISOTROPY * left[4])
    below_four = to_next(left[4])
    above_sum = to_previous(left[0] - left[1] + ANISOTROPY * left[4])
    above_four = to_previous(left[4])
    raise_here = jnp.where(sector < last, ROOT_TWO * left[2], 0.0)
    lower_here = jnp.where(sector > 0, ROOT_TWO * left[3], 0.0)
    right_plus = right[4] + right[1]
    right_minus = right[4] - right[1]
    half = ROOT_TWO / 2
    up_matrix = half * right[2].T
    down_matrix = half * right[3].T

    lower_turned, raise_turned = lower_here.T, raise_here.T
    quarter_zero = quarter_of(below_sum, below_four, lower_turned)
    quarter_one = quarter_of(left[4], lower_here, left[0], raise_here)
    quarter_two = quarter_of(above_sum, above_four, raise_turned)

    def apply_site(blocks, sums):
        x0, x1, x2 = blocks
        z1 = mm(x1, left[4])
        send_down1 = mm(down_matrix, z1)
        send_up1 = mm(up_matrix, z1)
        above1 = to_previous(send_down1)
        below1 = to_next(send_up1)
        z0 = mm(x0, below_four)
        above0 = to_previous(mm(down_matrix, z0))
        z2 = mm(x2, above_four)
        send_up2 = mm(up_matrix, z2)
        below2 = to_next(send_up2)
        totals = None
        if sums is not None:
            sums, _ = lax.optimization_barrier((sums, send_up2))
            totals = exchange(sums, "sec")
        p0 = mm(x0, below_sum) + mm(x1, lower_here)
        p1 = mm(x1, left[0]) + mm(x0, lower_turned) + mm(x2, raise_turned)
        p2 = mm(x2, above_sum) + mm(x1, raise_here)
        y0 = mm(right[0], p0) + mm(right_plus, z0)
        y1 = mm(right[0], p1) + mm(right[4], z1)
        y2 = mm(right[0], p2) + mm(right_minus, z2)
        return [y0, below1, y1, below2, above0, y2, above1], totals

    def apply_site_quarter(blocks):
        x0, x1, x2 = blocks
        p0, z0, p1 = cut(mm(x0, quarter_zero))
        z1, more0, more1, p2 = cut(mm(x1, quarter_one))
        last2, z2, last1 = cut(mm(x2, quarter_two))
        above = to_previous(mm(down_matrix, join(z0, z1)))
        below = to_next(mm(up_matrix, join(z1, z2)))
        y0, y1, y2 = cut(mm(right[0], join(p0 + more0, p1 + more1 + last1, p2 + last2)))
        y0 = y0 + mm(right_plus, z0)
        y1 = y1 + mm(right[4], z1)
        y2 = y2 + mm(right_minus, z2)
        above0, above1 = cut(above)
        below1, below2 = cut(below)
        return [y0, below1, y1, below2, above0, y2, above1]

    states, weights = evolve(
        place, site_full, site_nu, apply_site, apply_site_quarter, -TIME_STEP, 3
    )
    evolved = weighted(weights, site_full, states, 3)
    out_site = output_rows(place, weights, site_full, states, 3, col_rows)[:, None, :]
    gram = None
    for s in range(3):
        term = lax.dot_general(
            evolved[s], evolved[s], (((1,), (1,)), ((), ())), precision=HIGHEST
        )
        gram = term if gram is None else gram + term
    live = (jnp.arange(size) < sector_sizes[0]).astype(jnp.float32)
    gram = gram + (1.0 - live)[:, None] * jnp.eye(size, dtype=jnp.float32)
    factor = jnp.linalg.cholesky(gram[None])[0]
    bond_scale = math.sqrt(3.0 * size)
    start = factor * live[:, None] * live[None, :] / bond_scale
    bond_nu = jnp.broadcast_to(weights[4:5] * bond_scale, (8, 128))

    bond = bond_env[0]
    down_bond, up_bond = ROOT_TWO * bond[3], ROOT_TWO * bond[2]
    quarter_bond = quarter_of(down_bond, up_bond, bond[0], bond[1], bond[4])

    def apply_bond(blocks, sums):
        (x,) = blocks
        from_above = to_previous(mm(down_matrix, mm(x, down_bond)))
        send_up = mm(up_matrix, mm(x, up_bond))
        from_below = to_next(send_up)
        totals = None
        if sums is not None:
            sums, _ = lax.optimization_barrier((sums, send_up))
            totals = exchange(sums, "sec")
        y = mm(right[0], mm(x, bond[0]))
        y = y + mm(right[1], mm(x, bond[1]))
        y = y + mm(right[4], mm(x, bond[4]))
        return [y, from_above, from_below], totals

    def apply_bond_quarter(blocks):
        down, up, m0, m1, m4 = cut(mm(blocks[0], quarter_bond))
        from_above = to_previous(mm(down_matrix, down))
        from_below = to_next(mm(up_matrix, up))
        y = mm(right[0], m0) + mm(right[1], m1) + mm(right[4], m4)
        return [y, from_above, from_below]

    states, weights = evolve(place, start, bond_nu, apply_bond, apply_bond_quarter, TIME_STEP, 1)
    out_bond = output_rows(place, weights, start, states, 1, col_rows)[:, None, :]
    return (out_site, out_bond)


def solution(mesh):
    in_specs = (
        P("col", "sec", None),
        P("sec", None, None, None),
        P("sec", None, None, "col"),
        P("sec", None, None, None),
        P("sec"),
    )
    out_specs = (P("col", "sec", None), P("col", "sec", None))
    return jax.shard_map(body, mesh=mesh, in_specs=in_specs, out_specs=out_specs, check_vma=False)
```

time: 653 us -> 606 us (0.928)
  matrix products: 227 us -> 201 us
  local copies, waits for them, and re-layouts: 33.9 us -> 53 us
  blocking collectives: 19.1 us -> 0 us
  Pallas kernels: 49 us -> 33.3 us
    dot_general x120 -> x105, matrix products: 220 us -> 193 us  [mm(): return jnp.dot(left, right, precision=HIGH)]
    unnamed x95 -> x160, local copies, waits for them, and re-layouts: 12.6 us -> 35.5 us
    all_to_all x1 -> x0, blocking collectives: 19.1 us -> none  [exchange(): return lax.all_to_all(sent, axis, 0, 0)]
    all_to_all x4 -> x5, starting transfers between devices: 44.4 us -> 56.7 us  [exchange(): return lax.all_to_all(sent, axis, 0, 0)]
    pallas_call x8 -> x10, Pallas kernels: 19.7 us -> 8.02 us  [the longest x2 3.53 us: gram_row(): pl.pallas_call(functools.partial(gram_kernel, spins, len(parts)), grid_sp...]
    all_gather x2, waiting for transfers between devices: 32.8 us -> 24.1 us  [gather_col(): return lax.all_gather(block, 'col', axis=axis, tiled=True)]
    ppermute x6 -> x0, starting transfers between devices: 8.18 us -> none  [sum_over_col(): lax.ppermute(rows, 'col', [(i, (i + step) % count) for i in range(count)])]
    dynamic_slice x7 -> x10, local copies, waits for them, and re-layouts: 3.14 us -> 11.3 us  [quarter_of(): lax.dynamic_slice_in_dim(m, col * col_rows, col_rows, 1)]
  transfers between devices with their start and end apart: 40 -> 33, of which waited for: 13 -> 12; matrix products, arithmetic and copies ran while one was open for 26% -> 28% of each run, Pallas kernels for 0% -> 0%
where the time goes in v3:
time: 606 us; the launch traced here: 599 us
  matrix products  201 us (33%)
  starting transfers between devices  132 us (22%)
  other arithmetic  93.7 us (15%)
  waiting for transfers between devices  66.9 us (11%)
  local copies, waits for them, and re-layouts  53 us (9%)
  Pallas kernels  33.3 us (5%)
  between operations  19.8 us (3%)
    dot_general x105, matrix products, mm(): return jnp.dot(left, right, precision=HIGH)  193 us
    another operation x15, other arithmetic, body(): factor = jnp.linalg.cholesky(gram[None])[0]  79.6 us
    all_to_all x5, starting transfers between devices, exchange(): return lax.all_to_all(sent, axis, 0, 0)  56.7 us
    ppermute x13, starting transfers between devices, to_next(): return lax.ppermute(block, 'sec', [(i, i + 1) for i in range(count - 1)])  46 us
    unnamed x160, local copies, waits for them, and re-layouts  35.5 us
    ppermute x13, starting transfers between devices, to_previous(): return lax.ppermute(block, 'sec', [(i + 1, i) for i in range(count - 1)])  28.7 us
    all_gather x2, waiting for transfers between devices, gather_col(): return lax.all_gather(block, 'col', axis=axis, tiled=True)  24.1 us
    ppermute x13, waiting for transfers between devices, to_previous(): return lax.ppermute(block, 'sec', [(i + 1, i) for i in range(count - 1)])  21.8 us
  transfers between devices with their start and end apart: 33, of which 12 were waited for; matrix products, arithmetic and copies ran while one was open for 28% of the time, Pallas kernels for 0%

profile of v3, /device:TPU:1, one launch (start us, length us, event | category | flops | bytes accessed | tf_op | source)
XLA Modules:
  0.0 599.0 jit_solution(9079659658900000107)
XLA Ops:
  10.1 4.7 multiply_select_fusion
  18.1 4.5 collective-permute-start.1
  25.7 10.6 %all-to-all-start = ((f32[128,8,128]{2,1,0:T(8,128)}), f32[128,8,128]{2,1,0:T(8,128)S(1)}, u32[]{:S(2)}, u32[]{:S(2)}) async-start(f32[128,8,128]{2,1,0:T(8,128)} %broadcast_in_dim.31), calls=%async_computation | async-start | bytes 1048576 | tf_op jit(solution)/shard_map/all_to_all | solution.py:45
  51.1 4.9 fusion.222
  96.7 24.1 %all-gather.7.cloned.1.call-done = f32[1,5,512,512]{3,2,1,0:T(8,128)} async-done(((f32[1,5,512,128]{3,2,1,0:T(8,128)}), f32[1,5,512,512]{3,2,1,0:T(8,128)}) %all-gather.7.cloned.1.call-update) | async-done | bytes 5242896 | tf_op jit(solution)/shard_map/all_gather | solution.py:31
  123.2 4.5 collective-permute-start.2
  148.8 8.8 %collective-permute-done.5.refs_8_ = f32[512,512]{1,0:T(8,128)S(1)} collective-permute-done((f32[512,512]{1,0:T(8,128)S(1)}, f32[512,512]{1,0:T(8,128)S(1)}, u32[]{:S(2)}, u32[]{:S(2)}) %collective-permute-start.5) | collective-permute-done | bytes 1048608 | tf_op jit(solution)/shard_map/ppermute | solution.py:27
  158.6 4.9 shard_map.70
  180.9 8.9 %all-to-all-start.1 = ((f32[32,8,128]{2,1,0:T(8,128)}), f32[32,8,128]{2,1,0:T(8,128)S(1)}, u32[]{:S(2)}, u32[]{:S(2)}) async-start(f32[32,8,128]{2,1,0:T(8,128)} %broadcast_in_dim.33), calls=%async_computation.1 | async-start | bytes 262144 | tf_op jit(solution)/shard_map/all_to_all | solution.py:45
  231.8 5.8 shard_map.72
  282.7 4.7 shard_map.73
  311.2 15.5 %all-to-all-start.2 = ((f32[128,8,128]{2,1,0:T(8,128)}), f32[128,8,128]{2,1,0:T(8,128)S(1)}, u32[]{:S(2)}, u32[]{:S(2)}) async-start(f32[128,8,128]{2,1,0:T(8,128)} %broadcast_in_dim.34), calls=%async_computation.2 | async-start | bytes 1048576 | tf_op jit(solution)/shard_map/all_to_all | solution.py:45
  333.6 6.9 %all-to-all-done.2.sums_ref = f32[128,8,128]{2,1,0:T(8,128)S(1)} async-done(((f32[128,8,128]{2,1,0:T(8,128)}), f32[128,8,128]{2,1,0:T(8,128)S(1)}, u32[]{:S(2)}, u32[]{:S(2)}) %all-to-all-start.2) | async-done | bytes 524320 | tf_op jit(solution)/shard_map/all_to_all | solution.py:45
  340.9 5.4 shard_map.77
  352.5 11.7 %custom-call.31 = f32[1,128,128]{2,1,0:T(8,128)S(1)} custom-call(f32[1,128,128]{2,1,0:T(8,128)S(1)} %cholesky.267), custom_call_target="Cholesky" | custom-call | tf_op jit(solution)/shard_map/jit(cholesky)/cholesky | solution.py:497
  364.9 10.0 %custom-call.32 = f32[1,1,128,128]{2,3,1,0:T(8,128)S(1)} custom-call(f32[1,1,128,128]{3,2,1,0:T(8,128)S(1)} %get-tuple-element.79), custom_call_target="InvertDiagBlocksLowerTriangular" | custom-call | tf_op jit(solution)/shard_map/jit(cholesky)/cholesky | solution.py:497
  375.7 11.7 %custom-call.33 = f32[1,128,128]{2,1,0:T(8,128)S(1)} custom-call(f32[1,128,128]{2,1,0:T(8,128)S(1)} %cholesky.271), custom_call_target="Cholesky" | custom-call | tf_op jit(solution)/shard_map/jit(cholesky)/cholesky | solution.py:497
  388.1 9.8 %custom-call.34 = f32[1,1,128,128]{2,3,1,0:T(8,128)S(1)} custom-call(f32[1,1,128,128]{3,2,1,0:T(8,128)S(1)} %get-tuple-element.76), custom_call_target="InvertDiagBlocksLowerTriangular" | custom-call | tf_op jit(solution)/shard_map/jit(cholesky)/cholesky | solution.py:497
  398.5 11.7 %custom-call.35 = f32[1,128,128]{2,1,0:T(8,128)S(1)} custom-call(f32[1,128,128]{2,1,0:T(8,128)S(1)} %cholesky.276), custom_call_target="Cholesky" | custom-call | tf_op jit(solution)/shard_map/jit(cholesky)/cholesky | solution.py:497
  410.9 10.2 %custom-call.36 = f32[1,1,128,128]{2,3,1,0:T(8,128)S(1)} custom-call(f32[1,1,128,128]{3,2,1,0:T(8,128)S(1)} %get-tuple-element.73), custom_call_target="InvertDiagBlocksLowerTriangular" | custom-call | tf_op jit(solution)/shard_map/jit(cholesky)/cholesky | solution.py:497
  421.7 11.7 %custom-call.37 = f32[1,128,128]{2,1,0:T(8,128)S(1)} custom-call(f32[1,128,128]{2,1,0:T(8,128)S(1)} %fusion.17), custom_call_target="Cholesky" | custom-call | tf_op jit(solution)/shard_map/jit(cholesky)/cholesky | solution.py:497
  493.1 9.1 %all-to-all-start.3 = ((f32[32,8,128]{2,1,0:T(8,128)}), f32[32,8,128]{2,1,0:T(8,128)S(1)}, u32[]{:S(2)}, u32[]{:S(2)}) async-start(f32[32,8,128]{2,1,0:T(8,128)} %broadcast_in_dim.69), calls=%async_computation.3 | async-start | bytes 262144 | tf_op jit(solution)/shard_map/all_to_all | solution.py:45
  560.8 12.6 %all-to-all-start.4 = ((f32[128,8,128]{2,1,0:T(8,128)}), f32[128,8,128]{2,1,0:T(8,128)}, u32[]{:S(2)}, u32[]{:S(2)}) async-start(f32[128,8,128]{2,1,0:T(8,128)} %broadcast_in_dim.70), calls=%async_computation.4 | async-start | bytes 1048576 | tf_op jit(solution)/shard_map/all_to_all | solution.py:45
  581.8 5.0 all-to-all-done.4.sums_ref
  (388 shorter events, 361.4 us)
Async XLA Ops:
  7.2 62.7 %all-gather.5.cloned.1.call-start = ((), (), s32[]{:S(2)}) async-start(), calls=%async_computation.5 | async-start | bytes 3932160 | tf_op jit(solution)/shard_map/all_gather | solution.py:31
  9.3 111.5 %all-gather.7.cloned.1.call-start = ((), (), s32[]{:S(2)}) async-start(), calls=%async_computation.6 | async-start | bytes 6553600 | tf_op jit(solution)/shard_map/all_gather | solution.py:31
  18.1 48.5 %collective-permute-start.1 = (f32[512,512]{0,1:T(8,128)}, f32[512,512]{0,1:T(8,128)}, u32[]{:S(2)}, u32[]{:S(2)}) collective-permute-start(f32[512,512]{0,1:T(8,128)} %bitcast.462), channel_id=1, source_target_pairs={{0,1},{1,2},{2,3},{3,4},{4,5},{5,6},{6,7},{7,8},{8,9},{9,10},{10,1... | collective-permute-start | bytes 3145736 | tf_op jit(solution)/shard_map/ppermute | solution.py:22
  22.6 45.6 %collective-permute-start.3 = (f32[512,512]{0,1:T(8,128)}, f32[512,512]{0,1:T(8,128)}, u32[]{:S(2)}, u32[]{:S(2)}) collective-permute-start(f32[512,512]{0,1:T(8,128)} %bitcast.463), channel_id=1, source_target_pairs={{1,0},{2,1},{3,2},{4,3},{5,4},{6,5},{7,6},{8,7},{9,8},{10,9},{11,1... | collective-permute-start | bytes 3145736 | tf_op jit(solution)/shard_map/ppermute | solution.py:27
  25.7 38.0 %all-to-all-start = ((f32[128,8,128]{2,1,0:T(8,128)}), f32[128,8,128]{2,1,0:T(8,128)S(1)}, u32[]{:S(2)}, u32[]{:S(2)}) async-start(f32[128,8,128]{2,1,0:T(8,128)} %broadcast_in_dim.31), calls=%async_computation | async-start | bytes 1048576 | tf_op jit(solution)/shard_map/all_to_all | solution.py:45
  45.1 18.8 %collective-permute-start.6 = (f32[512,512]{0,1:T(8,128)}, f32[512,512]{0,1:T(8,128)}, u32[]{:S(2)}, u32[]{:S(2)}) collective-permute-start(f32[512,512]{0,1:T(8,128)} %get-tuple-element.56), channel_id=1, source_target_pairs={{1,0},{2,1},{3,2},{4,3},{5,4},{6,5},{7,6},{8,7},{9,8},{10,9},{11,1... | collective-permute-start | bytes 3145736 | tf_op jit(solution)/shard_map/ppermute | solution.py:27
  123.2 25.5 %collective-permute-start.2 = (f32[512,512]{1,0:T(8,128)S(1)}, f32[512,512]{1,0:T(8,128)S(1)}, u32[]{:S(2)}, u32[]{:S(2)}) collective-permute-start(f32[512,512]{1,0:T(8,128)S(1)} %fusion.200), channel_id=1, source_target_pairs={{0,1},{1,2},{2,3},{3,4},{4,5},{5,6},{6,7},{7,8},{8,9},{9,10},{10,1... | collective-permute-start | bytes 3145736 | tf_op jit(solution)/shard_map/ppermute | solution.py:22
  130.1 18.7 %collective-permute-start.7 = (f32[512,512]{1,0:T(8,128)S(1)}, f32[512,512]{1,0:T(8,128)S(1)}, u32[]{:S(2)}, u32[]{:S(2)}) collective-permute-start(f32[512,512]{1,0:T(8,128)S(1)} %fusion.218), channel_id=1, source_target_pairs={{1,0},{2,1},{3,2},{4,3},{5,4},{6,5},{7,6},{8,7},{9,8},{10,9},{11,1... | collective-permute-start | bytes 3145736 | tf_op jit(solution)/shard_map/ppermute | solution.py:27
  133.2 24.3 %collective-permute-start.5 = (f32[512,512]{1,0:T(8,128)S(1)}, f32[512,512]{1,0:T(8,128)S(1)}, u32[]{:S(2)}, u32[]{:S(2)}) collective-permute-start(f32[512,512]{1,0:T(8,128)S(1)} %fusion.220), channel_id=1, source_target_pairs={{1,0},{2,1},{3,2},{4,3},{5,4},{6,5},{7,6},{8,7},{9,8},{10,9},{11,1... | collective-permute-start | bytes 3145736 | tf_op jit(solution)/shard_map/ppermute | solution.py:27
  136.4 22.2 %collective-permute-start.4 = (f32[512,512]{1,0:T(8,128)S(1)}, f32[512,512]{1,0:T(8,128)}, u32[]{:S(2)}, u32[]{:S(2)}) collective-permute-start(f32[512,512]{1,0:T(8,128)S(1)} %fusion.198), channel_id=1, source_target_pairs={{0,1},{1,2},{2,3},{3,4},{4,5},{5,6},{6,7},{7,8},{8,9},{9,10},{10,1... | collective-permute-start | bytes 3145736 | tf_op jit(solution)/shard_map/ppermute | solution.py:22
  178.3 52.3 %collective-permute-start.9 = (f32[512,512]{1,0:T(8,128)}, f32[512,512]{1,0:T(8,128)}, u32[]{:S(2)}, u32[]{:S(2)}) collective-permute-start(f32[512,512]{1,0:T(8,128)} %fusion.196), channel_id=1, source_target_pairs={{0,1},{1,2},{2,3},{3,4},{4,5},{5,6},{6,7},{7,8},{8,9},{9,10},{10,1... | collective-permute-start | bytes 3145736 | tf_op jit(solution)/shard_map/ppermute | solution.py:22
  180.9 46.8 %all-to-all-start.1 = ((f32[32,8,128]{2,1,0:T(8,128)}), f32[32,8,128]{2,1,0:T(8,128)S(1)}, u32[]{:S(2)}, u32[]{:S(2)}) async-start(f32[32,8,128]{2,1,0:T(8,128)} %broadcast_in_dim.33), calls=%async_computation.1 | async-start | bytes 262144 | tf_op jit(solution)/shard_map/all_to_all | solution.py:45
  195.8 32.0 %collective-permute-start.8 = (f32[512,512]{1,0:T(8,128)}, f32[512,512]{1,0:T(8,128)}, u32[]{:S(2)}, u32[]{:S(2)}) collective-permute-start(f32[512,512]{1,0:T(8,128)} %fusion.194), channel_id=1, source_target_pairs={{0,1},{1,2},{2,3},{3,4},{4,5},{5,6},{6,7},{7,8},{8,9},{9,10},{10,1... | collective-permute-start | bytes 3145736 | tf_op jit(solution)/shard_map/ppermute | solution.py:22
  202.9 25.0 %collective-permute-start.11 = (f32[512,512]{1,0:T(8,128)}, f32[512,512]{1,0:T(8,128)}, u32[]{:S(2)}, u32[]{:S(2)}) collective-permute-start(f32[512,512]{1,0:T(8,128)} %fusion.214), channel_id=1, source_target_pairs={{1,0},{2,1},{3,2},{4,3},{5,4},{6,5},{7,6},{8,7},{9,8},{10,9},{11,1... | collective-permute-start | bytes 3145736 | tf_op jit(solution)/shard_map/ppermute | solution.py:27
  209.5 21.0 %collective-permute-start.10 = (f32[512,512]{1,0:T(8,128)}, f32[512,512]{1,0:T(8,128)}, u32[]{:S(2)}, u32[]{:S(2)}) collective-permute-start(f32[512,512]{1,0:T(8,128)} %fusion.216), channel_id=1, source_target_pairs={{1,0},{2,1},{3,2},{4,3},{5,4},{6,5},{7,6},{8,7},{9,8},{10,9},{11,1... | collective-permute-start | bytes 3145736 | tf_op jit(solution)/shard_map/ppermute | solution.py:27
  248.3 32.0 %collective-permute-start.14 = (f32[512,512]{1,0:T(8,128)S(1)}, f32[512,512]{1,0:T(8,128)S(1)}, u32[]{:S(2)}, u32[]{:S(2)}) collective-permute-start(f32[512,512]{1,0:T(8,128)S(1)} %fusion.212), channel_id=1, source_target_pairs={{1,0},{2,1},{3,2},{4,3},{5,4},{6,5},{7,6},{8,7},{9,8},{10,9},{11,1... | collective-permute-start | bytes 3145736 | tf_op jit(solution)/shard_map/ppermute | solution.py:27
  253.6 26.8 %collective-permute-start.13 = (f32[512,512]{1,0:T(8,128)S(1)}, f32[512,512]{1,0:T(8,128)S(1)}, u32[]{:S(2)}, u32[]{:S(2)}) collective-permute-start(f32[512,512]{1,0:T(8,128)S(1)} %fusion.190), channel_id=1, source_target_pairs={{0,1},{1,2},{2,3},{3,4},{4,5},{5,6},{6,7},{7,8},{8,9},{9,10},{10,1... | collective-permute-start | bytes 3145736 | tf_op jit(solution)/shard_map/ppermute | solution.py:22
  258.3 22.1 %collective-permute-start.12 = (f32[512,512]{1,0:T(8,128)S(1)}, f32[512,512]{1,0:T(8,128)S(1)}, u32[]{:S(2)}, u32[]{:S(2)}) collective-permute-start(f32[512,512]{1,0:T(8,128)S(1)} %fusion.192), channel_id=1, source_target_pairs={{0,1},{1,2},{2,3},{3,4},{4,5},{5,6},{6,7},{7,8},{8,9},{9,10},{10,1... | collective-permute-start | bytes 3145736 | tf_op jit(solution)/shard_map/ppermute | solution.py:22
  261.5 21.1 %collective-permute-start.15 = (f32[512,512]{1,0:T(8,128)S(1)}, f32[512,512]{1,0:T(8,128)}, u32[]{:S(2)}, u32[]{:S(2)}) collective-permute-start(f32[512,512]{1,0:T(8,128)S(1)} %fusion.210), channel_id=1, source_target_pairs={{1,0},{2,1},{3,2},{4,3},{5,4},{6,5},{7,6},{8,7},{9,8},{10,9},{11,1... | collective-permute-start | bytes 3145736 | tf_op jit(solution)/shard_map/ppermute | solution.py:27
  311.2 29.3 %all-to-all-start.2 = ((f32[128,8,128]{2,1,0:T(8,128)}), f32[128,8,128]{2,1,0:T(8,128)S(1)}, u32[]{:S(2)}, u32[]{:S(2)}) async-start(f32[128,8,128]{2,1,0:T(8,128)} %broadcast_in_dim.34), calls=%async_computation.2 | async-start | bytes 1048576 | tf_op jit(solution)/shard_map/all_to_all | solution.py:45
  480.6 30.2 %collective-permute-start.21 = (f32[512,512]{1,0:T(8,128)}, f32[512,512]{1,0:T(8,128)}, u32[]{:S(2)}, u32[]{:S(2)}) collective-permute-start(f32[512,512]{1,0:T(8,128)} %fusion.185), channel_id=1, source_target_pairs={{0,1},{1,2},{2,3},{3,4},{4,5},{5,6},{6,7},{7,8},{8,9},{9,10},{10,1... | collective-permute-start | bytes 3145736 | tf_op jit(solution)/shard_map/ppermute | solution.py:22
  487.1 23.7 %collective-permute-start.20 = (f32[512,512]{1,0:T(8,128)}, f32[512,512]{1,0:T(8,128)S(1)}, u32[]{:S(2)}, u32[]{:S(2)}) collective-permute-start(f32[512,512]{1,0:T(8,128)} %fusion.205), channel_id=1, source_target_pairs={{1,0},{2,1},{3,2},{4,3},{5,4},{6,5},{7,6},{8,7},{9,8},{10,9},{11,1... | collective-permute-start | bytes 3145736 | tf_op jit(solution)/shard_map/ppermute | solution.py:27
  493.1 17.6 %all-to-all-start.3 = ((f32[32,8,128]{2,1,0:T(8,128)}), f32[32,8,128]{2,1,0:T(8,128)S(1)}, u32[]{:S(2)}, u32[]{:S(2)}) async-start(f32[32,8,128]{2,1,0:T(8,128)} %broadcast_in_dim.69), calls=%async_computation.3 | async-start | bytes 262144 | tf_op jit(solution)/shard_map/all_to_all | solution.py:45
  560.8 26.0 %all-to-all-start.4 = ((f32[128,8,128]{2,1,0:T(8,128)}), f32[128,8,128]{2,1,0:T(8,128)}, u32[]{:S(2)}, u32[]{:S(2)}) async-start(f32[128,8,128]{2,1,0:T(8,128)} %broadcast_in_dim.70), calls=%async_computation.4 | async-start | bytes 1048576 | tf_op jit(solution)/shard_map/all_to_all | solution.py:45
  (84 other events, 1291.3 us)
Sparse Core Ops, SparseCore 0:
  10.2 48.5 all-gather.4
  60.5 60.2 all-gather.6

commit v4 on v3

v4 whole, which is shorter than its diff:
```python
import functools
import math

import jax
import jax.numpy as jnp
from jax import lax
from jax.experimental import pallas as pl
from jax.experimental.pallas import tpu as pltpu
from jax.sharding import PartitionSpec as P

KRYLOV = 4
HIGHEST = lax.Precision.HIGHEST
ROOT_TWO = math.sqrt(2.0)
ANISOTROPY = 0.5
TIME_STEP = 0.1
VMEM_LIMIT = 48 * 1024 * 1024


def to_next(block):
    count = lax.axis_size("sec")
    return lax.ppermute(block, "sec", [(i, i + 1) for i in range(count - 1)])


def to_previous(block):
    count = lax.axis_size("sec")
    return lax.ppermute(block, "sec", [(i + 1, i) for i in range(count - 1)])


def gather_col(block, axis):
    return lax.all_gather(block, "col", axis=axis, tiled=True)


def params():
    return pltpu.CompilerParams(vmem_limit_bytes=VMEM_LIMIT)


def exchange(rows, axis):
    count = lax.axis_size(axis) if isinstance(axis, str) else lax.axis_size(axis[0]) * lax.axis_size(axis[1])
    sent = jnp.broadcast_to(rows[None], (count,) + rows.shape)
    return lax.all_to_all(sent, axis, 0, 0)


def row_of(values, shape):
    lane = lax.broadcasted_iota(jnp.int32, shape, 1)
    row = lax.broadcasted_iota(jnp.int32, shape, 0)
    out = jnp.zeros(shape, jnp.float32)
    for p, value in enumerate(values):
        out = jnp.where((lane == p) & (row == 0), value, out)
    return out


def add_parts(spins, part_refs, rows=slice(None)):
    local = part_refs[0]
    if spins == 1:
        return [local[0, rows, :] + part_refs[1][rows, :] + part_refs[2][rows, :]]
    down0, down1, up1, up2 = (ref[rows, :] for ref in part_refs[1:])
    return [local[0, rows, :] + up1, local[1, rows, :] + (up2 + down0), local[2, rows, :] + down1]


BF16 = jnp.bfloat16


def split(value):
    high = value.astype(BF16)
    return high, (value - high.astype(jnp.float32)).astype(BF16)


def product(left, right):
    def dot(a, b):
        return jnp.dot(a, b, preferred_element_type=jnp.float32)

    return dot(left[0], right[0]) + (dot(left[0], right[1]) + dot(left[1], right[0]))


SCALARS = jax.ShapeDtypeStruct((8, 128), jnp.float32)


def scalar_spec():
    return pl.BlockSpec((8, 128), lambda *i: (0, 0))


def norm_kernel(a_ref, out_ref):
    a = a_ref[...]
    out_ref[...] = row_of([jnp.sum(a * a)], out_ref.shape)


def norm_row(block):
    return pl.pallas_call(norm_kernel, out_shape=SCALARS, compiler_params=params())(block)


def inverse_norm_kernel(parts_ref, out_ref):
    total = jnp.sum(parts_ref[...], axis=0)
    out_ref[...] = jnp.broadcast_to(1.0 / jnp.sqrt(total[0:1, 0:1]), out_ref.shape)


def inverse_norm(parts):
    return pl.pallas_call(inverse_norm_kernel, out_shape=SCALARS, compiler_params=params())(parts)


def split_kernel(x_ref, high_ref, low_ref):
    high_ref[...], low_ref[...] = split(x_ref[...])


def split_state(x):
    rows, columns = x.shape
    step = 128
    spec = pl.BlockSpec((step, columns), lambda i: (i, 0))
    return pl.pallas_call(
        split_kernel,
        grid=(rows // step,),
        in_specs=[spec],
        out_specs=[spec] * 2,
        out_shape=[jax.ShapeDtypeStruct((rows, columns), BF16)] * 2,
        compiler_params=params(),
    )(x)


def right_kernel(block_ref, stack_ref, up_ref, down_ref):
    r0, r1, r2, r3, r4 = (block_ref[0, b] for b in range(5))
    for k, value in enumerate((r0, r4 + r1, r4, r4 - r1, r1)):
        stack_ref[k, 0], stack_ref[k, 1] = split(value)
    half = ROOT_TWO / 2
    up_ref[0], up_ref[1] = split(half * r2.T)
    down_ref[0], down_ref[1] = split(half * r3.T)


def right_parts(blocks):
    count, _, size, width = blocks.shape
    turned = pl.BlockSpec((2, width, size), lambda i: (0, i, 0))
    pair = jax.ShapeDtypeStruct((2, size, size), BF16)
    return pl.pallas_call(
        right_kernel,
        grid=(count,),
        in_specs=[pl.BlockSpec((1, 5, size, width), lambda i: (i, 0, 0, 0))],
        out_specs=[pl.BlockSpec((5, 2, size, width), lambda i: (0, 0, 0, i)), turned, turned],
        out_shape=[jax.ShapeDtypeStruct((5, 2, size, size), BF16), pair, pair],
        compiler_params=params(),
    )(blocks)


def left_kernel(flag_ref, left_ref, bsum_ref, bfour_ref, asum_ref, afour_ref, four_ref, mix_ref):
    has_above, has_below = flag_ref[0], flag_ref[1]
    for k, value in enumerate((bfour_ref[...], left_ref[4], afour_ref[...])):
        four_ref[k, 0], four_ref[k, 1] = split(value)
    raise_here = jnp.where(has_above > 0, ROOT_TWO * left_ref[2], 0.0)
    lower_here = jnp.where(has_below > 0, ROOT_TWO * left_ref[3], 0.0)
    mixes = (
        bsum_ref[...], lower_here, left_ref[0], lower_here.T, raise_here.T, asum_ref[...], raise_here
    )
    for k, value in enumerate(mixes):
        mix_ref[k, 0], mix_ref[k, 1] = split(value)


def left_parts(flags, left, below_sum, below_four, above_sum, above_four):
    size = left.shape[1]
    vmem = pl.BlockSpec(memory_space=pltpu.VMEM)
    return pl.pallas_call(
        left_kernel,
        in_specs=[pl.BlockSpec(memory_space=pltpu.SMEM)] + [vmem] * 5,
        out_specs=[vmem] * 2,
        out_shape=[
            jax.ShapeDtypeStruct((3, 2, size, size), BF16),
            jax.ShapeDtypeStruct((7, 2, size, size), BF16),
        ],
        compiler_params=params(),
    )(flags, left, below_sum, below_four, above_sum, above_four)


def bond_kernel(p_ref, out_ref):
    a = pl.program_id(0)
    scale = jnp.where((a == 2) | (a == 3), ROOT_TWO, 1.0).astype(jnp.float32)
    out_ref[0, 0], out_ref[0, 1] = split(scale * p_ref[0])


def bond_parts(bond):
    count, size, _ = bond.shape
    return pl.pallas_call(
        bond_kernel,
        grid=(count,),
        in_specs=[pl.BlockSpec((1, size, size), lambda i: (i, 0, 0))],
        out_specs=pl.BlockSpec((1, 2, size, size), lambda i: (i, 0, 0, 0)),
        out_shape=jax.ShapeDtypeStruct((count, 2, size, size), BF16),
        compiler_params=params(),
    )(bond)


def pair_of(ref, index):
    return ref[index, 0], ref[index, 1]


def columns_of(high_ref, low_ref, s):
    size = high_ref.shape[0]
    cut = slice(s * size, (s + 1) * size)
    return high_ref[:, cut], low_ref[:, cut]


def site_send_kernel(place_ref, high, low, four_ref, up_ref, down_ref, d0, d1, u1, u2, zh, zl):
    up, down = (up_ref[0], up_ref[1]), (down_ref[0], down_ref[1])
    z = []
    for s in (1, 0, 2):
        pair = split(product(columns_of(high, low, s), pair_of(four_ref, s)))
        zh[s], zl[s] = pair
        if s < 2:
            (d0, d1)[s][...] = product(down, pair)
        if s > 0:
            (u1, u2)[s - 1][...] = product(up, pair)


def site_local_kernel(place_ref, high, low, mix_ref, stack_ref, zh, zl, out_ref):
    x = [columns_of(high, low, s) for s in range(3)]
    terms = (((0, 0), (1, 1)), ((1, 2), (0, 3), (2, 4)), ((2, 5), (1, 6)))
    for s in range(3):
        total = None
        for source, matrix in terms[s]:
            value = product(x[source], pair_of(mix_ref, matrix))
            total = value if total is None else total + value
        y = product(pair_of(stack_ref, 0), split(total))
        out_ref[s] = y + product(pair_of(stack_ref, 1 + s), (zh[s], zl[s]))


def bond_send_kernel(place_ref, high, low, p_ref, up_ref, down_ref, d_ref, u_ref):
    x = (high[...], low[...])
    d_ref[...] = product((down_ref[0], down_ref[1]), split(product(x, pair_of(p_ref, 3))))
    u_ref[...] = product((up_ref[0], up_ref[1]), split(product(x, pair_of(p_ref, 2))))


def bond_local_kernel(place_ref, high, low, p_ref, stack_ref, out_ref):
    x = (high[...], low[...])
    total = None
    for a, matrix in ((0, 0), (4, 2), (1, 4)):
        value = product(pair_of(stack_ref, matrix), split(product(x, pair_of(p_ref, a))))
        total = value if total is None else total + value
    out_ref[0] = total


def product_call(kernel, place, whole, cut, outs, quarter, flops):
    size = cut[0].shape[-1]
    width = size // 4 if quarter else size // 2

    def by_place(array):
        lead = (0,) * (array.ndim - 1)
        block = array.shape[:-1] + (width,)
        if quarter and array.shape[-1] == width:
            return pl.BlockSpec(block, lambda i, p: lead + (0,))
        if quarter:
            return pl.BlockSpec(block, lambda i, p: lead + (p[0],))
        return pl.BlockSpec(block, lambda i, p: lead + (i,))

    def all_of(array):
        lead = (0,) * array.ndim
        return pl.BlockSpec(array.shape, lambda i, p: lead)

    shapes = [
        jax.ShapeDtypeStruct(shape + (size, width if quarter else size), dtype) for shape, dtype in outs
    ]
    return pl.pallas_call(
        kernel,
        grid_spec=pltpu.PrefetchScalarGridSpec(
            num_scalar_prefetch=1,
            grid=(1 if quarter else size // width,),
            in_specs=[all_of(a) if is_whole else by_place(a) for is_whole, a in whole],
            out_specs=[by_place(shape) for shape in shapes],
        ),
        out_shape=shapes,
        compiler_params=params(),
        cost_estimate=pl.CostEstimate(
            flops=flops // (4 if quarter else 1), bytes_accessed=16 * 2**20, transcendentals=0
        ),
    )(place, *[a for _, a in whole])


UNIT = 6 * 512**3


def state_spec(spins, step, size):
    return pl.BlockSpec((step, spins * size), lambda i: (i, 0))


def part_specs(spins, step, size, count):
    row = pl.BlockSpec((step, size), lambda i: (i, 0))
    return [pl.BlockSpec((spins, step, size), lambda i: (0, i, 0))] + [row] * (count - 1)


def state_shapes(spins, size):
    full = (size, spins * size)
    return [jax.ShapeDtypeStruct(full, t) for t in (jnp.float32, BF16, BF16)]


def first_combine_kernel(spins, scale_ref, x_ref, *refs):
    part_refs, (y_ref, high_ref, low_ref, sums_ref) = refs[:-4], refs[-4:]
    nu = scale_ref[2:3, 0:1]
    size = part_refs[0].shape[2]
    cross = jnp.float32(0.0)
    square = jnp.float32(0.0)
    for s, total in enumerate(add_parts(spins, part_refs)):
        cut = slice(s * size, (s + 1) * size)
        y = total * nu
        y_ref[:, cut] = y
        high_ref[:, cut], low_ref[:, cut] = split(y)
        cross += jnp.sum(x_ref[:, cut] * nu * y)
        square += jnp.sum(y * y)

    @pl.when(pl.program_id(0) == 0)
    def _():
        sums_ref[...] = jnp.zeros_like(sums_ref)

    sums_ref[...] += row_of([cross, square], sums_ref.shape)


def first_combine(x, nu, parts, spins):
    size = x.shape[0]
    step = 128
    state = state_spec(spins, step, size)
    *y, sums = pl.pallas_call(
        functools.partial(first_combine_kernel, spins),
        grid=(size // step,),
        in_specs=[scalar_spec(), state] + part_specs(spins, step, size, len(parts)),
        out_specs=[state] * 3 + [scalar_spec()],
        out_shape=state_shapes(spins, size) + [SCALARS],
        compiler_params=params(),
    )(nu, x, *parts)
    return y, sums


def shift_kernel(nu_ref, parts_ref, out_ref):
    total = jnp.sum(parts_ref[...], axis=0)
    row = lax.broadcasted_iota(jnp.int32, out_ref.shape, 0)
    sigma = total[0:1, 0:1]
    tau = 1.0 / jnp.sqrt(total[0:1, 1:2])
    out_ref[...] = jnp.where(row == 0, sigma, jnp.where(row == 1, tau, nu_ref[...]))


def shift_rows(nu, parts):
    return pl.pallas_call(shift_kernel, out_shape=SCALARS, compiler_params=params())(nu, parts)


def combine_kernel(second, spins, scale_ref, w_ref, *refs):
    sigma, tau, nu = scale_ref[0:1, 0:1], scale_ref[1:2, 0:1], scale_ref[2:3, 0:1]
    if second:
        x_ref, refs = refs[0], refs[1:]
    part_refs, (out_ref, high_ref, low_ref) = refs[:-3], refs[-3:]
    size = part_refs[0].shape[2]
    for s, total in enumerate(add_parts(spins, part_refs)):
        cut = slice(s * size, (s + 1) * size)
        w = w_ref[:, cut]
        if second:
            inner = w - sigma * (nu * x_ref[:, cut])
            value = tau * tau * ((total - sigma * w) - sigma * inner)
        else:
            value = tau * (total - sigma * w)
        out_ref[:, cut] = value
        high_ref[:, cut], low_ref[:, cut] = split(value)


def combine(scales, w, x, parts, spins):
    size = w.shape[0]
    step = 128
    state = state_spec(spins, step, size)
    second = x is not None
    return pl.pallas_call(
        functools.partial(combine_kernel, second, spins),
        grid=(size // step,),
        in_specs=[scalar_spec()]
        + [state] * (2 if second else 1)
        + part_specs(spins, step, size, len(parts)),
        out_specs=[state] * 3,
        out_shape=state_shapes(spins, size),
        compiler_params=params(),
    )(scales, w, *([x] if second else []), *parts)


PAIRS = [(i, j) for j in range(5) for i in range(j + 1) if (i, j) != (4, 4)]


def gram_kernel(spins, place_ref, scale_ref, *refs):
    bases = [refs[k * spins : (k + 1) * spins] for k in range(4)]
    part_refs, out_ref = refs[4 * spins : -1], refs[-1]
    sigma, tau, nu = scale_ref[0:1, 0:1], scale_ref[1:2, 0:1], scale_ref[2:3, 0:1]
    sums = [jnp.zeros((8, 128), jnp.float32)] * len(PAIRS)
    chunk = 64
    size = part_refs[0].shape[1]
    for start in range(0, size, chunk):
        rows = slice(start, start + chunk)
        for s, total in enumerate(add_parts(spins, part_refs, rows)):
            x, y, w2, w3 = (bases[k][s][rows, :] for k in range(4))
            w = [nu * x, None, w2, w3, None]
            w[1] = tau * (y - sigma * w[0])
            w[4] = tau * (total - sigma * w[3])
            for p, (i, j) in enumerate(PAIRS):
                terms = (w[i] * w[j]).reshape(chunk // 8, 8, 128)
                sums[p] = sums[p] + jnp.sum(terms, axis=0)
    out_ref[...] = row_of([jnp.sum(value) for value in sums], out_ref.shape)


def gram_row(place, scales, states, parts, spins):
    size = states[0].shape[0]
    width = parts[0].shape[-1]
    per = size // width
    quarter = [
        pl.BlockSpec((size, width), functools.partial(lambda s, i, p: (0, s * per + p[0]), s))
        for s in range(spins)
    ]
    whole = [pl.BlockSpec((spins, size, width), lambda i, p: (0, 0, 0))]
    whole += [pl.BlockSpec((size, width), lambda i, p: (0, 0))] * (len(parts) - 1)
    flat = [state for state in states for s in range(spins)]
    return pl.pallas_call(
        functools.partial(gram_kernel, spins),
        grid_spec=pltpu.PrefetchScalarGridSpec(
            num_scalar_prefetch=1,
            grid=(1,),
            in_specs=[scalar_spec()] + quarter * 4 + whole,
            out_specs=scalar_spec(),
        ),
        out_shape=SCALARS,
        compiler_params=params(),
    )(place, scales, *flat, *parts)


def weights_kernel(step_size, scale_ref, sums_ref, out_ref):
    sigma, tau, nu = scale_ref[0:1], scale_ref[1:2], scale_ref[2:3]
    total = jnp.sum(sums_ref[...], axis=0)[0:1]
    gram = {}
    for p, (i, j) in enumerate(PAIRS):
        gram[(i, j)] = jnp.broadcast_to(total[:, p : p + 1], (1, 128))
    low = {}
    inverse = []
    for j in range(4):
        pivot = gram[(j, j)]
        for k in range(j):
            pivot = pivot - low[(j, k)] * low[(j, k)]
        low[(j, j)] = jnp.sqrt(pivot)
        inverse.append(1.0 / low[(j, j)])
        for i in range(j + 1, 5):
            value = gram[(j, i)]
            for k in range(j):
                value = value - low[(i, k)] * low[(j, k)]
            low[(i, j)] = value * inverse[j]
    stretch = 1.0 / tau
    beta = [low[(j + 1, j + 1)] * inverse[j] * stretch for j in range(3)]
    alpha = []
    for j in range(4):
        value = low[(j + 1, j)] * stretch
        if j > 0:
            value = value - low[(j, j - 1)] * beta[j - 1]
        alpha.append(sigma + value * inverse[j])
    factor = step_size / 16.0
    diag = [factor * a for a in alpha]
    off = [factor * b for b in beta]
    one = jnp.ones_like(sigma)
    zero = jnp.zeros_like(sigma)
    result = {(i, j): one if i == j else zero for i in range(4) for j in range(i, 4)}

    def entry(table, i, j):
        return table[(min(i, j), max(i, j))]

    for degree in range(8, 0, -1):
        fresh = {}
        for i in range(4):
            for j in range(i, 4):
                value = diag[i] * entry(result, i, j)
                if i > 0:
                    value = value + off[i - 1] * entry(result, i - 1, j)
                if i < 3:
                    value = value + off[i] * entry(result, i + 1, j)
                value = value * (1.0 / degree)
                fresh[(i, j)] = one + value if i == j else value
        result = fresh
    for squaring in range(4):
        fresh = {}
        for i in range(4):
            for j in range(i, 4):
                if squaring == 3 and i > 0:
                    continue
                value = entry(result, i, 0) * entry(result, 0, j)
                for k in range(1, 4):
                    value = value + entry(result, i, k) * entry(result, k, j)
                fresh[(i, j)] = value
        result = fresh
    column = [result[(0, j)] for j in range(4)]
    size = jnp.sqrt(sum(c * c for c in column))
    c = [None] * 4
    for i in range(3, -1, -1):
        value = column[i]
        for j in range(i + 1, 4):
            value = value - low[(j, i)] * c[j]
        c[i] = value * inverse[i]
    norm = low[(0, 0)] / nu
    c = [norm * v for v in c]
    rows = [(c[0] - c[1] * tau * sigma) * nu, c[1] * tau, c[2], c[3], 1.0 / (norm * size)]
    for p, value in enumerate(rows):
        out_ref[p : p + 1, :] = value
    for p in range(len(rows), 8):
        out_ref[p : p + 1, :] = zero


def basis_weights(scales, sums, step_size):
    return pl.pallas_call(
        functools.partial(weights_kernel, step_size),
        out_shape=SCALARS,
        compiler_params=params(),
    )(scales, sums)


def result_kernel(place_ref, weight_ref, *refs):
    value = weight_ref[0:1, 0:1] * refs[0][...]
    for k in range(1, 4):
        value = value + weight_ref[k : k + 1, 0:1] * refs[k][...]
    refs[4][...] = value


def weighted(place, weights, states, rows):
    size, columns = states[0].shape
    step = 128 if rows is None else rows
    if rows is None:
        spec = pl.BlockSpec((step, columns), lambda i, p: (i, 0))
    else:
        spec = pl.BlockSpec((step, columns), lambda i, p: (p[0], 0))
    return pl.pallas_call(
        result_kernel,
        grid_spec=pltpu.PrefetchScalarGridSpec(
            num_scalar_prefetch=1,
            grid=(size // step if rows is None else 1,),
            in_specs=[scalar_spec()] + [spec] * 4,
            out_specs=pl.BlockSpec((step, columns), lambda i, p: (i, 0)),
        ),
        out_shape=jax.ShapeDtypeStruct((size if rows is None else rows, columns), jnp.float32),
        compiler_params=params(),
    )(place, weights, *states)


def evolve(place, x, nu, apply_op, step_size, spins):
    parts, _ = apply_op(split_state(x), None, False)
    (y, *y_split), sums = first_combine(x, nu, parts, spins)
    parts, totals = apply_op(y_split, sums, False)
    scales = shift_rows(nu, totals)
    w2, *w2_split = combine(scales, y, x, parts, spins)
    parts, _ = apply_op(w2_split, None, False)
    w3, *w3_split = combine(scales, w2, None, parts, spins)
    parts, _ = apply_op(w3_split, None, True)
    states = [x, y, w2, w3]
    row = gram_row(place, scales, states, parts, spins)
    weights = basis_weights(scales, exchange(row, ("col", "sec")), step_size)
    return states, weights


def body(site_tensor, left_env, right_env, bond_env, sector_sizes):
    col_rows = site_tensor.shape[0]
    size = left_env.shape[2]
    sector = lax.axis_index("sec")
    last = lax.axis_size("sec") - 1
    place = lax.axis_index("col").reshape(1).astype(jnp.int32)

    left = left_env[0]
    site_block = site_tensor[:, 0]
    site_full = gather_col(site_block, 0)
    right_blocks = gather_col(right_env, 0)
    site_nu = inverse_norm(exchange(norm_row(site_block), ("col", "sec")))

    below_four = to_next(left[4])
    above_four = to_previous(left[4])
    below_sum = to_next(left[0] + left[1] + ANISOTROPY * left[4])
    above_sum = to_previous(left[0] - left[1] + ANISOTROPY * left[4])
    flags = jnp.stack([sector < last, sector > 0]).astype(jnp.int32)
    four, mix = left_parts(flags, left, below_sum, below_four, above_sum, above_four)
    stack, up, down = right_parts(right_blocks)
    bond = bond_parts(bond_env[0])

    def send_sums(sums, after):
        if sums is None:
            return None
        sums, _ = lax.optimization_barrier((sums, after))
        return exchange(sums, "sec")

    def apply_site(pair, sums, quarter):
        plain = ((), jnp.float32)
        d0, d1, u1, u2, zh, zl = product_call(
            site_send_kernel,
            place,
            [(True, pair[0]), (True, pair[1]), (False, four), (True, up), (True, down)],
            [four],
            [plain] * 4 + [((3,), BF16)] * 2,
            quarter,
            7 * UNIT,
        )
        d1, u1 = to_previous(d1), to_next(u1)
        d0, u2 = to_previous(d0), to_next(u2)
        totals = send_sums(sums, zh)
        (local,) = product_call(
            site_local_kernel,
            place,
            [(True, pair[0]), (True, pair[1]), (False, mix), (True, stack), (False, zh), (False, zl)],
            [mix],
            [((3,), jnp.float32)],
            quarter,
            13 * UNIT,
        )
        return [local, d0, d1, u1, u2], totals

    states, weights = evolve(place, site_full, site_nu, apply_site, -TIME_STEP, 3)
    evolved = weighted(place, weights, states, None)
    out_site = weighted(place, weights, states, col_rows)[:, None, :]
    gram = lax.dot_general(evolved, evolved, (((1,), (1,)), ((), ())), precision=HIGHEST)
    live = (jnp.arange(size) < sector_sizes[0]).astype(jnp.float32)
    gram = gram + (1.0 - live)[:, None] * jnp.eye(size, dtype=jnp.float32)
    factor = jnp.linalg.cholesky(gram[None])[0]
    bond_scale = math.sqrt(3.0 * size)
    start = factor * live[:, None] * live[None, :] / bond_scale
    bond_nu = jnp.broadcast_to(weights[4:5] * bond_scale, (8, 128))

    def apply_bond(pair, sums, quarter):
        plain = ((), jnp.float32)
        down_term, up_term = product_call(
            bond_send_kernel,
            place,
            [(True, pair[0]), (True, pair[1]), (False, bond), (True, up), (True, down)],
            [bond],
            [plain] * 2,
            quarter,
            4 * UNIT,
        )
        totals = send_sums(sums, up_term)
        down_term, up_term = to_previous(down_term), to_next(up_term)
        (local,) = product_call(
            bond_local_kernel,
            place,
            [(True, pair[0]), (True, pair[1]), (False, bond), (True, stack)],
            [bond],
            [((1,), jnp.float32)],
            quarter,
            6 * UNIT,
        )
        return [local, down_term, up_term], totals

    states, weights = evolve(place, start, bond_nu, apply_bond, TIME_STEP, 1)
    out_bond = weighted(place, weights, states, col_rows)[:, None, :]
    return (out_site, out_bond)


def solution(mesh):
    in_specs = (
        P("col", "sec", None),
        P("sec", None, None, None),
        P("sec", None, None, "col"),
        P("sec", None, None, None),
        P("sec"),
    )
    out_specs = (P("col", "sec", None), P("col", "sec", None))
    return jax.shard_map(body, mesh=mesh, in_specs=in_specs, out_specs=out_specs, check_vma=False)
```

time: 606 us -> 632 us (1.043)
  Pallas kernels: 33.3 us -> 252 us
  matrix products: 201 us -> 12.4 us
  waiting for transfers between devices: 66.9 us -> 84.6 us
  local copies, waits for them, and re-layouts: 53 us -> 41.4 us
  other arithmetic: 93.7 us -> 86 us
    pallas_call x11 -> x32, Pallas kernels: 30.7 us -> 249 us  [the longest x16 186 us: product_call(): pl.pallas_call(kernel, grid_spec=pltpu.PrefetchScalarGridSpec(num_scalar_...]
    dot_general x108 -> x1, matrix products: 199 us -> 5.23 us  [body(): lax.dot_general(evolved, evolved, (((1,), (1,)), ((), ())), precision=HIG...]
    all_gather x2, waiting for transfers between devices: 24.1 us -> 50.6 us  [gather_col(): return lax.all_gather(block, 'col', axis=axis, tiled=True)]
    dynamic_slice x10 -> x0, local copies, waits for them, and re-layouts: 11.3 us -> none  [quarter_of(): lax.dynamic_slice_in_dim(m, col * col_rows, col_rows, 1)]
    ppermute x13 -> x14, waiting for transfers between devices: 21.8 us -> 10.5 us  [to_previous(): return lax.ppermute(block, 'sec', [(i + 1, i) for i in range(count - 1)])]
    ppermute x13 -> x14, starting transfers between devices: 28.7 us -> 31.8 us  [to_previous(): return lax.ppermute(block, 'sec', [(i + 1, i) for i in range(count - 1)])]
    unnamed x160 -> x91, local copies, waits for them, and re-layouts: 35.5 us -> 33.8 us
    another operation x15 -> x14, other arithmetic: 79.6 us -> 80.6 us  [body(): factor = jnp.linalg.cholesky(gram[None])[0]]
  transfers between devices with their start and end apart: 33 -> 35, of which waited for: 12 -> 9; matrix products, arithmetic and copies ran while one was open for 28% -> 2% of each run, Pallas kernels for 0% -> 25%
where the time goes in v4:
time: 632 us; the launch traced here: 624 us
  Pallas kernels  252 us (40%)
  starting transfers between devices  129 us (20%)
  other arithmetic  86 us (14%)
  waiting for transfers between devices  84.6 us (13%)
  local copies, waits for them, and re-layouts  41.4 us (7%)
  between operations  18.5 us (3%)
  matrix products  12.4 us (2%)
    pallas_call x16, Pallas kernels, product_call(): pl.pallas_call(kernel, grid_spec=pltpu.PrefetchScalarGridSpec(num_scalar_...  186 us
    another operation x14, other arithmetic, body(): factor = jnp.linalg.cholesky(gram[None])[0]  80.6 us
    all_to_all x5, starting transfers between devices, exchange(): return lax.all_to_all(sent, axis, 0, 0)  51.9 us
    all_gather x2, waiting for transfers between devices, gather_col(): return lax.all_gather(block, 'col', axis=axis, tiled=True)  50.6 us
    ppermute x14, starting transfers between devices, to_next(): return lax.ppermute(block, 'sec', [(i, i + 1) for i in range(count - 1)])  45.4 us
    unnamed x91, local copies, waits for them, and re-layouts  33.8 us
    ppermute x14, starting transfers between devices, to_previous(): return lax.ppermute(block, 'sec', [(i + 1, i) for i in range(count - 1)])  31.8 us
    pallas_call x4, Pallas kernels, combine(): pl.pallas_call(functools.partial(combine_kernel, second, spins), grid=(si...  18.9 us
  transfers between devices with their start and end apart: 35, of which 9 were waited for; matrix products, arithmetic and copies ran while one was open for 2% of the time, Pallas kernels for 25%

profile of v4, /device:TPU:1, one launch (start us, length us, event | category | flops | bytes accessed | tf_op | source)
XLA Modules:
  0.0 624.0 jit_solution(12759098744927237841)
XLA Ops:
  28.9 9.8 %all-to-all-start = ((f32[128,8,128]{2,1,0:T(8,128)}), f32[128,8,128]{2,1,0:T(8,128)S(1)}, u32[]{:S(2)}, u32[]{:S(2)}) async-start(f32[128,8,128]{2,1,0:T(8,128)} %broadcast_in_dim.24), calls=%async_computation | async-start | bytes 1048576 | tf_op jit(solution)/shard_map/all_to_all | solution.py:40
  43.2 10.0 %collective-permute-done.3.afour_ref = f32[512,512]{1,0:T(8,128)} collective-permute-done((f32[512,512]{1,0:T(8,128)}, f32[512,512]{1,0:T(8,128)}, u32[]{:S(2)}, u32[]{:S(2)}) %collective-permute-start.3) | collective-permute-done | bytes 1048608 | tf_op jit(solution)/shard_map/ppermute | solution.py:26
  67.1 50.6 %all-gather.4.cloned.1.call-done.block_ref = f32[4,5,512,128]{3,2,1,0:T(8,128)} async-done(((f32[1,5,512,128]{3,2,1,0:T(8,128)}), f32[4,5,512,128]{3,2,1,0:T(8,128)}) %all-gather.4.cloned.1.call-update) | async-done | bytes 5242896 | tf_op jit(solution)/shard_map/all_gather | solution.py:30
  124.7 12.0 %shard_map.73 = (f32[512,512]{1,0:T(8,128)}, f32[512,512]{1,0:T(8,128)}, f32[512,512]{1,0:T(8,128)}, f32[512,512]{1,0:T(8,128)}, bf16[3,512,512]{2,1,0:T(8,128)(2,1)}, /*index=5*/bf16[3,512,512]{2,1,0:T(8,128)(2,1)}) custom-call(s32[1]{0:T(128)} %bitcast.place_ref, bf16[512,1536]{1,0:T(8,128)(2,1)} %copy-done.24, bf16[512,1536]{1,0:T(8,128)(2,1)} %copy-done.26, ...), custom_call_target="tpu_custom_call" | custom-call | flops 5637144576 | bytes 16777216 | tf_op jit(solution)/shard_map/pallas_call | solution.py:256
  151.8 22.6 %shard_map.74.refs_0_ = f32[3,512,512]{2,1,0:T(8,128)} custom-call(s32[1]{0:T(128)} %bitcast.place_ref, bf16[512,1536]{1,0:T(8,128)(2,1)S(1)} %copy-done.25, bf16[512,1536]{1,0:T(8,128)(2,1)S(1)} %copy-done.27, bf16[7,2,512,512]{3,2,1,0:T(8,128)(2,1)} %get-tuple-element.67.mix_ref, bf16[5,2,512,512]{3,2,1,0:T(8,128)(2,1)} %get-tuple-element.68.stack_ref, ...), custom_call_target="tpu_custom_call" | custom-call | flops 10468982784 | bytes 16777216 | tf_op jit(solution)/shard_map/pallas_call | solution.py:256
  182.7 11.6 %shard_map.76 = (f32[512,512]{1,0:T(8,128)}, f32[512,512]{1,0:T(8,128)}, f32[512,512]{1,0:T(8,128)}, f32[512,512]{1,0:T(8,128)}, bf16[3,512,512]{2,1,0:T(8,128)(2,1)}, /*index=5*/bf16[3,512,512]{2,1,0:T(8,128)(2,1)}) custom-call(s32[1]{0:T(128)} %bitcast.place_ref, bf16[512,1536]{1,0:T(8,128)(2,1)} %copy-done.28, bf16[512,1536]{1,0:T(8,128)(2,1)} %get-tuple-element.80.low, ...), custom_call_target="tpu_custom_call" | custom-call | flops 5637144576 | bytes 16777216 | tf_op jit(solution)/shard_map/pallas_call | solution.py:256
  205.9 10.6 %all-to-all-start.1 = ((f32[32,8,128]{2,1,0:T(8,128)}), f32[32,8,128]{2,1,0:T(8,128)S(1)}, u32[]{:S(2)}, u32[]{:S(2)}) async-start(f32[32,8,128]{2,1,0:T(8,128)} %broadcast_in_dim.25), calls=%async_computation.1 | async-start | bytes 262144 | tf_op jit(solution)/shard_map/all_to_all | solution.py:40
  220.7 22.7 %shard_map.78.refs_1_ = f32[3,512,512]{2,1,0:T(8,128)} custom-call(s32[1]{0:T(128)} %bitcast.place_ref, bf16[512,1536]{1,0:T(8,128)(2,1)S(1)} %copy-done.29, bf16[512,1536]{1,0:T(8,128)(2,1)S(1)} %copy-done.30, bf16[7,2,512,512]{3,2,1,0:T(8,128)(2,1)} %get-tuple-element.67.mix_ref, bf16[5,2,512,512]{3,2,1,0:T(8,128)(2,1)} %get-tuple-element.68.stack_ref, ...), custom_call_target="tpu_custom_call" | custom-call | flops 10468982784 | bytes 16777216 | tf_op jit(solution)/shard_map/pallas_call | solution.py:256
  252.3 12.2 %shard_map.80 = (f32[512,512]{1,0:T(8,128)S(1)}, f32[512,512]{1,0:T(8,128)S(1)}, f32[512,512]{1,0:T(8,128)S(1)}, f32[512,512]{1,0:T(8,128)S(1)}, bf16[3,512,512]...) custom-call(s32[1]{0:T(128)} %bitcast.place_ref, bf16[512,1536]{1,0:T(8,128)(2,1)} %copy-done.31, ...), custom_call_target="tpu_custom_call" | custom-call | flops 5637144576 | bytes 16777216 | tf_op jit(solution)/shard_map/pallas_call | solution.py:256
  276.1 22.6 %shard_map.81.refs_0_ = f32[3,512,512]{2,1,0:T(8,128)} custom-call(s32[1]{0:T(128)} %bitcast.place_ref, bf16[512,1536]{1,0:T(8,128)(2,1)S(1)} %copy-done.32, bf16[512,1536]{1,0:T(8,128)(2,1)S(1)} %copy-done.33, bf16[7,2,512,512]{3,2,1,0:T(8,128)(2,1)} %get-tuple-element.67.mix_ref, bf16[5,2,512,512]{3,2,1,0:T(8,128)(2,1)} %get-tuple-element.68.stack_ref, ...), custom_call_target="tpu_custom_call" | custom-call | flops 10468982784 | bytes 16777216 | tf_op jit(solution)/shard_map/pallas_call | solution.py:256
  320.6 12.0 %shard_map.84.refs_12_ = f32[3,512,128]{2,1,0:T(8,128)S(1)} custom-call(s32[1]{0:T(128)} %bitcast.place_ref, bf16[512,1536]{1,0:T(8,128)(2,1)S(1)} %get-tuple-element.99.high, bf16[512,1536]{1,0:T(8,128)(2,1)S(1)} %copy-done.12, bf16[7,2,512,512]{3,2,1,0:T(8,128)(2,1)} %get-tuple-element.67.mix_ref, bf16[5,2,512,512]{3,2,1,0:T(8,128)(2,1)} %get-tuple-element.68.stack_ref, ...), custom_call_target="tpu_custom_call" | custom-call | flops 2617245696 | bytes 16777216 | tf_op jit(solution)/shard_map/pallas_call | solution.py:256
  336.4 12.4 %all-to-all-start.2 = ((f32[128,8,128]{2,1,0:T(8,128)}), f32[128,8,128]{2,1,0:T(8,128)S(1)}, u32[]{:S(2)}, u32[]{:S(2)}) async-start(f32[128,8,128]{2,1,0:T(8,128)} %broadcast_in_dim.26), calls=%async_computation.2 | async-start | bytes 1048576 | tf_op jit(solution)/shard_map/all_to_all | solution.py:40
  375.0 11.7 %custom-call.31 = f32[1,128,128]{2,1,0:T(8,128)S(1)} custom-call(f32[1,128,128]{2,1,0:T(8,128)S(1)} %cholesky.267), custom_call_target="Cholesky" | custom-call | tf_op jit(solution)/shard_map/jit(cholesky)/cholesky | solution.py:605
  387.8 9.8 %custom-call.32 = f32[1,1,128,128]{2,3,1,0:T(8,128)S(1)} custom-call(f32[1,1,128,128]{3,2,1,0:T(8,128)S(1)} %get-tuple-element.145), custom_call_target="InvertDiagBlocksLowerTriangular" | custom-call | tf_op jit(solution)/shard_map/jit(cholesky)/cholesky | solution.py:605
  400.3 11.7 %custom-call.33 = f32[1,128,128]{2,1,0:T(8,128)S(1)} custom-call(f32[1,128,128]{2,1,0:T(8,128)S(1)} %cholesky.271), custom_call_target="Cholesky" | custom-call | tf_op jit(solution)/shard_map/jit(cholesky)/cholesky | solution.py:605
  412.6 9.8 %custom-call.34 = f32[1,1,128,128]{2,3,1,0:T(8,128)S(1)} custom-call(f32[1,1,128,128]{3,2,1,0:T(8,128)S(1)} %get-tuple-element.142), custom_call_target="InvertDiagBlocksLowerTriangular" | custom-call | tf_op jit(solution)/shard_map/jit(cholesky)/cholesky | solution.py:605
  424.8 11.7 %custom-call.35 = f32[1,128,128]{2,1,0:T(8,128)S(1)} custom-call(f32[1,128,128]{2,1,0:T(8,128)S(1)} %cholesky.276), custom_call_target="Cholesky" | custom-call | tf_op jit(solution)/shard_map/jit(cholesky)/cholesky | solution.py:605
  437.2 10.2 %custom-call.36 = f32[1,1,128,128]{2,3,1,0:T(8,128)S(1)} custom-call(f32[1,1,128,128]{3,2,1,0:T(8,128)S(1)} %get-tuple-element.139), custom_call_target="InvertDiagBlocksLowerTriangular" | custom-call | tf_op jit(solution)/shard_map/jit(cholesky)/cholesky | solution.py:605
  449.6 11.7 %custom-call.37 = f32[1,128,128]{2,1,0:T(8,128)S(1)} custom-call(f32[1,128,128]{2,1,0:T(8,128)S(1)} %fusion.4), custom_call_target="Cholesky" | custom-call | tf_op jit(solution)/shard_map/jit(cholesky)/cholesky | solution.py:605
  481.0 10.3 %shard_map.91.refs_0_ = f32[1,512,512]{2,1,0:T(8,128)S(1)} custom-call(s32[1]{0:T(128)} %bitcast.place_ref, bf16[512,512]{1,0:T(8,128)(2,1)S(1)} %get-tuple-element.107.high, bf16[512,512]{1,0:T(8,128)(2,1)S(1)} %get-tuple-element.108.low, bf16[5,2,512,512]{3,2,1,0:T(8,128)(2,1)} %copy-done.2, bf16[5,2,512,512]{3,2,1,0:T(8,128)(2,1)} %get-tuple-element.68.stack_ref), custom_call_target="tpu_custom_call" | custom-call | flops 4831838208 | bytes 16777216 | tf_op jit(solution)/shard_map/pallas_call | solution.py:256
  522.3 10.3 %shard_map.96.refs_1_ = f32[1,512,512]{2,1,0:T(8,128)S(1)} custom-call(s32[1]{0:T(128)} %bitcast.place_ref, bf16[512,512]{1,0:T(8,128)(2,1)S(1)} %copy-done.35, bf16[512,512]{1,0:T(8,128)(2,1)S(1)} %copy-done.37, bf16[5,2,512,512]{3,2,1,0:T(8,128)(2,1)} %copy-done.2, bf16[5,2,512,512]{3,2,1,0:T(8,128)(2,1)} %get-tuple-element.68.stack_ref), custom_call_target="tpu_custom_call" | custom-call | flops 4831838208 | bytes 16777216 | tf_op jit(solution)/shard_map/pallas_call | solution.py:256
  551.1 10.3 %shard_map.98.refs_0_ = f32[1,512,512]{2,1,0:T(8,128)S(1)} custom-call(s32[1]{0:T(128)} %bitcast.place_ref, bf16[512,512]{1,0:T(8,128)(2,1)S(1)} %get-tuple-element.119.high, bf16[512,512]{1,0:T(8,128)(2,1)S(1)} %get-tuple-element.120.low, bf16[5,2,512,512]{3,2,1,0:T(8,128)(2,1)} %copy-done.2, bf16[5,2,512,512]{3,2,1,0:T(8,128)(2,1)} %get-tuple-element.68.stack_ref), custom_call_target="tpu_custom_call" | custom-call | flops 4831838208 | bytes 16777216 | tf_op jit(solution)/shard_map/pallas_call | solution.py:256
  585.0 11.1 %all-to-all-start.4 = ((f32[128,8,128]{2,1,0:T(8,128)}), f32[128,8,128]{2,1,0:T(8,128)}, u32[]{:S(2)}, u32[]{:S(2)}) async-start(f32[128,8,128]{2,1,0:T(8,128)} %broadcast_in_dim.32), calls=%async_computation.4 | async-start | bytes 1048576 | tf_op jit(solution)/shard_map/all_to_all | solution.py:40
  599.9 9.6 %all-to-all-done.4.sums_ref = f32[128,8,128]{2,1,0:T(8,128)} async-done(((f32[128,8,128]{2,1,0:T(8,128)}), f32[128,8,128]{2,1,0:T(8,128)}, u32[]{:S(2)}, u32[]{:S(2)}) %all-to-all-start.4) | async-done | bytes 524320 | tf_op jit(solution)/shard_map/all_to_all | solution.py:40
  (217 shorter events, 268.1 us)
Async XLA Ops:
  7.2 54.8 %all-gather.6.cloned.1.call-start = ((), (), s32[]{:S(2)}) async-start(), calls=%async_computation.6 | async-start | bytes 3932160 | tf_op jit(solution)/shard_map/all_gather | solution.py:30
  9.3 108.4 %all-gather.4.cloned.1.call-start = ((), (), s32[]{:S(2)}) async-start(), calls=%async_computation.5 | async-start | bytes 6553600 | tf_op jit(solution)/shard_map/all_gather | solution.py:30
  13.7 25.1 %collective-permute-start = (f32[512,512]{1,0:T(8,128)}, f32[512,512]{1,0:T(8,128)S(1)}, u32[]{:S(2)}, u32[]{:S(2)}) collective-permute-start(f32[512,512]{1,0:T(8,128)} %get-tuple-element.133), channel_id=1, source_target_pairs={{0,1},{1,2},{2,3},{3,4},{4,5},{5,6},{6,7},{7,8},{8,9},{9,10},{10,1... | collective-permute-start | bytes 3145736 | tf_op jit(solution)/shard_map/ppermute | solution.py:21
  20.5 22.7 %collective-permute-start.1 = (f32[512,512]{1,0:T(8,128)}, f32[512,512]{1,0:T(8,128)}, u32[]{:S(2)}, u32[]{:S(2)}) collective-permute-start(f32[512,512]{1,0:T(8,128)} %slice_bitcast_fusion), channel_id=1, source_target_pairs={{0,1},{1,2},{2,3},{3,4},{4,5},{5,6},{6,7},{7,8},{8,9},{9,10},{10,1... | collective-permute-start | bytes 3145736 | tf_op jit(solution)/shard_map/ppermute | solution.py:21
  25.8 27.4 %collective-permute-start.3 = (f32[512,512]{1,0:T(8,128)}, f32[512,512]{1,0:T(8,128)}, u32[]{:S(2)}, u32[]{:S(2)}) collective-permute-start(f32[512,512]{1,0:T(8,128)} %slice_bitcast_fusion), channel_id=1, source_target_pairs={{1,0},{2,1},{3,2},{4,3},{5,4},{6,5},{7,6},{8,7},{9,8},{10,9},{11,1... | collective-permute-start | bytes 3145736 | tf_op jit(solution)/shard_map/ppermute | solution.py:26
  28.9 118.5 %all-to-all-start = ((f32[128,8,128]{2,1,0:T(8,128)}), f32[128,8,128]{2,1,0:T(8,128)S(1)}, u32[]{:S(2)}, u32[]{:S(2)}) async-start(f32[128,8,128]{2,1,0:T(8,128)} %broadcast_in_dim.24), calls=%async_computation | async-start | bytes 1048576 | tf_op jit(solution)/shard_map/all_to_all | solution.py:40
  136.8 37.7 %collective-permute-start.4 = (f32[512,512]{1,0:T(8,128)}, f32[512,512]{1,0:T(8,128)S(1)}, u32[]{:S(2)}, u32[]{:S(2)}) collective-permute-start(f32[512,512]{1,0:T(8,128)} %get-tuple-element.74), channel_id=1, source_target_pairs={{1,0},{2,1},{3,2},{4,3},{5,4},{6,5},{7,6},{8,7},{9,8},{10,9},{11,1... | collective-permute-start | bytes 3145736 | tf_op jit(solution)/shard_map/ppermute | solution.py:26
  139.4 35.0 %collective-permute-start.5 = (f32[512,512]{1,0:T(8,128)}, f32[512,512]{1,0:T(8,128)}, u32[]{:S(2)}, u32[]{:S(2)}) collective-permute-start(f32[512,512]{1,0:T(8,128)} %get-tuple-element.75), channel_id=1, source_target_pairs={{1,0},{2,1},{3,2},{4,3},{5,4},{6,5},{7,6},{8,7},{9,8},{10,9},{11,1... | collective-permute-start | bytes 3145736 | tf_op jit(solution)/shard_map/ppermute | solution.py:26
  141.3 33.1 %collective-permute-start.6 = (f32[512,512]{1,0:T(8,128)}, f32[512,512]{1,0:T(8,128)}, u32[]{:S(2)}, u32[]{:S(2)}) collective-permute-start(f32[512,512]{1,0:T(8,128)} %get-tuple-element.76), channel_id=1, source_target_pairs={{0,1},{1,2},{2,3},{3,4},{4,5},{5,6},{6,7},{7,8},{8,9},{9,10},{10,1... | collective-permute-start | bytes 3145736 | tf_op jit(solution)/shard_map/ppermute | solution.py:21
  145.0 29.5 %collective-permute-start.7 = (f32[512,512]{1,0:T(8,128)}, f32[512,512]{1,0:T(8,128)}, u32[]{:S(2)}, u32[]{:S(2)}) collective-permute-start(f32[512,512]{1,0:T(8,128)} %get-tuple-element.77), channel_id=1, source_target_pairs={{0,1},{1,2},{2,3},{3,4},{4,5},{5,6},{6,7},{7,8},{8,9},{9,10},{10,1... | collective-permute-start | bytes 3145736 | tf_op jit(solution)/shard_map/ppermute | solution.py:21
  194.3 49.2 %collective-permute-start.8 = (f32[512,512]{1,0:T(8,128)}, f32[512,512]{1,0:T(8,128)S(1)}, u32[]{:S(2)}, u32[]{:S(2)}) collective-permute-start(f32[512,512]{1,0:T(8,128)} %get-tuple-element.85), channel_id=1, source_target_pairs={{1,0},{2,1},{3,2},{4,3},{5,4},{6,5},{7,6},{8,7},{9,8},{10,9},{11,1... | collective-permute-start | bytes 3145736 | tf_op jit(solution)/shard_map/ppermute | solution.py:26
  197.7 45.8 %collective-permute-start.9 = (f32[512,512]{1,0:T(8,128)}, f32[512,512]{1,0:T(8,128)S(1)}, u32[]{:S(2)}, u32[]{:S(2)}) collective-permute-start(f32[512,512]{1,0:T(8,128)} %get-tuple-element.86), channel_id=1, source_target_pairs={{1,0},{2,1},{3,2},{4,3},{5,4},{6,5},{7,6},{8,7},{9,8},{10,9},{11,1... | collective-permute-start | bytes 3145736 | tf_op jit(solution)/shard_map/ppermute | solution.py:26
  199.6 43.9 %collective-permute-start.10 = (f32[512,512]{1,0:T(8,128)}, f32[512,512]{1,0:T(8,128)}, u32[]{:S(2)}, u32[]{:S(2)}) collective-permute-start(f32[512,512]{1,0:T(8,128)} %get-tuple-element.87), channel_id=1, source_target_pairs={{0,1},{1,2},{2,3},{3,4},{4,5},{5,6},{6,7},{7,8},{8,9},{9,10},{10,1... | collective-permute-start | bytes 3145736 | tf_op jit(solution)/shard_map/ppermute | solution.py:21
  203.3 40.2 %collective-permute-start.11 = (f32[512,512]{1,0:T(8,128)}, f32[512,512]{1,0:T(8,128)}, u32[]{:S(2)}, u32[]{:S(2)}) collective-permute-start(f32[512,512]{1,0:T(8,128)} %get-tuple-element.88), channel_id=1, source_target_pairs={{0,1},{1,2},{2,3},{3,4},{4,5},{5,6},{6,7},{7,8},{8,9},{9,10},{10,1... | collective-permute-start | bytes 3145736 | tf_op jit(solution)/shard_map/ppermute | solution.py:21
  205.9 37.4 %all-to-all-start.1 = ((f32[32,8,128]{2,1,0:T(8,128)}), f32[32,8,128]{2,1,0:T(8,128)S(1)}, u32[]{:S(2)}, u32[]{:S(2)}) async-start(f32[32,8,128]{2,1,0:T(8,128)} %broadcast_in_dim.25), calls=%async_computation.1 | async-start | bytes 262144 | tf_op jit(solution)/shard_map/all_to_all | solution.py:40
  264.5 34.2 %collective-permute-start.12 = (f32[512,512]{1,0:T(8,128)S(1)}, f32[512,512]{1,0:T(8,128)S(1)}, u32[]{:S(2)}, u32[]{:S(2)}) collective-permute-start(f32[512,512]{1,0:T(8,128)S(1)} %get-tuple-element.94), channel_id=1, source_target_pairs={{1,0},{2,1},{3,2},{4,3},{5,4},{6,5},{7,6},{8,7},{9,8},{10,9},{11,1... | collective-permute-start | bytes 3145736 | tf_op jit(solution)/shard_map/ppermute | solution.py:26
  266.5 32.1 %collective-permute-start.13 = (f32[512,512]{1,0:T(8,128)S(1)}, f32[512,512]{1,0:T(8,128)S(1)}, u32[]{:S(2)}, u32[]{:S(2)}) collective-permute-start(f32[512,512]{1,0:T(8,128)S(1)} %get-tuple-element.95), channel_id=1, source_target_pairs={{1,0},{2,1},{3,2},{4,3},{5,4},{6,5},{7,6},{8,7},{9,8},{10,9},{11,1... | collective-permute-start | bytes 3145736 | tf_op jit(solution)/shard_map/ppermute | solution.py:26
  268.5 30.2 %collective-permute-start.14 = (f32[512,512]{1,0:T(8,128)S(1)}, f32[512,512]{1,0:T(8,128)S(1)}, u32[]{:S(2)}, u32[]{:S(2)}) collective-permute-start(f32[512,512]{1,0:T(8,128)S(1)} %get-tuple-element.96), channel_id=1, source_target_pairs={{0,1},{1,2},{2,3},{3,4},{4,5},{5,6},{6,7},{7,8},{8,9},{9,10},{10,1... | collective-permute-start | bytes 3145736 | tf_op jit(solution)/shard_map/ppermute | solution.py:21
  272.1 26.6 %collective-permute-start.15 = (f32[512,512]{1,0:T(8,128)S(1)}, f32[512,512]{1,0:T(8,128)S(1)}, u32[]{:S(2)}, u32[]{:S(2)}) collective-permute-start(f32[512,512]{1,0:T(8,128)S(1)} %get-tuple-element.97), channel_id=1, source_target_pairs={{0,1},{1,2},{2,3},{3,4},{4,5},{5,6},{6,7},{7,8},{8,9},{9,10},{10,1... | collective-permute-start | bytes 3145736 | tf_op jit(solution)/shard_map/ppermute | solution.py:21
  310.4 22.2 %collective-permute-start.16 = (f32[512,128]{1,0:T(8,128)S(1)}, f32[512,128]{1,0:T(8,128)S(1)}, u32[]{:S(2)}, u32[]{:S(2)}) collective-permute-start(f32[512,128]{1,0:T(8,128)S(1)} %get-tuple-element.103), channel_id=1, source_target_pairs={{1,0},{2,1},{3,2},{4,3},{5,4},{6,5},{7,6},{8,7},{9,8},{10,9},{11,1... | collective-permute-start | bytes 786440 | tf_op jit(solution)/shard_map/ppermute | solution.py:26
  336.4 26.1 %all-to-all-start.2 = ((f32[128,8,128]{2,1,0:T(8,128)}), f32[128,8,128]{2,1,0:T(8,128)S(1)}, u32[]{:S(2)}, u32[]{:S(2)}) async-start(f32[128,8,128]{2,1,0:T(8,128)} %broadcast_in_dim.26), calls=%async_computation.2 | async-start | bytes 1048576 | tf_op jit(solution)/shard_map/all_to_all | solution.py:40
  505.2 28.5 %collective-permute-start.22 = (f32[512,512]{1,0:T(8,128)}, f32[512,512]{1,0:T(8,128)}, u32[]{:S(2)}, u32[]{:S(2)}) collective-permute-start(f32[512,512]{1,0:T(8,128)} %get-tuple-element.117), channel_id=1, source_target_pairs={{1,0},{2,1},{3,2},{4,3},{5,4},{6,5},{7,6},{8,7},{9,8},{10,9},{11,1... | collective-permute-start | bytes 3145736 | tf_op jit(solution)/shard_map/ppermute | solution.py:26
  507.1 26.6 %collective-permute-start.23 = (f32[512,512]{1,0:T(8,128)}, f32[512,512]{1,0:T(8,128)}, u32[]{:S(2)}, u32[]{:S(2)}) collective-permute-start(f32[512,512]{1,0:T(8,128)} %get-tuple-element.114), channel_id=1, source_target_pairs={{0,1},{1,2},{2,3},{3,4},{4,5},{5,6},{6,7},{7,8},{8,9},{9,10},{10,1... | collective-permute-start | bytes 3145736 | tf_op jit(solution)/shard_map/ppermute | solution.py:21
  585.0 24.5 %all-to-all-start.4 = ((f32[128,8,128]{2,1,0:T(8,128)}), f32[128,8,128]{2,1,0:T(8,128)}, u32[]{:S(2)}, u32[]{:S(2)}) async-start(f32[128,8,128]{2,1,0:T(8,128)} %broadcast_in_dim.32), calls=%async_computation.4 | async-start | bytes 1048576 | tf_op jit(solution)/shard_map/all_to_all | solution.py:40
  (55 other events, 874.4 us)
Sparse Core Ops, SparseCore 0:
  10.2 47.9 all-gather.5
  59.9 57.7 all-gather.3

commit v5 on v4

--- a/solution.py
+++ b/solution.py
@@ -13,7 +13,7 @@
 ROOT_TWO = math.sqrt(2.0)
 ANISOTROPY = 0.5
 TIME_STEP = 0.1
-VMEM_LIMIT = 48 * 1024 * 1024
+VMEM_LIMIT = 56 * 1024 * 1024
 
 
 def to_next(block):
@@ -194,82 +194,237 @@
     return high_ref[:, cut], low_ref[:, cut]
 
 
-def site_send_kernel(place_ref, high, low, four_ref, up_ref, down_ref, d0, d1, u1, u2, zh, zl):
-    up, down = (up_ref[0], up_ref[1]), (down_ref[0], down_ref[1])
-    z = []
+def join(*blocks):
+    return jnp.concatenate(blocks, axis=1)
+
+
+def cut_columns(value, count):
+    width = value.shape[1] // count
+    return [value[:, i * width : (i + 1) * width] for i in range(count)]
+
+
+class Fetch:
+    def __init__(self, sems):
+        self.sems = sems
+        self.used = 0
+        self.waiting = {}
+
+    def start(self, name, source, target):
+        copy = pltpu.make_async_copy(source, target, self.sems.at[self.used])
+        self.used += 1
+        copy.start()
+        self.waiting[name] = copy
+
+    def wait(self, *names):
+        for name in names:
+            if name in self.waiting:
+                self.waiting.pop(name).wait()
+
+    def wait_all(self):
+        self.wait(*list(self.waiting))
+
+
+def start_state(fetch, s, high, low, high_v, low_v):
+    size = high_v.shape[1]
+    cut = pl.ds(s * size, size)
+    fetch.start(("xh", s), high.at[:, cut], high_v.at[s])
+    fetch.start(("xl", s), low.at[:, cut], low_v.at[s])
+
+
+def site_send_kernel(high, low, four, up, down, *refs):
+    d0, d1, u1, u2, zh, zl = refs[:6]
+    xh_v, xl_v, four_v, up_v, down_v, zh_v, zl_v, d_v, u_v, sems = refs[6:]
+    fetch = Fetch(sems)
     for s in (1, 0, 2):
-        pair = split(product(columns_of(high, low, s), pair_of(four_ref, s)))
-        zh[s], zl[s] = pair
+        start_state(fetch, s, high, low, xh_v, xl_v)
+        fetch.start(("four", s), four.at[s], four_v.at[s])
+        if s == 1:
+            fetch.start("down", down, down_v)
+            fetch.start("up", up, up_v)
+    outs = Fetch(sems)
+    outs.used = fetch.used
+    for s in (1, 0, 2):
+        fetch.wait(("xh", s), ("xl", s), ("four", s))
+        z = product((xh_v[s], xl_v[s]), (four_v[s, 0], four_v[s, 1]))
+        zh_v[s], zl_v[s] = split(z)
+        outs.start(("zh", s), zh_v.at[s], zh.at[s])
+        outs.start(("zl", s), zl_v.at[s], zl.at[s])
+        pair = (zh_v[s], zl_v[s])
         if s < 2:
-            (d0, d1)[s][...] = product(down, pair)
+            fetch.wait("down")
+            d_v[s] = product((down_v[0], down_v[1]), pair)
+            outs.start(("d", s), d_v.at[s], (d0, d1)[s])
         if s > 0:
-            (u1, u2)[s - 1][...] = product(up, pair)
-
-
-def site_local_kernel(place_ref, high, low, mix_ref, stack_ref, zh, zl, out_ref):
-    x = [columns_of(high, low, s) for s in range(3)]
-    terms = (((0, 0), (1, 1)), ((1, 2), (0, 3), (2, 4)), ((2, 5), (1, 6)))
+            fetch.wait("up")
+            u_v[s - 1] = product((up_v[0], up_v[1]), pair)
+            outs.start(("u", s), u_v.at[s - 1], (u1, u2)[s - 1])
+    outs.wait_all()
+
+
+TERMS = (((0, 0), (1, 1)), ((1, 2), (0, 3), (2, 4)), ((2, 5), (1, 6)))
+
+
+def site_local_kernel(high, low, mix, stack, zh, zl, out, *refs):
+    xh_v, xl_v, mix_v, stack_v, zh_v, zl_v, out_v, sems = refs
+    fetch = Fetch(sems)
+    seen = set()
+    for s in range(3):
+        for source, matrix in TERMS[s]:
+            if source not in seen:
+                seen.add(source)
+                start_state(fetch, source, high, low, xh_v, xl_v)
+            fetch.start(("mix", matrix), mix.at[matrix], mix_v.at[matrix])
+        if s == 0:
+            fetch.start(("stack", 0), stack.at[0], stack_v.at[0])
+        fetch.start(("stack", 1 + s), stack.at[1 + s], stack_v.at[1 + s])
+        fetch.start(("zh", s), zh.at[s], zh_v.at[s])
+        fetch.start(("zl", s), zl.at[s], zl_v.at[s])
+    outs = Fetch(sems)
+    outs.used = fetch.used
     for s in range(3):
         total = None
-        for source, matrix in terms[s]:
-            value = product(x[source], pair_of(mix_ref, matrix))
+        for source, matrix in TERMS[s]:
+            fetch.wait(("xh", source), ("xl", source), ("mix", matrix))
+            value = product((xh_v[source], xl_v[source]), (mix_v[matrix, 0], mix_v[matrix, 1]))
             total = value if total is None else total + value
-        y = product(pair_of(stack_ref, 0), split(total))
-        out_ref[s] = y + product(pair_of(stack_ref, 1 + s), (zh[s], zl[s]))
-
-
-def bond_send_kernel(place_ref, high, low, p_ref, up_ref, down_ref, d_ref, u_ref):
-    x = (high[...], low[...])
-    d_ref[...] = product((down_ref[0], down_ref[1]), split(product(x, pair_of(p_ref, 3))))
-    u_ref[...] = product((up_ref[0], up_ref[1]), split(product(x, pair_of(p_ref, 2))))
-
-
-def bond_local_kernel(place_ref, high, low, p_ref, stack_ref, out_ref):
-    x = (high[...], low[...])
+        fetch.wait(("stack", 0), ("stack", 1 + s), ("zh", s), ("zl", s))
+        y = product((stack_v[0, 0], stack_v[0, 1]), split(total))
+        out_v[s] = y + product((stack_v[1 + s, 0], stack_v[1 + s, 1]), (zh_v[s], zl_v[s]))
+        outs.start(("out", s), out_v.at[s], out.at[s])
+    outs.wait_all()
+
+
+def bond_send_kernel(high, low, bond, up, down, d_out, u_out, *refs):
+    xh_v, xl_v, bond_v, up_v, down_v, d_v, u_v, sems = refs
+    fetch = Fetch(sems)
+    start_state(fetch, 0, high, low, xh_v, xl_v)
+    fetch.start(("p", 3), bond.at[3], bond_v.at[1])
+    fetch.start("down", down, down_v)
+    fetch.start(("p", 2), bond.at[2], bond_v.at[0])
+    fetch.start("up", up, up_v)
+    outs = Fetch(sems)
+    outs.used = fetch.used
+    fetch.wait(("xh", 0), ("xl", 0), ("p", 3))
+    x = (xh_v[0], xl_v[0])
+    moved = split(product(x, (bond_v[1, 0], bond_v[1, 1])))
+    fetch.wait("down")
+    d_v[...] = product((down_v[0], down_v[1]), moved)
+    outs.start("d", d_v, d_out)
+    fetch.wait(("p", 2))
+    moved = split(product(x, (bond_v[0, 0], bond_v[0, 1])))
+    fetch.wait("up")
+    u_v[...] = product((up_v[0], up_v[1]), moved)
+    outs.start("u", u_v, u_out)
+    outs.wait_all()
+
+
+BOND_TERMS = ((0, 0), (4, 2), (1, 4))
+
+
+def bond_local_kernel(high, low, bond, stack, out, *refs):
+    xh_v, xl_v, bond_v, stack_v, out_v, sems = refs
+    fetch = Fetch(sems)
+    start_state(fetch, 0, high, low, xh_v, xl_v)
+    for k, (a, matrix) in enumerate(BOND_TERMS):
+        fetch.start(("p", k), bond.at[a], bond_v.at[k])
+        fetch.start(("r", k), stack.at[matrix], stack_v.at[k])
     total = None
-    for a, matrix in ((0, 0), (4, 2), (1, 4)):
-        value = product(pair_of(stack_ref, matrix), split(product(x, pair_of(p_ref, a))))
+    for k in range(3):
+        fetch.wait(("xh", 0), ("xl", 0), ("p", k))
+        moved = split(product((xh_v[0], xl_v[0]), (bond_v[k, 0], bond_v[k, 1])))
+        fetch.wait(("r", k))
+        value = product((stack_v[k, 0], stack_v[k, 1]), moved)
+        total = value if total is None else total + value
+    out_v[...] = total
+    outs = Fetch(sems)
+    outs.used = fetch.used
+    outs.start("out", out_v, out.at[0])
+    outs.wait_all()
+
+
+def site_send_quarter(place_ref, high, low, four_ref, up_ref, down_ref, d0, d1, u1, u2, zh, zl):
+    z = [product(columns_of(high, low, s), pair_of(four_ref, s)) for s in range(3)]
+    for s in range(3):
+        zh[s], zl[s] = split(z[s])
+    d0[...], d1[...] = cut_columns(product((down_ref[0], down_ref[1]), split(join(z[0], z[1]))), 2)
+    u1[...], u2[...] = cut_columns(product((up_ref[0], up_ref[1]), split(join(z[1], z[2]))), 2)
+
+
+def site_local_quarter(place_ref, high, low, mix_ref, stack_ref, zh, zl, out_ref):
+    def merged(s, *matrices):
+        right = (join(*[mix_ref[m, part] for m in matrices]) for part in range(2))
+        return cut_columns(product(columns_of(high, low, s), tuple(right)), len(matrices))
+
+    p0, p1 = merged(0, 0, 3)
+    more0, more1, p2 = merged(1, 1, 2, 6)
+    last2, last1 = merged(2, 5, 4)
+    mixed = split(join(p0 + more0, p1 + more1 + last1, p2 + last2))
+    y = cut_columns(product(pair_of(stack_ref, 0), mixed), 3)
+    for s in range(3):
+        out_ref[s] = y[s] + product(pair_of(stack_ref, 1 + s), (zh[s], zl[s]))
+
+
+def bond_send_quarter(place_ref, high, low, p_ref, up_ref, down_ref, d_ref, u_ref):
+    right = (join(p_ref[3, part], p_ref[2, part]) for part in range(2))
+    down, up = cut_columns(product((high[...], low[...]), tuple(right)), 2)
+    d_ref[...] = product((down_ref[0], down_ref[1]), split(down))
+    u_ref[...] = product((up_ref[0], up_ref[1]), split(up))
+
+
+def bond_local_quarter(place_ref, high, low, p_ref, stack_ref, out_ref):
+    right = (join(*[p_ref[a, part] for a, _ in BOND_TERMS]) for part in range(2))
+    moved = cut_columns(product((high[...], low[...]), tuple(right)), 3)
+    total = None
+    for value, (_, matrix) in zip(moved, BOND_TERMS):
+        value = product(pair_of(stack_ref, matrix), split(value))
         total = value if total is None else total + value
     out_ref[0] = total
 
 
-def product_call(kernel, place, whole, cut, outs, quarter, flops):
-    size = cut[0].shape[-1]
-    width = size // 4 if quarter else size // 2
-
-    def by_place(array):
+UNIT = 6 * 512**3
+
+
+def quarter_call(kernel, place, operands, outs, products):
+    size = operands[0][1].shape[0]
+    width = size // 4
+
+    def spec(is_whole, array):
         lead = (0,) * (array.ndim - 1)
-        block = array.shape[:-1] + (width,)
-        if quarter and array.shape[-1] == width:
-            return pl.BlockSpec(block, lambda i, p: lead + (0,))
-        if quarter:
-            return pl.BlockSpec(block, lambda i, p: lead + (p[0],))
-        return pl.BlockSpec(block, lambda i, p: lead + (i,))
-
-    def all_of(array):
-        lead = (0,) * array.ndim
-        return pl.BlockSpec(array.shape, lambda i, p: lead)
-
-    shapes = [
-        jax.ShapeDtypeStruct(shape + (size, width if quarter else size), dtype) for shape, dtype in outs
-    ]
+        if is_whole:
+            return pl.BlockSpec(array.shape, lambda i, p: lead + (0,))
+        return pl.BlockSpec(array.shape[:-1] + (width,), lambda i, p: lead + (p[0],))
+
+    shapes = [jax.ShapeDtypeStruct(shape + (size, width), dtype) for shape, dtype in outs]
     return pl.pallas_call(
         kernel,
         grid_spec=pltpu.PrefetchScalarGridSpec(
             num_scalar_prefetch=1,
-            grid=(1 if quarter else size // width,),
-            in_specs=[all_of(a) if is_whole else by_place(a) for is_whole, a in whole],
-            out_specs=[by_place(shape) for shape in shapes],
+            grid=(1,),
+            in_specs=[spec(*operand) for operand in operands],
+            out_specs=[spec(True, shape) for shape in shapes],
         ),
         out_shape=shapes,
         compiler_params=params(),
         cost_estimate=pl.CostEstimate(
-            flops=flops // (4 if quarter else 1), bytes_accessed=16 * 2**20, transcendentals=0
+            flops=products * UNIT // 4, bytes_accessed=12 * 2**20, transcendentals=0
         ),
-    )(place, *[a for _, a in whole])
-
-
-UNIT = 6 * 512**3
+    )(place, *[array for _, array in operands])
+
+
+def full_call(kernel, operands, outs, scratch, copies, products):
+    anywhere = pl.BlockSpec(memory_space=pl.ANY)
+    return pl.pallas_call(
+        kernel,
+        in_specs=[anywhere] * len(operands),
+        out_specs=[anywhere] * len(outs),
+        out_shape=[jax.ShapeDtypeStruct(shape, dtype) for shape, dtype in outs],
+        scratch_shapes=[pltpu.VMEM(shape, dtype) for shape, dtype in scratch]
+        + [pltpu.SemaphoreType.DMA((copies,))],
+        compiler_params=params(),
+        cost_estimate=pl.CostEstimate(
+            flops=products * UNIT, bytes_accessed=16 * 2**20, transcendentals=0
+        ),
+    )(*operands)
 
 
 def state_spec(spins, step, size):
@@ -571,29 +726,51 @@
         sums, _ = lax.optimization_barrier((sums, after))
         return exchange(sums, "sec")
 
+    matrix = (size, size)
+    thirds = ((3,) + matrix, BF16)
+    pairs = ((2,) + matrix, BF16)
+    f32 = jnp.float32
+
     def apply_site(pair, sums, quarter):
-        plain = ((), jnp.float32)
-        d0, d1, u1, u2, zh, zl = product_call(
-            site_send_kernel,
-            place,
-            [(True, pair[0]), (True, pair[1]), (False, four), (True, up), (True, down)],
-            [four],
-            [plain] * 4 + [((3,), BF16)] * 2,
-            quarter,
-            7 * UNIT,
-        )
+        if quarter:
+            d0, d1, u1, u2, zh, zl = quarter_call(
+                site_send_quarter,
+                place,
+                [(True, pair[0]), (True, pair[1]), (False, four), (True, up), (True, down)],
+                [((), f32)] * 4 + [((3,), BF16)] * 2,
+                7,
+            )
+        else:
+            d0, d1, u1, u2, zh, zl = full_call(
+                site_send_kernel,
+                [pair[0], pair[1], four, up, down],
+                [(matrix, f32)] * 4 + [thirds] * 2,
+                [thirds, thirds, ((3, 2) + matrix, BF16), pairs, pairs, thirds, thirds]
+                + [((2,) + matrix, f32)] * 2,
+                24,
+                7,
+            )
         d1, u1 = to_previous(d1), to_next(u1)
         d0, u2 = to_previous(d0), to_next(u2)
         totals = send_sums(sums, zh)
-        (local,) = product_call(
-            site_local_kernel,
-            place,
-            [(True, pair[0]), (True, pair[1]), (False, mix), (True, stack), (False, zh), (False, zl)],
-            [mix],
-            [((3,), jnp.float32)],
-            quarter,
-            13 * UNIT,
-        )
+        if quarter:
+            (local,) = quarter_call(
+                site_local_quarter,
+                place,
+                [(True, pair[0]), (True, pair[1]), (False, mix), (True, stack), (True, zh), (True, zl)],
+                [((3,), f32)],
+                13,
+            )
+        else:
+            (local,) = full_call(
+                site_local_kernel,
+                [pair[0], pair[1], mix, stack, zh, zl],
+                [((3,) + matrix, f32)],
+                [thirds, thirds, ((7, 2) + matrix, BF16), ((4, 2) + matrix, BF16), thirds, thirds]
+                + [((3,) + matrix, f32)],
+                32,
+                13,
+            )
         return [local, d0, d1, u1, u2], totals
 
     states, weights = evolve(place, site_full, site_nu, apply_site, -TIME_STEP, 3)
@@ -607,28 +784,45 @@
     start = factor * live[:, None] * live[None, :] / bond_scale
     bond_nu = jnp.broadcast_to(weights[4:5] * bond_scale, (8, 128))
 
+    single = ((1,) + matrix, BF16)
+
     def apply_bond(pair, sums, quarter):
-        plain = ((), jnp.float32)
-        down_term, up_term = product_call(
-            bond_send_kernel,
-            place,
-            [(True, pair[0]), (True, pair[1]), (False, bond), (True, up), (True, down)],
-            [bond],
-            [plain] * 2,
-            quarter,
-            4 * UNIT,
-        )
+        if quarter:
+            down_term, up_term = quarter_call(
+                bond_send_quarter,
+                place,
+                [(True, pair[0]), (True, pair[1]), (False, bond), (True, up), (True, down)],
+                [((), f32)] * 2,
+                4,
+            )
+        else:
+            down_term, up_term = full_call(
+                bond_send_kernel,
+                [pair[0], pair[1], bond, up, down],
+                [(matrix, f32)] * 2,
+                [single, single, ((2, 2) + matrix, BF16), pairs, pairs] + [(matrix, f32)] * 2,
+                8,
+                4,
+            )
         totals = send_sums(sums, up_term)
         down_term, up_term = to_previous(down_term), to_next(up_term)
-        (local,) = product_call(
-            bond_local_kernel,
-            place,
-            [(True, pair[0]), (True, pair[1]), (False, bond), (True, stack)],
-            [bond],
-            [((1,), jnp.float32)],
-            quarter,
-            6 * UNIT,
-        )
+        if quarter:
+            (local,) = quarter_call(
+                bond_local_quarter,
+                place,
+                [(True, pair[0]), (True, pair[1]), (False, bond), (True, stack)],
+                [((1,), f32)],
+                6,
+            )
+        else:
+            (local,) = full_call(
+                bond_local_kernel,
+                [pair[0], pair[1], bond, stack],
+                [((1,) + matrix, f32)],
+                [single, single, ((3, 2) + matrix, BF16), ((3, 2) + matrix, BF16), (matrix, f32)],
+                9,
+                6,
+            )
         return [local, down_term, up_term], totals
 
     states, weights = evolve(place, start, bond_nu, apply_bond, TIME_STEP, 1)

time: 632 us -> 614 us (0.972)
  waiting for transfers between devices: 84.6 us -> 102 us
  local copies, waits for them, and re-layouts: 41.4 us -> 25.9 us
  Pallas kernels: 252 us -> 242 us
  starting transfers between devices: 129 us -> 122 us
    pallas_call x16, Pallas kernels: 186 us -> 144 us  [the longest x12 117 us: full_call(): pl.pallas_call(kernel, in_specs=[anywhere] * len(operands), out_specs=[an...]
    unnamed x91 -> x61, local copies, waits for them, and re-layouts: 33.8 us -> 16.6 us
    ppermute x14, waiting for transfers between devices: 10.5 us -> 18.5 us  [to_previous(): return lax.ppermute(block, 'sec', [(i + 1, i) for i in range(count - 1)])]
    all_to_all x5, starting transfers between devices: 51.9 us -> 45.3 us  [exchange(): return lax.all_to_all(sent, axis, 0, 0)]
  transfers between devices with their start and end apart: 35 -> 35, of which waited for: 9 -> 13; matrix products, arithmetic and copies ran while one was open for 2% -> 2% of each run, Pallas kernels for 25% -> 22%
where the time goes in v5:
time: 614 us; the launch traced here: 605 us
  Pallas kernels  242 us (39%)
  starting transfers between devices  122 us (20%)
  waiting for transfers between devices  102 us (17%)
  other arithmetic  84.9 us (14%)
  local copies, waits for them, and re-layouts  25.9 us (4%)
  between operations  18.3 us (3%)
  matrix products  10.1 us (2%)
    pallas_call x12, Pallas kernels, full_call(): pl.pallas_call(kernel, in_specs=[anywhere] * len(operands), out_specs=[an...  117 us
    another operation x14, other arithmetic, body(): factor = jnp.linalg.cholesky(gram[None])[0]  78.7 us
    all_gather x2, waiting for transfers between devices, gather_col(): return lax.all_gather(block, 'col', axis=axis, tiled=True)  51.3 us
    ppermute x14, starting transfers between devices, to_next(): return lax.ppermute(block, 'sec', [(i, i + 1) for i in range(count - 1)])  46.2 us
    all_to_all x5, starting transfers between devices, exchange(): return lax.all_to_all(sent, axis, 0, 0)  45.3 us
    ppermute x14, starting transfers between devices, to_previous(): return lax.ppermute(block, 'sec', [(i + 1, i) for i in range(count - 1)])  30 us
    pallas_call x4, Pallas kernels, quarter_call(): pl.pallas_call(kernel, grid_spec=pltpu.PrefetchScalarGridSpec(num_scalar_...  27.6 us
    pallas_call x4, Pallas kernels, combine(): pl.pallas_call(functools.partial(combine_kernel, second, spins), grid=(si...  24.4 us
  transfers between devices with their start and end apart: 35, of which 13 were waited for; matrix products, arithmetic and copies ran while one was open for 2% of the time, Pallas kernels for 22%

profile of v5, /device:TPU:1, one launch (start us, length us, event | category | flops | bytes accessed | tf_op | source)
XLA Modules:
  0.0 605.5 jit_solution(5115966418041838096)
XLA Ops:
  30.3 10.7 %all-to-all-start = ((f32[128,8,128]{2,1,0:T(8,128)}), f32[128,8,128]{2,1,0:T(8,128)S(1)}, u32[]{:S(2)}, u32[]{:S(2)}) async-start(f32[128,8,128]{2,1,0:T(8,128)} %broadcast_in_dim.24), calls=%async_computation | async-start | bytes 1048576 | tf_op jit(solution)/shard_map/all_to_all | solution.py:40
  41.7 11.4 %collective-permute-done.3.afour_ref = f32[512,512]{1,0:T(8,128)} collective-permute-done((f32[512,512]{1,0:T(8,128)}, f32[512,512]{1,0:T(8,128)}, u32[]{:S(2)}, u32[]{:S(2)}) %collective-permute-start.3) | collective-permute-done | bytes 1048608 | tf_op jit(solution)/shard_map/ppermute | solution.py:26
  53.1 9.1 %shard_map.71 = (bf16[3,2,512,512]{3,2,1,0:T(8,128)(2,1)}, bf16[7,2,512,512]{3,2,1,0:T(8,128)(2,1)}) custom-call(s32[2]{0:T(128)} %add_convert_fusion.flag_ref, f32[5,512,512]{2,1,0:T(8,128)} %bitcast.110, f32[512,512]{1,0:T(8,128)} %copy-done.4, f32[512,512]{1,0:T(8,128)} %copy-done.6, f32[512,512]{1,0:T(8,128)} %collective-permute-done.2.asum_ref, ...), custom_call_target="tpu_custom_call" | custom-call | tf_op jit(solution)/shard_map/pallas_call | solution.py:157
  66.4 51.3 %all-gather.4.cloned.1.call-done.block_ref = f32[4,5,512,128]{3,2,1,0:T(8,128)} async-done(((f32[1,5,512,128]{3,2,1,0:T(8,128)}), f32[4,5,512,128]{3,2,1,0:T(8,128)}) %all-gather.4.cloned.1.call-update) | async-done | bytes 5242896 | tf_op jit(solution)/shard_map/all_gather | solution.py:30
  124.3 9.4 %shard_map.73 = (f32[512,512]{1,0:T(8,128)}, f32[512,512]{1,0:T(8,128)}, f32[512,512]{1,0:T(8,128)}, f32[512,512]{1,0:T(8,128)}, bf16[3,512,512]{2,1,0:T(8,128)(2,1)}, /*index=5*/bf16[3,512,512]{2,1,0:T(8,128)(2,1)}) custom-call(bf16[512,1536]{1,0:T(8,128)(2,1)} %get-tuple-element.65.high, bf16[512,1536]{1,0:T(8,128)(2,1)} %get-tuple-element.66.low, ...), custom_call_target="tpu_custom_call" | custom-call | flops 5637144576 | bytes 16777216 | tf_op jit(solution)/shard_map/pallas_call | solution.py:416
  146.8 14.6 %shard_map.74.refs_0_ = f32[3,512,512]{2,1,0:T(8,128)} custom-call(bf16[512,1536]{1,0:T(8,128)(2,1)} %get-tuple-element.65.high, bf16[512,1536]{1,0:T(8,128)(2,1)} %get-tuple-element.66.low, bf16[7,2,512,512]{3,2,1,0:T(8,128)(2,1)} %get-tuple-element.67.mix.mix_ref, bf16[5,2,512,512]{3,2,1,0:T(8,128)(2,1)} %get-tuple-element.68.stack.stack_ref, ...), custom_call_target="tpu_custom_call" | custom-call | flops 10468982784 | bytes 16777216 | tf_op jit(solution)/shard_map/pallas_call | solution.py:416
  172.8 9.5 %shard_map.76 = (f32[512,512]{1,0:T(8,128)}, f32[512,512]{1,0:T(8,128)}, f32[512,512]{1,0:T(8,128)}, f32[512,512]{1,0:T(8,128)}, bf16[3,512,512]{2,1,0:T(8,128)(2,1)}, /*index=5*/bf16[3,512,512]{2,1,0:T(8,128)(2,1)}) custom-call(bf16[512,1536]{1,0:T(8,128)(2,1)} %get-tuple-element.79.high, bf16[512,1536]{1,0:T(8,128)(2,1)} %get-tuple-element.80.low, ...), custom_call_target="tpu_custom_call" | custom-call | flops 5637144576 | bytes 16777216 | tf_op jit(solution)/shard_map/pallas_call | solution.py:416
  193.7 11.6 %all-to-all-start.1 = ((f32[32,8,128]{2,1,0:T(8,128)}), f32[32,8,128]{2,1,0:T(8,128)S(1)}, u32[]{:S(2)}, u32[]{:S(2)}) async-start(f32[32,8,128]{2,1,0:T(8,128)} %broadcast_in_dim.25), calls=%async_computation.1 | async-start | bytes 262144 | tf_op jit(solution)/shard_map/all_to_all | solution.py:40
  205.2 14.6 %shard_map.78.refs_1_ = f32[3,512,512]{2,1,0:T(8,128)} custom-call(bf16[512,1536]{1,0:T(8,128)(2,1)} %get-tuple-element.79.high, bf16[512,1536]{1,0:T(8,128)(2,1)} %get-tuple-element.80.low, bf16[7,2,512,512]{3,2,1,0:T(8,128)(2,1)} %get-tuple-element.67.mix.mix_ref, bf16[5,2,512,512]{3,2,1,0:T(8,128)(2,1)} %get-tuple-element.68.stack.stack_ref, ...), custom_call_target="tpu_custom_call" | custom-call | flops 10468982784 | bytes 16777216 | tf_op jit(solution)/shard_map/pallas_call | solution.py:416
  228.7 8.4 %shard_map.79 = (f32[512,1536]{1,0:T(8,128)}, bf16[512,1536]{1,0:T(8,128)(2,1)}, bf16[512,1536]{1,0:T(8,128)(2,1)}) custom-call(f32[8,128]{1,0:T(8,128)} %shard_map.77.scale_ref, f32[512,1536]{1,0:T(8,128)} %get-tuple-element.83.w_ref.refs_3_.refs_4_.refs_5_.refs_1_, f32[512,1536]{1,0:T(8,128)} %bitcast.104, f32[3,512,512]{2,1,0:T(8,128)} %shard_map.78.refs_1_, ...), custom_call_target="tpu_custom_call" | custom-call | tf_op jit(solution)/shard_map/pallas_call | solution.py:515
  237.1 9.4 %shard_map.80 = (f32[512,512]{1,0:T(8,128)}, f32[512,512]{1,0:T(8,128)}, f32[512,512]{1,0:T(8,128)}, f32[512,512]{1,0:T(8,128)}, bf16[3,512,512]{2,1,0:T(8,128)(2,1)}, /*index=5*/bf16[3,512,512]{2,1,0:T(8,128)(2,1)}) custom-call(bf16[512,1536]{1,0:T(8,128)(2,1)} %get-tuple-element.90.high, bf16[512,1536]{1,0:T(8,128)(2,1)} %get-tuple-element.91.low, ...), custom_call_target="tpu_custom_call" | custom-call | flops 5637144576 | bytes 16777216 | tf_op jit(solution)/shard_map/pallas_call | solution.py:416
  256.7 14.6 %shard_map.81.refs_0_ = f32[3,512,512]{2,1,0:T(8,128)} custom-call(bf16[512,1536]{1,0:T(8,128)(2,1)} %get-tuple-element.90.high, bf16[512,1536]{1,0:T(8,128)(2,1)} %get-tuple-element.91.low, bf16[7,2,512,512]{3,2,1,0:T(8,128)(2,1)} %get-tuple-element.67.mix.mix_ref, bf16[5,2,512,512]{3,2,1,0:T(8,128)(2,1)} %get-tuple-element.68.stack.stack_ref, ...), custom_call_target="tpu_custom_call" | custom-call | flops 10468982784 | bytes 16777216 | tf_op jit(solution)/shard_map/pallas_call | solution.py:416
  301.7 9.4 %shard_map.84.refs_12_ = f32[3,512,128]{2,1,0:T(8,128)} custom-call(s32[1]{0:T(128)} %bitcast.place_ref, bf16[512,1536]{1,0:T(8,128)(2,1)} %get-tuple-element.99.high, bf16[512,1536]{1,0:T(8,128)(2,1)} %get-tuple-element.100.low, bf16[7,2,512,512]{3,2,1,0:T(8,128)(2,1)} %get-tuple-element.67.mix.mix_ref, ...), custom_call_target="tpu_custom_call" | custom-call | flops 2617245696 | bytes 12582912 | tf_op jit(solution)/shard_map/pallas_call | solution.py:398
  349.3 8.0 %convolution_add_fusion = f32[512,512]{0,1:T(8,128)S(1)} fusion(f32[512,1536]{1,0:T(8,128)} %shard_map.88, f32[512]{0:T(512)S(1)} %broadcast_subtract_fusion), kind=kOutput, calls=%fused_computation | convolution fusion | flops 4832624640 | bytes 4196352 | tf_op jit(solution)/shard_map/dot_general | solution.py:779
  357.9 11.7 %custom-call.31 = f32[1,128,128]{2,1,0:T(8,128)S(1)} custom-call(f32[1,128,128]{2,1,0:T(8,128)S(1)} %cholesky.267), custom_call_target="Cholesky" | custom-call | tf_op jit(solution)/shard_map/jit(cholesky)/cholesky | solution.py:782
  369.8 9.8 %custom-call.32 = f32[1,1,128,128]{2,3,1,0:T(8,128)S(1)} custom-call(f32[1,1,128,128]{3,2,1,0:T(8,128)S(1)} %get-tuple-element.145), custom_call_target="InvertDiagBlocksLowerTriangular" | custom-call | tf_op jit(solution)/shard_map/jit(cholesky)/cholesky | solution.py:782
  380.5 11.7 %custom-call.33 = f32[1,128,128]{2,1,0:T(8,128)S(1)} custom-call(f32[1,128,128]{2,1,0:T(8,128)S(1)} %cholesky.271), custom_call_target="Cholesky" | custom-call | tf_op jit(solution)/shard_map/jit(cholesky)/cholesky | solution.py:782
  392.3 9.8 %custom-call.34 = f32[1,1,128,128]{2,3,1,0:T(8,128)S(1)} custom-call(f32[1,1,128,128]{3,2,1,0:T(8,128)S(1)} %get-tuple-element.142), custom_call_target="InvertDiagBlocksLowerTriangular" | custom-call | tf_op jit(solution)/shard_map/jit(cholesky)/cholesky | solution.py:782
  402.7 11.7 %custom-call.35 = f32[1,128,128]{2,1,0:T(8,128)S(1)} custom-call(f32[1,128,128]{2,1,0:T(8,128)S(1)} %cholesky.276), custom_call_target="Cholesky" | custom-call | tf_op jit(solution)/shard_map/jit(cholesky)/cholesky | solution.py:782
  414.5 10.0 %custom-call.36 = f32[1,1,128,128]{2,3,1,0:T(8,128)S(1)} custom-call(f32[1,1,128,128]{3,2,1,0:T(8,128)S(1)} %get-tuple-element.139), custom_call_target="InvertDiagBlocksLowerTriangular" | custom-call | tf_op jit(solution)/shard_map/jit(cholesky)/cholesky | solution.py:782
  425.1 11.7 %custom-call.37 = f32[1,128,128]{2,1,0:T(8,128)S(1)} custom-call(f32[1,128,128]{2,1,0:T(8,128)S(1)} %fusion.4), custom_call_target="Cholesky" | custom-call | tf_op jit(solution)/shard_map/jit(cholesky)/cholesky | solution.py:782
  459.0 8.2 %shard_map.91.refs_0_ = f32[1,512,512]{2,1,0:T(8,128)} custom-call(bf16[512,512]{1,0:T(8,128)(2,1)} %get-tuple-element.107.high, bf16[512,512]{1,0:T(8,128)(2,1)} %get-tuple-element.108.low, bf16[5,2,512,512]{3,2,1,0:T(8,128)(2,1)} %shard_map.90.bond.p_ref, bf16[5,2,512,512]{3,2,1,0:T(8,128)(2,1)} %get-tuple-element.68.stack.stack_ref), custom_call_target="tpu_custom_call" | custom-call | flops 4831838208 | bytes 16777216 | tf_op jit(solution)/shard_map/pallas_call | solution.py:416
  497.8 8.3 %shard_map.96.refs_1_ = f32[1,512,512]{2,1,0:T(8,128)} custom-call(bf16[512,512]{1,0:T(8,128)(2,1)} %get-tuple-element.112.high, bf16[512,512]{1,0:T(8,128)(2,1)} %get-tuple-element.113.low, bf16[5,2,512,512]{3,2,1,0:T(8,128)(2,1)} %shard_map.90.bond.p_ref, bf16[5,2,512,512]{3,2,1,0:T(8,128)(2,1)} %get-tuple-element.68.stack.stack_ref), custom_call_target="tpu_custom_call" | custom-call | flops 4831838208 | bytes 16777216 | tf_op jit(solution)/shard_map/pallas_call | solution.py:416
  529.6 8.3 %shard_map.98.refs_0_ = f32[1,512,512]{2,1,0:T(8,128)} custom-call(bf16[512,512]{1,0:T(8,128)(2,1)} %get-tuple-element.119.high, bf16[512,512]{1,0:T(8,128)(2,1)} %get-tuple-element.120.low, bf16[5,2,512,512]{3,2,1,0:T(8,128)(2,1)} %shard_map.90.bond.p_ref, bf16[5,2,512,512]{3,2,1,0:T(8,128)(2,1)} %get-tuple-element.68.stack.stack_ref), custom_call_target="tpu_custom_call" | custom-call | flops 4831838208 | bytes 16777216 | tf_op jit(solution)/shard_map/pallas_call | solution.py:416
  (187 shorter events, 293.9 us)
Async XLA Ops:
  7.2 55.0 %all-gather.6.cloned.1.call-start = ((), (), s32[]{:S(2)}) async-start(), calls=%async_computation.6 | async-start | bytes 3932160 | tf_op jit(solution)/shard_map/all_gather | solution.py:30
  9.3 108.4 %all-gather.4.cloned.1.call-start = ((), (), s32[]{:S(2)}) async-start(), calls=%async_computation.5 | async-start | bytes 6553600 | tf_op jit(solution)/shard_map/all_gather | solution.py:30
  13.6 28.0 %collective-permute-start = (f32[512,512]{1,0:T(8,128)}, f32[512,512]{1,0:T(8,128)S(1)}, u32[]{:S(2)}, u32[]{:S(2)}) collective-permute-start(f32[512,512]{1,0:T(8,128)} %get-tuple-element.133), channel_id=1, source_target_pairs={{0,1},{1,2},{2,3},{3,4},{4,5},{5,6},{6,7},{7,8},{8,9},{9,10},{10,1... | collective-permute-start | bytes 3145736 | tf_op jit(solution)/shard_map/ppermute | solution.py:21
  20.4 21.2 %collective-permute-start.1 = (f32[512,512]{1,0:T(8,128)}, f32[512,512]{1,0:T(8,128)S(1)}, u32[]{:S(2)}, u32[]{:S(2)}) collective-permute-start(f32[512,512]{1,0:T(8,128)} %slice_bitcast_fusion), channel_id=1, source_target_pairs={{0,1},{1,2},{2,3},{3,4},{4,5},{5,6},{6,7},{7,8},{8,9},{9,10},{10,1... | collective-permute-start | bytes 3145736 | tf_op jit(solution)/shard_map/ppermute | solution.py:21
  24.8 28.3 %collective-permute-start.3 = (f32[512,512]{1,0:T(8,128)}, f32[512,512]{1,0:T(8,128)}, u32[]{:S(2)}, u32[]{:S(2)}) collective-permute-start(f32[512,512]{1,0:T(8,128)} %slice_bitcast_fusion), channel_id=1, source_target_pairs={{1,0},{2,1},{3,2},{4,3},{5,4},{6,5},{7,6},{8,7},{9,8},{10,9},{11,1... | collective-permute-start | bytes 3145736 | tf_op jit(solution)/shard_map/ppermute | solution.py:26
  30.3 113.8 %all-to-all-start = ((f32[128,8,128]{2,1,0:T(8,128)}), f32[128,8,128]{2,1,0:T(8,128)S(1)}, u32[]{:S(2)}, u32[]{:S(2)}) async-start(f32[128,8,128]{2,1,0:T(8,128)} %broadcast_in_dim.24), calls=%async_computation | async-start | bytes 1048576 | tf_op jit(solution)/shard_map/all_to_all | solution.py:40
  133.7 27.7 %collective-permute-start.4 = (f32[512,512]{1,0:T(8,128)}, f32[512,512]{1,0:T(8,128)S(1)}, u32[]{:S(2)}, u32[]{:S(2)}) collective-permute-start(f32[512,512]{1,0:T(8,128)} %get-tuple-element.74), channel_id=1, source_target_pairs={{1,0},{2,1},{3,2},{4,3},{5,4},{6,5},{7,6},{8,7},{9,8},{10,9},{11,1... | collective-permute-start | bytes 3145736 | tf_op jit(solution)/shard_map/ppermute | solution.py:26
  136.3 25.1 %collective-permute-start.5 = (f32[512,512]{1,0:T(8,128)}, f32[512,512]{1,0:T(8,128)S(1)}, u32[]{:S(2)}, u32[]{:S(2)}) collective-permute-start(f32[512,512]{1,0:T(8,128)} %get-tuple-element.75), channel_id=1, source_target_pairs={{1,0},{2,1},{3,2},{4,3},{5,4},{6,5},{7,6},{8,7},{9,8},{10,9},{11,1... | collective-permute-start | bytes 3145736 | tf_op jit(solution)/shard_map/ppermute | solution.py:26
  138.3 23.2 %collective-permute-start.6 = (f32[512,512]{1,0:T(8,128)}, f32[512,512]{1,0:T(8,128)}, u32[]{:S(2)}, u32[]{:S(2)}) collective-permute-start(f32[512,512]{1,0:T(8,128)} %get-tuple-element.76), channel_id=1, source_target_pairs={{0,1},{1,2},{2,3},{3,4},{4,5},{5,6},{6,7},{7,8},{8,9},{9,10},{10,1... | collective-permute-start | bytes 3145736 | tf_op jit(solution)/shard_map/ppermute | solution.py:21
  141.9 23.3 %collective-permute-start.7 = (f32[512,512]{1,0:T(8,128)}, f32[512,512]{1,0:T(8,128)}, u32[]{:S(2)}, u32[]{:S(2)}) collective-permute-start(f32[512,512]{1,0:T(8,128)} %get-tuple-element.77), channel_id=1, source_target_pairs={{0,1},{1,2},{2,3},{3,4},{4,5},{5,6},{6,7},{7,8},{8,9},{9,10},{10,1... | collective-permute-start | bytes 3145736 | tf_op jit(solution)/shard_map/ppermute | solution.py:21
  182.3 44.8 %collective-permute-start.8 = (f32[512,512]{1,0:T(8,128)}, f32[512,512]{1,0:T(8,128)S(1)}, u32[]{:S(2)}, u32[]{:S(2)}) collective-permute-start(f32[512,512]{1,0:T(8,128)} %get-tuple-element.85), channel_id=1, source_target_pairs={{1,0},{2,1},{3,2},{4,3},{5,4},{6,5},{7,6},{8,7},{9,8},{10,9},{11,1... | collective-permute-start | bytes 3145736 | tf_op jit(solution)/shard_map/ppermute | solution.py:26
  184.2 42.9 %collective-permute-start.9 = (f32[512,512]{1,0:T(8,128)}, f32[512,512]{1,0:T(8,128)S(1)}, u32[]{:S(2)}, u32[]{:S(2)}) collective-permute-start(f32[512,512]{1,0:T(8,128)} %get-tuple-element.86), channel_id=1, source_target_pairs={{1,0},{2,1},{3,2},{4,3},{5,4},{6,5},{7,6},{8,7},{9,8},{10,9},{11,1... | collective-permute-start | bytes 3145736 | tf_op jit(solution)/shard_map/ppermute | solution.py:26
  186.2 41.0 %collective-permute-start.10 = (f32[512,512]{1,0:T(8,128)}, f32[512,512]{1,0:T(8,128)S(1)}, u32[]{:S(2)}, u32[]{:S(2)}) collective-permute-start(f32[512,512]{1,0:T(8,128)} %get-tuple-element.87), channel_id=1, source_target_pairs={{0,1},{1,2},{2,3},{3,4},{4,5},{5,6},{6,7},{7,8},{8,9},{9,10},{10,1... | collective-permute-start | bytes 3145736 | tf_op jit(solution)/shard_map/ppermute | solution.py:21
  190.6 36.6 %collective-permute-start.11 = (f32[512,512]{1,0:T(8,128)}, f32[512,512]{1,0:T(8,128)}, u32[]{:S(2)}, u32[]{:S(2)}) collective-permute-start(f32[512,512]{1,0:T(8,128)} %get-tuple-element.88), channel_id=1, source_target_pairs={{0,1},{1,2},{2,3},{3,4},{4,5},{5,6},{6,7},{7,8},{8,9},{9,10},{10,1... | collective-permute-start | bytes 3145736 | tf_op jit(solution)/shard_map/ppermute | solution.py:21
  193.7 31.2 %all-to-all-start.1 = ((f32[32,8,128]{2,1,0:T(8,128)}), f32[32,8,128]{2,1,0:T(8,128)S(1)}, u32[]{:S(2)}, u32[]{:S(2)}) async-start(f32[32,8,128]{2,1,0:T(8,128)} %broadcast_in_dim.25), calls=%async_computation.1 | async-start | bytes 262144 | tf_op jit(solution)/shard_map/all_to_all | solution.py:40
  246.6 24.7 %collective-permute-start.12 = (f32[512,512]{1,0:T(8,128)}, f32[512,512]{1,0:T(8,128)S(1)}, u32[]{:S(2)}, u32[]{:S(2)}) collective-permute-start(f32[512,512]{1,0:T(8,128)} %get-tuple-element.94), channel_id=1, source_target_pairs={{1,0},{2,1},{3,2},{4,3},{5,4},{6,5},{7,6},{8,7},{9,8},{10,9},{11,1... | collective-permute-start | bytes 3145736 | tf_op jit(solution)/shard_map/ppermute | solution.py:26
  248.9 25.2 %collective-permute-start.13 = (f32[512,512]{1,0:T(8,128)}, f32[512,512]{1,0:T(8,128)S(1)}, u32[]{:S(2)}, u32[]{:S(2)}) collective-permute-start(f32[512,512]{1,0:T(8,128)} %get-tuple-element.95), channel_id=1, source_target_pairs={{1,0},{2,1},{3,2},{4,3},{5,4},{6,5},{7,6},{8,7},{9,8},{10,9},{11,1... | collective-permute-start | bytes 3145736 | tf_op jit(solution)/shard_map/ppermute | solution.py:26
  250.9 23.3 %collective-permute-start.14 = (f32[512,512]{1,0:T(8,128)}, f32[512,512]{1,0:T(8,128)S(1)}, u32[]{:S(2)}, u32[]{:S(2)}) collective-permute-start(f32[512,512]{1,0:T(8,128)} %get-tuple-element.96), channel_id=1, source_target_pairs={{0,1},{1,2},{2,3},{3,4},{4,5},{5,6},{6,7},{7,8},{8,9},{9,10},{10,1... | collective-permute-start | bytes 3145736 | tf_op jit(solution)/shard_map/ppermute | solution.py:21
  254.5 23.3 %collective-permute-start.15 = (f32[512,512]{1,0:T(8,128)}, f32[512,512]{1,0:T(8,128)}, u32[]{:S(2)}, u32[]{:S(2)}) collective-permute-start(f32[512,512]{1,0:T(8,128)} %get-tuple-element.97), channel_id=1, source_target_pairs={{0,1},{1,2},{2,3},{3,4},{4,5},{5,6},{6,7},{7,8},{8,9},{9,10},{10,1... | collective-permute-start | bytes 3145736 | tf_op jit(solution)/shard_map/ppermute | solution.py:21
  291.0 20.0 %collective-permute-start.16 = (f32[512,128]{1,0:T(8,128)}, f32[512,128]{1,0:T(8,128)S(1)}, u32[]{:S(2)}, u32[]{:S(2)}) collective-permute-start(f32[512,128]{1,0:T(8,128)} %get-tuple-element.103), channel_id=1, source_target_pairs={{1,0},{2,1},{3,2},{4,3},{5,4},{6,5},{7,6},{8,7},{9,8},{10,9},{11,1... | collective-permute-start | bytes 786440 | tf_op jit(solution)/shard_map/ppermute | solution.py:26
  317.8 21.1 %all-to-all-start.2 = ((f32[128,8,128]{2,1,0:T(8,128)}), f32[128,8,128]{2,1,0:T(8,128)S(1)}, u32[]{:S(2)}, u32[]{:S(2)}) async-start(f32[128,8,128]{2,1,0:T(8,128)} %broadcast_in_dim.26), calls=%async_computation.2 | async-start | bytes 1048576 | tf_op jit(solution)/shard_map/all_to_all | solution.py:40
  482.9 28.5 %collective-permute-start.22 = (f32[512,512]{1,0:T(8,128)}, f32[512,512]{1,0:T(8,128)S(1)}, u32[]{:S(2)}, u32[]{:S(2)}) collective-permute-start(f32[512,512]{1,0:T(8,128)} %get-tuple-element.117), channel_id=1, source_target_pairs={{1,0},{2,1},{3,2},{4,3},{5,4},{6,5},{7,6},{8,7},{9,8},{10,9},{11,1... | collective-permute-start | bytes 3145736 | tf_op jit(solution)/shard_map/ppermute | solution.py:26
  484.9 26.6 %collective-permute-start.23 = (f32[512,512]{1,0:T(8,128)}, f32[512,512]{1,0:T(8,128)S(1)}, u32[]{:S(2)}, u32[]{:S(2)}) collective-permute-start(f32[512,512]{1,0:T(8,128)} %get-tuple-element.114), channel_id=1, source_target_pairs={{0,1},{1,2},{2,3},{3,4},{4,5},{5,6},{6,7},{7,8},{8,9},{9,10},{10,1... | collective-permute-start | bytes 3145736 | tf_op jit(solution)/shard_map/ppermute | solution.py:21
  570.2 21.4 %all-to-all-start.4 = ((f32[128,8,128]{2,1,0:T(8,128)}), f32[128,8,128]{2,1,0:T(8,128)S(1)}, u32[]{:S(2)}, u32[]{:S(2)}) async-start(f32[128,8,128]{2,1,0:T(8,128)} %broadcast_in_dim.32), calls=%async_computation.4 | async-start | bytes 1048576 | tf_op jit(solution)/shard_map/all_to_all | solution.py:40
  (40 other events, 270.6 us)
Sparse Core Ops, SparseCore 0:
  10.2 48.0 all-gather.5
  60.0 57.6 all-gather.3

commit v6 on v5

--- a/solution.py
+++ b/solution.py
@@ -52,8 +52,9 @@
 def add_parts(spins, part_refs, rows=slice(None)):
     local = part_refs[0]
     if spins == 1:
-        return [local[0, rows, :] + part_refs[1][rows, :] + part_refs[2][rows, :]]
-    down0, down1, up1, up2 = (ref[rows, :] for ref in part_refs[1:])
+        return [local[0, rows, :] + part_refs[1][0, rows, :] + part_refs[2][0, rows, :]]
+    down0, down1 = (part_refs[1][k, rows, :] for k in range(2))
+    up1, up2 = (part_refs[2][k, rows, :] for k in range(2))
     return [local[0, rows, :] + up1, local[1, rows, :] + (up2 + down0), local[2, rows, :] + down1]
 
 
@@ -232,8 +233,8 @@
 
 
 def site_send_kernel(high, low, four, up, down, *refs):
-    d0, d1, u1, u2, zh, zl = refs[:6]
-    xh_v, xl_v, four_v, up_v, down_v, zh_v, zl_v, d_v, u_v, sems = refs[6:]
+    d_out, u_out, zh, zl = refs[:4]
+    xh_v, xl_v, four_v, up_v, down_v, zh_v, zl_v, d_v, u_v, sems = refs[4:]
     fetch = Fetch(sems)
     for s in (1, 0, 2):
         start_state(fetch, s, high, low, xh_v, xl_v)
@@ -253,11 +254,11 @@
         if s < 2:
             fetch.wait("down")
             d_v[s] = product((down_v[0], down_v[1]), pair)
-            outs.start(("d", s), d_v.at[s], (d0, d1)[s])
+            outs.start(("d", s), d_v.at[s], d_out.at[s])
         if s > 0:
             fetch.wait("up")
             u_v[s - 1] = product((up_v[0], up_v[1]), pair)
-            outs.start(("u", s), u_v.at[s - 1], (u1, u2)[s - 1])
+            outs.start(("u", s), u_v.at[s - 1], u_out.at[s - 1])
     outs.wait_all()
 
 
@@ -309,12 +310,12 @@
     moved = split(product(x, (bond_v[1, 0], bond_v[1, 1])))
     fetch.wait("down")
     d_v[...] = product((down_v[0], down_v[1]), moved)
-    outs.start("d", d_v, d_out)
+    outs.start("d", d_v, d_out.at[0])
     fetch.wait(("p", 2))
     moved = split(product(x, (bond_v[0, 0], bond_v[0, 1])))
     fetch.wait("up")
     u_v[...] = product((up_v[0], up_v[1]), moved)
-    outs.start("u", u_v, u_out)
+    outs.start("u", u_v, u_out.at[0])
     outs.wait_all()
 
 
@@ -342,43 +343,122 @@
     outs.wait_all()
 
 
-def site_send_quarter(place_ref, high, low, four_ref, up_ref, down_ref, d0, d1, u1, u2, zh, zl):
-    z = [product(columns_of(high, low, s), pair_of(four_ref, s)) for s in range(3)]
+def rough(left, right):
+    return jnp.dot(left, right, preferred_element_type=jnp.float32)
+
+
+def site_send_quarter(place_ref, high, four_ref, up_ref, down_ref, d_ref, u_ref, z_ref):
+    size = high.shape[0]
     for s in range(3):
-        zh[s], zl[s] = split(z[s])
-    d0[...], d1[...] = cut_columns(product((down_ref[0], down_ref[1]), split(join(z[0], z[1]))), 2)
-    u1[...], u2[...] = cut_columns(product((up_ref[0], up_ref[1]), split(join(z[1], z[2]))), 2)
-
-
-def site_local_quarter(place_ref, high, low, mix_ref, stack_ref, zh, zl, out_ref):
+        z_ref[s] = rough(high[:, s * size : (s + 1) * size], four_ref[s, 0]).astype(BF16)
+    d_ref[0], d_ref[1] = cut_columns(rough(down_ref[0], join(z_ref[0], z_ref[1])), 2)
+    u_ref[0], u_ref[1] = cut_columns(rough(up_ref[0], join(z_ref[1], z_ref[2])), 2)
+
+
+def site_local_quarter(place_ref, high, mix_ref, stack_ref, z_ref, out_ref):
+    size = high.shape[0]
+
     def merged(s, *matrices):
-        right = (join(*[mix_ref[m, part] for m in matrices]) for part in range(2))
-        return cut_columns(product(columns_of(high, low, s), tuple(right)), len(matrices))
+        right = join(*[mix_ref[m, 0] for m in matrices])
+        return cut_columns(rough(high[:, s * size : (s + 1) * size], right), len(matrices))
 
     p0, p1 = merged(0, 0, 3)
     more0, more1, p2 = merged(1, 1, 2, 6)
     last2, last1 = merged(2, 5, 4)
-    mixed = split(join(p0 + more0, p1 + more1 + last1, p2 + last2))
-    y = cut_columns(product(pair_of(stack_ref, 0), mixed), 3)
+    mixed = join(p0 + more0, p1 + more1 + last1, p2 + last2).astype(BF16)
+    y = cut_columns(rough(stack_ref[0, 0], mixed), 3)
     for s in range(3):
-        out_ref[s] = y[s] + product(pair_of(stack_ref, 1 + s), (zh[s], zl[s]))
-
-
-def bond_send_quarter(place_ref, high, low, p_ref, up_ref, down_ref, d_ref, u_ref):
-    right = (join(p_ref[3, part], p_ref[2, part]) for part in range(2))
-    down, up = cut_columns(product((high[...], low[...]), tuple(right)), 2)
-    d_ref[...] = product((down_ref[0], down_ref[1]), split(down))
-    u_ref[...] = product((up_ref[0], up_ref[1]), split(up))
-
-
-def bond_local_quarter(place_ref, high, low, p_ref, stack_ref, out_ref):
-    right = (join(*[p_ref[a, part] for a, _ in BOND_TERMS]) for part in range(2))
-    moved = cut_columns(product((high[...], low[...]), tuple(right)), 3)
+        out_ref[s] = y[s] + rough(stack_ref[1 + s, 0], z_ref[s])
+
+
+def bond_send_quarter(place_ref, high, p_ref, up_ref, down_ref, d_ref, u_ref):
+    right = join(p_ref[3, 0], p_ref[2, 0])
+    down, up = cut_columns(rough(high[...], right).astype(BF16), 2)
+    d_ref[0] = rough(down_ref[0], down)
+    u_ref[0] = rough(up_ref[0], up)
+
+
+def bond_local_quarter(place_ref, high, p_ref, stack_ref, out_ref):
+    right = join(*[p_ref[a, 0] for a, _ in BOND_TERMS])
+    moved = cut_columns(rough(high[...], right).astype(BF16), 3)
     total = None
     for value, (_, matrix) in zip(moved, BOND_TERMS):
-        value = product(pair_of(stack_ref, matrix), split(value))
+        value = rough(stack_ref[matrix, 0], value)
         total = value if total is None else total + value
     out_ref[0] = total
+
+
+def site_first_kernel(high, low, four_ref, mix_ref, zh, zl, ph, pl_out):
+    x = [columns_of(high, low, s) for s in range(3)]
+    for s in range(3):
+        zh[s], zl[s] = split(product(x[s], pair_of(four_ref, s)))
+        total = None
+        for source, matrix in TERMS[s]:
+            value = product(x[source], pair_of(mix_ref, matrix))
+            total = value if total is None else total + value
+        ph[s], pl_out[s] = split(total)
+
+
+def first_products(pair, four, mix):
+    size = four.shape[-1]
+    width = size // 2
+    thirds = pl.BlockSpec((3, size, width), lambda i: (0, 0, i))
+    state = pl.BlockSpec((size, 3 * size), lambda i: (0, 0))
+    return pl.pallas_call(
+        site_first_kernel,
+        grid=(2,),
+        in_specs=[state, state]
+        + [pl.BlockSpec((m.shape[0], 2, size, width), lambda i: (0, 0, 0, i)) for m in (four, mix)],
+        out_specs=[thirds] * 4,
+        out_shape=[jax.ShapeDtypeStruct((3, size, size), BF16)] * 4,
+        compiler_params=params(),
+        cost_estimate=pl.CostEstimate(
+            flops=10 * UNIT, bytes_accessed=16 * 2**20, transcendentals=0
+        ),
+    )(*pair, four, mix)
+
+
+def site_first_send(zh, zl, up, down, d_out, u_out, zh_v, zl_v, up_v, down_v, d_v, u_v, sems):
+    fetch = Fetch(sems)
+    for s in (1, 0, 2):
+        fetch.start(("zh", s), zh.at[s], zh_v.at[s])
+        fetch.start(("zl", s), zl.at[s], zl_v.at[s])
+        if s == 1:
+            fetch.start("down", down, down_v)
+            fetch.start("up", up, up_v)
+    outs = Fetch(sems)
+    outs.used = fetch.used
+    for s in (1, 0, 2):
+        fetch.wait(("zh", s), ("zl", s), "down", "up")
+        pair = (zh_v[s], zl_v[s])
+        if s < 2:
+            d_v[s] = product((down_v[0], down_v[1]), pair)
+            outs.start(("d", s), d_v.at[s], d_out.at[s])
+        if s > 0:
+            u_v[s - 1] = product((up_v[0], up_v[1]), pair)
+            outs.start(("u", s), u_v.at[s - 1], u_out.at[s - 1])
+    outs.wait_all()
+
+
+def site_first_local(ph, pl_in, stack, zh, zl, out, ph_v, pl_v, stack_v, zh_v, zl_v, out_v, sems):
+    fetch = Fetch(sems)
+    for s in range(3):
+        if s == 0:
+            fetch.start(("stack", 0), stack.at[0], stack_v.at[0])
+        fetch.start(("ph", s), ph.at[s], ph_v.at[s])
+        fetch.start(("pl", s), pl_in.at[s], pl_v.at[s])
+        fetch.start(("stack", 1 + s), stack.at[1 + s], stack_v.at[1 + s])
+        fetch.start(("zh", s), zh.at[s], zh_v.at[s])
+        fetch.start(("zl", s), zl.at[s], zl_v.at[s])
+    outs = Fetch(sems)
+    outs.used = fetch.used
+    for s in range(3):
+        fetch.wait(("stack", 0), ("ph", s), ("pl", s))
+        y = product((stack_v[0, 0], stack_v[0, 1]), (ph_v[s], pl_v[s]))
+        fetch.wait(("stack", 1 + s), ("zh", s), ("zl", s))
+        out_v[s] = y + product((stack_v[1 + s, 0], stack_v[1 + s, 1]), (zh_v[s], zl_v[s]))
+        outs.start(("out", s), out_v.at[s], out.at[s])
+    outs.wait_all()
 
 
 UNIT = 6 * 512**3
@@ -431,9 +511,10 @@
     return pl.BlockSpec((step, spins * size), lambda i: (i, 0))
 
 
-def part_specs(spins, step, size, count):
-    row = pl.BlockSpec((step, size), lambda i: (i, 0))
-    return [pl.BlockSpec((spins, step, size), lambda i: (0, i, 0))] + [row] * (count - 1)
+def part_specs(step, parts):
+    return [
+        pl.BlockSpec((part.shape[0], step, part.shape[2]), lambda i: (0, i, 0)) for part in parts
+    ]
 
 
 def state_shapes(spins, size):
@@ -469,7 +550,7 @@
     *y, sums = pl.pallas_call(
         functools.partial(first_combine_kernel, spins),
         grid=(size // step,),
-        in_specs=[scalar_spec(), state] + part_specs(spins, step, size, len(parts)),
+        in_specs=[scalar_spec(), state] + part_specs(step, parts),
         out_specs=[state] * 3 + [scalar_spec()],
         out_shape=state_shapes(spins, size) + [SCALARS],
         compiler_params=params(),
@@ -517,7 +598,7 @@
         grid=(size // step,),
         in_specs=[scalar_spec()]
         + [state] * (2 if second else 1)
-        + part_specs(spins, step, size, len(parts)),
+        + part_specs(step, parts),
         out_specs=[state] * 3,
         out_shape=state_shapes(spins, size),
         compiler_params=params(),
@@ -555,8 +636,7 @@
         pl.BlockSpec((size, width), functools.partial(lambda s, i, p: (0, s * per + p[0]), s))
         for s in range(spins)
     ]
-    whole = [pl.BlockSpec((spins, size, width), lambda i, p: (0, 0, 0))]
-    whole += [pl.BlockSpec((size, width), lambda i, p: (0, 0))] * (len(parts) - 1)
+    whole = [pl.BlockSpec(part.shape, lambda i, p: (0, 0, 0)) for part in parts]
     flat = [state for state in states for s in range(spins)]
     return pl.pallas_call(
         functools.partial(gram_kernel, spins),
@@ -684,14 +764,14 @@
 
 
 def evolve(place, x, nu, apply_op, step_size, spins):
-    parts, _ = apply_op(split_state(x), None, False)
+    parts, _ = apply_op(split_state(x), None, "first")
     (y, *y_split), sums = first_combine(x, nu, parts, spins)
-    parts, totals = apply_op(y_split, sums, False)
+    parts, totals = apply_op(y_split, sums, "middle")
     scales = shift_rows(nu, totals)
     w2, *w2_split = combine(scales, y, x, parts, spins)
-    parts, _ = apply_op(w2_split, None, False)
+    parts, _ = apply_op(w2_split, None, "middle")
     w3, *w3_split = combine(scales, w2, None, parts, spins)
-    parts, _ = apply_op(w3_split, None, True)
+    parts, _ = apply_op(w3_split, None, "last")
     states = [x, y, w2, w3]
     row = gram_row(place, scales, states, parts, spins)
     weights = basis_weights(scales, exchange(row, ("col", "sec")), step_size)
@@ -731,35 +811,55 @@
     pairs = ((2,) + matrix, BF16)
     f32 = jnp.float32
 
-    def apply_site(pair, sums, quarter):
-        if quarter:
-            d0, d1, u1, u2, zh, zl = quarter_call(
+    doubles = ((2,) + matrix, f32)
+
+    def apply_site(pair, sums, stage):
+        if stage == "last":
+            d, u, z = quarter_call(
                 site_send_quarter,
                 place,
-                [(True, pair[0]), (True, pair[1]), (False, four), (True, up), (True, down)],
-                [((), f32)] * 4 + [((3,), BF16)] * 2,
+                [(True, pair[0]), (False, four), (True, up), (True, down)],
+                [((2,), f32)] * 2 + [((3,), BF16)],
                 7,
             )
+        elif stage == "first":
+            zh, zl, ph, pl_part = first_products(pair, four, mix)
+            d, u = full_call(
+                site_first_send,
+                [zh, zl, up, down],
+                [doubles] * 2,
+                [thirds, thirds, pairs, pairs, doubles, doubles],
+                16,
+                4,
+            )
         else:
-            d0, d1, u1, u2, zh, zl = full_call(
+            d, u, zh, zl = full_call(
                 site_send_kernel,
                 [pair[0], pair[1], four, up, down],
-                [(matrix, f32)] * 4 + [thirds] * 2,
+                [doubles] * 2 + [thirds] * 2,
                 [thirds, thirds, ((3, 2) + matrix, BF16), pairs, pairs, thirds, thirds]
-                + [((2,) + matrix, f32)] * 2,
+                + [doubles] * 2,
                 24,
                 7,
             )
-        d1, u1 = to_previous(d1), to_next(u1)
-        d0, u2 = to_previous(d0), to_next(u2)
-        totals = send_sums(sums, zh)
-        if quarter:
+        totals = send_sums(sums, u)
+        d, u = to_previous(d), to_next(u)
+        if stage == "last":
             (local,) = quarter_call(
                 site_local_quarter,
                 place,
-                [(True, pair[0]), (True, pair[1]), (False, mix), (True, stack), (True, zh), (True, zl)],
+                [(True, pair[0]), (False, mix), (True, stack), (True, z)],
                 [((3,), f32)],
                 13,
+            )
+        elif stage == "first":
+            (local,) = full_call(
+                site_first_local,
+                [ph, pl_part, stack, zh, zl],
+                [((3,) + matrix, f32)],
+                [thirds, thirds, ((4, 2) + matrix, BF16), thirds, thirds, ((3,) + matrix, f32)],
+                24,
+                6,
             )
         else:
             (local,) = full_call(
@@ -771,7 +871,7 @@
                 32,
                 13,
             )
-        return [local, d0, d1, u1, u2], totals
+        return [local, d, u], totals
 
     states, weights = evolve(place, site_full, site_nu, apply_site, -TIME_STEP, 3)
     evolved = weighted(place, weights, states, None)
@@ -786,31 +886,31 @@
 
     single = ((1,) + matrix, BF16)
 
-    def apply_bond(pair, sums, quarter):
-        if quarter:
+    def apply_bond(pair, sums, stage):
+        if stage == "last":
             down_term, up_term = quarter_call(
                 bond_send_quarter,
                 place,
-                [(True, pair[0]), (True, pair[1]), (False, bond), (True, up), (True, down)],
-                [((), f32)] * 2,
+                [(True, pair[0]), (False, bond), (True, up), (True, down)],
+                [((1,), f32)] * 2,
                 4,
             )
         else:
             down_term, up_term = full_call(
                 bond_send_kernel,
                 [pair[0], pair[1], bond, up, down],
-                [(matrix, f32)] * 2,
+                [((1,) + matrix, f32)] * 2,
                 [single, single, ((2, 2) + matrix, BF16), pairs, pairs] + [(matrix, f32)] * 2,
                 8,
                 4,
             )
         totals = send_sums(sums, up_term)
         down_term, up_term = to_previous(down_term), to_next(up_term)
-        if quarter:
+        if stage == "last":
             (local,) = quarter_call(
                 bond_local_quarter,
                 place,
-                [(True, pair[0]), (True, pair[1]), (False, bond), (True, stack)],
+                [(True, pair[0]), (False, bond), (True, stack)],
                 [((1,), f32)],
                 6,
             )

time: 614 us -> 608 us (level)
  blocking collectives: 0 us -> 35.8 us
  starting transfers between devices: 122 us -> 86.3 us
    all_to_all x0 -> x1, blocking collectives: none -> 35.8 us  [exchange(): return lax.all_to_all(sent, axis, 0, 0)]
    all_to_all x5 -> x4, starting transfers between devices: 45.3 us -> 28.5 us  [exchange(): return lax.all_to_all(sent, axis, 0, 0)]
    all_gather x2, waiting for transfers between devices: 51.3 us -> 35.2 us  [gather_col(): return lax.all_gather(block, 'col', axis=axis, tiled=True)]
    pallas_call x0 -> x1, Pallas kernels: none -> 14 us  [first_products(): pl.pallas_call(site_first_kernel, grid=(2,), in_specs=[state, state] + [p...]
    ppermute x14 -> x10, starting transfers between devices: 46.2 us -> 34.8 us  [to_next(): return lax.ppermute(block, 'sec', [(i, i + 1) for i in range(count - 1)])]
    pallas_call x12, Pallas kernels: 117 us -> 107 us  [full_call(): pl.pallas_call(kernel, in_specs=[anywhere] * len(operands), out_specs=[an...]
    pallas_call x4, Pallas kernels: 27.6 us -> 19 us  [quarter_call(): pl.pallas_call(kernel, grid_spec=pltpu.PrefetchScalarGridSpec(num_scalar_...]
    ppermute x14 -> x10, waiting for transfers between devices: 9.99 us -> 18.2 us  [to_next(): return lax.ppermute(block, 'sec', [(i, i + 1) for i in range(count - 1)])]
  transfers between devices with their start and end apart: 35 -> 26, of which waited for: 13 -> 15; matrix products, arithmetic and copies ran while one was open for 2% -> 2% of each run, Pallas kernels for 22% -> 20%
where the time goes in v6:
time: 608 us; the launch traced here: 598 us
  Pallas kernels  238 us (39%)
  waiting for transfers between devices  98.8 us (16%)
  starting transfers between devices  86.3 us (14%)
  other arithmetic  84.5 us (14%)
  blocking collectives  35.8 us (6%)
  local copies, waits for them, and re-layouts  26.5 us (4%)
  between operations  17.9 us (3%)
  matrix products  10.2 us (2%)
    pallas_call x12, Pallas kernels, full_call(): pl.pallas_call(kernel, in_specs=[anywhere] * len(operands), out_specs=[an...  107 us
    another operation x14, other arithmetic, body(): factor = jnp.linalg.cholesky(gram[None])[0]  78.6 us
    all_to_all x1, blocking collectives, exchange(): return lax.all_to_all(sent, axis, 0, 0)  35.8 us
    all_gather x2, waiting for transfers between devices, gather_col(): return lax.all_gather(block, 'col', axis=axis, tiled=True)  35.2 us
    ppermute x10, starting transfers between devices, to_next(): return lax.ppermute(block, 'sec', [(i, i + 1) for i in range(count - 1)])  34.8 us
    all_to_all x4, starting transfers between devices, exchange(): return lax.all_to_all(sent, axis, 0, 0)  28.5 us
    all_to_all x4, waiting for transfers between devices, exchange(): return lax.all_to_all(sent, axis, 0, 0)  24.5 us
    pallas_call x4, Pallas kernels, combine(): pl.pallas_call(functools.partial(combine_kernel, second, spins), grid=(si...  24.4 us
  transfers between devices with their start and end apart: 26, of which 15 were waited for; matrix products, arithmetic and copies ran while one was open for 2% of the time, Pallas kernels for 20%

profile of v6, /device:TPU:1, one launch (start us, length us, event | category | flops | bytes accessed | tf_op | source)
XLA Modules:
  0.0 598.3 jit_solution(17581807010594766318)
XLA Ops:
  29.8 11.2 %collective-permute-done.1.bfour_ref = f32[512,512]{1,0:T(8,128)S(1)} collective-permute-done((f32[512,512]{1,0:T(8,128)}, f32[512,512]{1,0:T(8,128)S(1)}, u32[]{:S(2)}, u32[]{:S(2)}) %collective-permute-start.1) | collective-permute-done | bytes 1048608 | tf_op jit(solution)/shard_map/ppermute | solution.py:21
  41.0 8.7 %collective-permute-done.3.afour_ref = f32[512,512]{1,0:T(8,128)} collective-permute-done((f32[512,512]{1,0:T(8,128)}, f32[512,512]{1,0:T(8,128)}, u32[]{:S(2)}, u32[]{:S(2)}) %collective-permute-start.3) | collective-permute-done | bytes 1048608 | tf_op jit(solution)/shard_map/ppermute | solution.py:26
  49.7 9.0 %shard_map.71 = (bf16[3,2,512,512]{3,2,1,0:T(8,128)(2,1)}, bf16[7,2,512,512]{3,2,1,0:T(8,128)(2,1)}) custom-call(s32[2]{0:T(128)} %add_convert_fusion.flag_ref, f32[5,512,512]{2,1,0:T(8,128)} %bitcast.110, f32[512,512]{1,0:T(8,128)} %copy-done.6, f32[512,512]{1,0:T(8,128)} %copy-done.7, f32[512,512]{1,0:T(8,128)} %collective-permute-done.2.asum_ref, ...), custom_call_target="tpu_custom_call" | custom-call | tf_op jit(solution)/shard_map/pallas_call | solution.py:158
  63.0 14.0 %shard_map.72 = (bf16[3,512,512]{2,1,0:T(8,128)(2,1)}, bf16[3,512,512]{2,1,0:T(8,128)(2,1)}, bf16[3,512,512]{2,1,0:T(8,128)(2,1)}, bf16[3,512,512]{2,1,0:T(8,128)(2,1)}) custom-call(bf16[512,1536]{1,0:T(8,128)(2,1)} %get-tuple-element.56.high, bf16[512,1536]{1,0:T(8,128)(2,1)} %get-tuple-element.57.low, ...), custom_call_target="tpu_custom_call" | custom-call | flops 8053063680 | bytes 16777216 | tf_op jit(solution)/shard_map/pallas_call | solution.py:407
  77.0 35.2 %all-gather.4.cloned.1.call-done.block_ref = f32[4,5,512,128]{3,2,1,0:T(8,128)} async-done(((f32[1,5,512,128]{3,2,1,0:T(8,128)}), f32[4,5,512,128]{3,2,1,0:T(8,128)}) %all-gather.4.cloned.1.call-update) | async-done | bytes 5242896 | tf_op jit(solution)/shard_map/all_gather | solution.py:30
  133.9 35.8 %all_to_all.25.parts_ref = f32[128,8,128]{2,1,0:T(8,128)} all-to-all(f32[128,8,128]{2,1,0:T(8,128)S(1)} %broadcast_in_dim.24), channel_id=1, replica_groups=mesh['col'=4,'sec'=32] {'col','sec'}, dimensions={0} | all-to-all | bytes 1048576 | tf_op jit(solution)/shard_map/all_to_all | solution.py:40
  171.5 8.2 %shard_map.74.refs_0_ = f32[3,512,512]{2,1,0:T(8,128)} custom-call(bf16[3,512,512]{2,1,0:T(8,128)(2,1)} %get-tuple-element.60.ph, bf16[3,512,512]{2,1,0:T(8,128)(2,1)} %get-tuple-element.61.pl_in, bf16[5,2,512,512]{3,2,1,0:T(8,128)(2,1)} %get-tuple-element.62.stack.stack_ref, bf16[3,512,512]{2,1,0:T(8,128)(2,1)} %get-tuple-element.63.zh, ...), custom_call_target="tpu_custom_call" | custom-call | flops 4831838208 | bytes 16777216 | tf_op jit(solution)/shard_map/pallas_call | solution.py:496
  190.2 9.4 %shard_map.77 = (f32[2,512,512]{2,1,0:T(8,128)}, f32[2,512,512]{2,1,0:T(8,128)}, bf16[3,512,512]{2,1,0:T(8,128)(2,1)}, bf16[3,512,512]{2,1,0:T(8,128)(2,1)}) custom-call(bf16[512,1536]{1,0:T(8,128)(2,1)} %get-tuple-element.70.high, bf16[512,1536]{1,0:T(8,128)(2,1)} %get-tuple-element.71.low, bf16[3,2,512,512]{3,2,1,0:T(8,128)(2,1)} %get-tuple-element.58.four_ref.four, ...), custom_call_target="tpu_custom_call" | custom-call | flops 5637144576 | bytes 16777216 | tf_op jit(solution)/shard_map/pallas_call | solution.py:496
  210.2 14.6 %shard_map.79.refs_1_ = f32[3,512,512]{2,1,0:T(8,128)} custom-call(bf16[512,1536]{1,0:T(8,128)(2,1)} %get-tuple-element.70.high, bf16[512,1536]{1,0:T(8,128)(2,1)} %get-tuple-element.71.low, bf16[7,2,512,512]{3,2,1,0:T(8,128)(2,1)} %get-tuple-element.59.mix_ref.mix, bf16[5,2,512,512]{3,2,1,0:T(8,128)(2,1)} %get-tuple-element.62.stack.stack_ref, ...), custom_call_target="tpu_custom_call" | custom-call | flops 10468982784 | bytes 16777216 | tf_op jit(solution)/shard_map/pallas_call | solution.py:496
  236.0 8.4 %shard_map.80 = (f32[512,1536]{1,0:T(8,128)}, bf16[512,1536]{1,0:T(8,128)(2,1)}, bf16[512,1536]{1,0:T(8,128)(2,1)}) custom-call(f32[8,128]{1,0:T(8,128)} %shard_map.78.scale_ref, f32[512,1536]{1,0:T(8,128)} %get-tuple-element.74.w_ref.refs_3_.refs_4_.refs_5_.refs_1_, f32[512,1536]{1,0:T(8,128)} %bitcast.104, f32[3,512,512]{2,1,0:T(8,128)} %shard_map.79.refs_1_, ...), custom_call_target="tpu_custom_call" | custom-call | tf_op jit(solution)/shard_map/pallas_call | solution.py:596
  244.4 9.4 %shard_map.81 = (f32[2,512,512]{2,1,0:T(8,128)}, f32[2,512,512]{2,1,0:T(8,128)}, bf16[3,512,512]{2,1,0:T(8,128)(2,1)}, bf16[3,512,512]{2,1,0:T(8,128)(2,1)}) custom-call(bf16[512,1536]{1,0:T(8,128)(2,1)} %get-tuple-element.79.high, bf16[512,1536]{1,0:T(8,128)(2,1)} %get-tuple-element.80.low, bf16[3,2,512,512]{3,2,1,0:T(8,128)(2,1)} %get-tuple-element.58.four_ref.four, ...), custom_call_target="tpu_custom_call" | custom-call | flops 5637144576 | bytes 16777216 | tf_op jit(solution)/shard_map/pallas_call | solution.py:496
  259.6 14.6 %shard_map.82.refs_0_ = f32[3,512,512]{2,1,0:T(8,128)} custom-call(bf16[512,1536]{1,0:T(8,128)(2,1)} %get-tuple-element.79.high, bf16[512,1536]{1,0:T(8,128)(2,1)} %get-tuple-element.80.low, bf16[7,2,512,512]{3,2,1,0:T(8,128)(2,1)} %get-tuple-element.59.mix_ref.mix, bf16[5,2,512,512]{3,2,1,0:T(8,128)(2,1)} %get-tuple-element.62.stack.stack_ref, ...), custom_call_target="tpu_custom_call" | custom-call | flops 10468982784 | bytes 16777216 | tf_op jit(solution)/shard_map/pallas_call | solution.py:496
  313.4 8.6 %all-to-all-start.2 = ((f32[128,8,128]{2,1,0:T(8,128)}), f32[128,8,128]{2,1,0:T(8,128)S(1)}, u32[]{:S(2)}, u32[]{:S(2)}) async-start(f32[128,8,128]{2,1,0:T(8,128)} %broadcast_in_dim.26), calls=%async_computation.2 | async-start | bytes 1048576 | tf_op jit(solution)/shard_map/all_to_all | solution.py:40
  346.2 8.1 %convolution_add_fusion = f32[512,512]{0,1:T(8,128)S(1)} fusion(f32[512,1536]{1,0:T(8,128)} %shard_map.89, f32[512]{0:T(512)S(1)} %broadcast_subtract_fusion), kind=kOutput, calls=%fused_computation | convolution fusion | flops 4832624640 | bytes 4196352 | tf_op jit(solution)/shard_map/dot_general | solution.py:879
  354.9 11.7 %custom-call.31 = f32[1,128,128]{2,1,0:T(8,128)S(1)} custom-call(f32[1,128,128]{2,1,0:T(8,128)S(1)} %cholesky.267), custom_call_target="Cholesky" | custom-call | tf_op jit(solution)/shard_map/jit(cholesky)/cholesky | solution.py:882
  366.8 9.8 %custom-call.32 = f32[1,1,128,128]{2,3,1,0:T(8,128)S(1)} custom-call(f32[1,1,128,128]{3,2,1,0:T(8,128)S(1)} %get-tuple-element.127), custom_call_target="InvertDiagBlocksLowerTriangular" | custom-call | tf_op jit(solution)/shard_map/jit(cholesky)/cholesky | solution.py:882
  377.4 11.7 %custom-call.33 = f32[1,128,128]{2,1,0:T(8,128)S(1)} custom-call(f32[1,128,128]{2,1,0:T(8,128)S(1)} %cholesky.271), custom_call_target="Cholesky" | custom-call | tf_op jit(solution)/shard_map/jit(cholesky)/cholesky | solution.py:882
  389.2 9.8 %custom-call.34 = f32[1,1,128,128]{2,3,1,0:T(8,128)S(1)} custom-call(f32[1,1,128,128]{3,2,1,0:T(8,128)S(1)} %get-tuple-element.124), custom_call_target="InvertDiagBlocksLowerTriangular" | custom-call | tf_op jit(solution)/shard_map/jit(cholesky)/cholesky | solution.py:882
  399.7 11.7 %custom-call.35 = f32[1,128,128]{2,1,0:T(8,128)S(1)} custom-call(f32[1,128,128]{2,1,0:T(8,128)S(1)} %cholesky.276), custom_call_target="Cholesky" | custom-call | tf_op jit(solution)/shard_map/jit(cholesky)/cholesky | solution.py:882
  411.4 10.0 %custom-call.36 = f32[1,1,128,128]{2,3,1,0:T(8,128)S(1)} custom-call(f32[1,1,128,128]{3,2,1,0:T(8,128)S(1)} %get-tuple-element.121), custom_call_target="InvertDiagBlocksLowerTriangular" | custom-call | tf_op jit(solution)/shard_map/jit(cholesky)/cholesky | solution.py:882
  422.0 11.7 %custom-call.37 = f32[1,128,128]{2,1,0:T(8,128)S(1)} custom-call(f32[1,128,128]{2,1,0:T(8,128)S(1)} %fusion.4), custom_call_target="Cholesky" | custom-call | tf_op jit(solution)/shard_map/jit(cholesky)/cholesky | solution.py:882
  455.6 8.2 %shard_map.92.refs_0_ = f32[1,512,512]{2,1,0:T(8,128)} custom-call(bf16[512,512]{1,0:T(8,128)(2,1)} %get-tuple-element.90.high, bf16[512,512]{1,0:T(8,128)(2,1)} %get-tuple-element.91.low, bf16[5,2,512,512]{3,2,1,0:T(8,128)(2,1)} %shard_map.91.bond.p_ref, bf16[5,2,512,512]{3,2,1,0:T(8,128)(2,1)} %get-tuple-element.62.stack.stack_ref), custom_call_target="tpu_custom_call" | custom-call | flops 4831838208 | bytes 16777216 | tf_op jit(solution)/shard_map/pallas_call | solution.py:496
  494.3 8.3 %shard_map.97.refs_1_ = f32[1,512,512]{2,1,0:T(8,128)} custom-call(bf16[512,512]{1,0:T(8,128)(2,1)} %get-tuple-element.95.high, bf16[512,512]{1,0:T(8,128)(2,1)} %get-tuple-element.96.low, bf16[5,2,512,512]{3,2,1,0:T(8,128)(2,1)} %shard_map.91.bond.p_ref, bf16[5,2,512,512]{3,2,1,0:T(8,128)(2,1)} %get-tuple-element.62.stack.stack_ref), custom_call_target="tpu_custom_call" | custom-call | flops 4831838208 | bytes 16777216 | tf_op jit(solution)/shard_map/pallas_call | solution.py:496
  526.1 8.2 %shard_map.99.refs_0_ = f32[1,512,512]{2,1,0:T(8,128)} custom-call(bf16[512,512]{1,0:T(8,128)(2,1)} %get-tuple-element.102.high, bf16[512,512]{1,0:T(8,128)(2,1)} %get-tuple-element.103.low, bf16[5,2,512,512]{3,2,1,0:T(8,128)(2,1)} %shard_map.91.bond.p_ref, bf16[5,2,512,512]{3,2,1,0:T(8,128)(2,1)} %get-tuple-element.62.stack.stack_ref), custom_call_target="tpu_custom_call" | custom-call | flops 4831838208 | bytes 16777216 | tf_op jit(solution)/shard_map/pallas_call | solution.py:496
  (157 shorter events, 284.0 us)
Async XLA Ops:
  7.2 51.5 %all-gather.6.cloned.1.call-start = ((), (), s32[]{:S(2)}) async-start(), calls=%async_computation.6 | async-start | bytes 3932160 | tf_op jit(solution)/shard_map/all_gather | solution.py:30
  9.3 102.9 %all-gather.4.cloned.1.call-start = ((), (), s32[]{:S(2)}) async-start(), calls=%async_computation.5 | async-start | bytes 6553600 | tf_op jit(solution)/shard_map/all_gather | solution.py:30
  13.2 16.5 %collective-permute-start = (f32[512,512]{1,0:T(8,128)}, f32[512,512]{1,0:T(8,128)S(1)}, u32[]{:S(2)}, u32[]{:S(2)}) collective-permute-start(f32[512,512]{1,0:T(8,128)} %get-tuple-element.115), channel_id=1, source_target_pairs={{0,1},{1,2},{2,3},{3,4},{4,5},{5,6},{6,7},{7,8},{8,9},{9,10},{10,1... | collective-permute-start | bytes 3145736 | tf_op jit(solution)/shard_map/ppermute | solution.py:21
  20.0 21.0 %collective-permute-start.1 = (f32[512,512]{1,0:T(8,128)}, f32[512,512]{1,0:T(8,128)S(1)}, u32[]{:S(2)}, u32[]{:S(2)}) collective-permute-start(f32[512,512]{1,0:T(8,128)} %slice_bitcast_fusion), channel_id=1, source_target_pairs={{0,1},{1,2},{2,3},{3,4},{4,5},{5,6},{6,7},{7,8},{8,9},{9,10},{10,1... | collective-permute-start | bytes 3145736 | tf_op jit(solution)/shard_map/ppermute | solution.py:21
  21.9 19.1 %collective-permute-start.2 = (f32[512,512]{1,0:T(8,128)S(1)}, f32[512,512]{1,0:T(8,128)}, u32[]{:S(2)}, u32[]{:S(2)}) collective-permute-start(f32[512,512]{1,0:T(8,128)S(1)} %get-tuple-element.114), channel_id=1, source_target_pairs={{1,0},{2,1},{3,2},{4,3},{5,4},{6,5},{7,6},{8,7},{9,8},{10,9},{11,1... | collective-permute-start | bytes 3145736 | tf_op jit(solution)/shard_map/ppermute | solution.py:26
  24.4 25.3 %collective-permute-start.3 = (f32[512,512]{1,0:T(8,128)}, f32[512,512]{1,0:T(8,128)}, u32[]{:S(2)}, u32[]{:S(2)}) collective-permute-start(f32[512,512]{1,0:T(8,128)} %slice_bitcast_fusion), channel_id=1, source_target_pairs={{1,0},{2,1},{3,2},{4,3},{5,4},{6,5},{7,6},{8,7},{9,8},{10,9},{11,1... | collective-permute-start | bytes 3145736 | tf_op jit(solution)/shard_map/ppermute | solution.py:26
  125.5 54.3 %collective-permute-start.4 = (f32[2,512,512]{2,1,0:T(8,128)}, f32[2,512,512]{2,1,0:T(8,128)S(1)}, u32[]{:S(2)}, u32[]{:S(2)}) collective-permute-start(f32[2,512,512]{2,1,0:T(8,128)} %get-tuple-element.67), channel_id=1, source_target_pairs={{1,0},{2,1},{3,2},{4,3},{5,4},{6,5},{7,6},{8,7},{9,8},{10,9},{11,1... | collective-permute-start | bytes 6291464 | tf_op jit(solution)/shard_map/ppermute | solution.py:26
  128.1 51.7 %collective-permute-start.5 = (f32[2,512,512]{2,1,0:T(8,128)}, f32[2,512,512]{2,1,0:T(8,128)S(1)}, u32[]{:S(2)}, u32[]{:S(2)}) collective-permute-start(f32[2,512,512]{2,1,0:T(8,128)} %get-tuple-element.68), channel_id=1, source_target_pairs={{0,1},{1,2},{2,3},{3,4},{4,5},{5,6},{6,7},{7,8},{8,9},{9,10},{10,1... | collective-permute-start | bytes 6291464 | tf_op jit(solution)/shard_map/ppermute | solution.py:21
  199.7 35.0 %collective-permute-start.6 = (f32[2,512,512]{2,1,0:T(8,128)}, f32[2,512,512]{2,1,0:T(8,128)S(1)}, u32[]{:S(2)}, u32[]{:S(2)}) collective-permute-start(f32[2,512,512]{2,1,0:T(8,128)} %get-tuple-element.77), channel_id=1, source_target_pairs={{1,0},{2,1},{3,2},{4,3},{5,4},{6,5},{7,6},{8,7},{9,8},{10,9},{11,1... | collective-permute-start | bytes 6291464 | tf_op jit(solution)/shard_map/ppermute | solution.py:26
  202.0 32.7 %collective-permute-start.7 = (f32[2,512,512]{2,1,0:T(8,128)}, f32[2,512,512]{2,1,0:T(8,128)}, u32[]{:S(2)}, u32[]{:S(2)}) collective-permute-start(f32[2,512,512]{2,1,0:T(8,128)} %get-tuple-element.72), channel_id=1, source_target_pairs={{0,1},{1,2},{2,3},{3,4},{4,5},{5,6},{6,7},{7,8},{8,9},{9,10},{10,1... | collective-permute-start | bytes 6291464 | tf_op jit(solution)/shard_map/ppermute | solution.py:21
  205.9 26.4 %all-to-all-start.1 = ((f32[32,8,128]{2,1,0:T(8,128)}), f32[32,8,128]{2,1,0:T(8,128)S(1)}, u32[]{:S(2)}, u32[]{:S(2)}) async-start(f32[32,8,128]{2,1,0:T(8,128)} %broadcast_in_dim.25), calls=%async_computation.1 | async-start | bytes 262144 | tf_op jit(solution)/shard_map/all_to_all | solution.py:40
  253.8 27.6 %collective-permute-start.8 = (f32[2,512,512]{2,1,0:T(8,128)}, f32[2,512,512]{2,1,0:T(8,128)S(1)}, u32[]{:S(2)}, u32[]{:S(2)}) collective-permute-start(f32[2,512,512]{2,1,0:T(8,128)} %get-tuple-element.83), channel_id=1, source_target_pairs={{1,0},{2,1},{3,2},{4,3},{5,4},{6,5},{7,6},{8,7},{9,8},{10,9},{11,1... | collective-permute-start | bytes 6291464 | tf_op jit(solution)/shard_map/ppermute | solution.py:26
  256.3 26.3 %collective-permute-start.9 = (f32[2,512,512]{2,1,0:T(8,128)}, f32[2,512,512]{2,1,0:T(8,128)}, u32[]{:S(2)}, u32[]{:S(2)}) collective-permute-start(f32[2,512,512]{2,1,0:T(8,128)} %get-tuple-element.84), channel_id=1, source_target_pairs={{0,1},{1,2},{2,3},{3,4},{4,5},{5,6},{6,7},{7,8},{8,9},{9,10},{10,1... | collective-permute-start | bytes 6291464 | tf_op jit(solution)/shard_map/ppermute | solution.py:21
  294.1 12.4 %collective-permute-start.10 = (f32[2,512,128]{2,1,0:T(8,128)}, f32[2,512,128]{2,1,0:T(8,128)S(1)}, u32[]{:S(2)}, u32[]{:S(2)}) collective-permute-start(f32[2,512,128]{2,1,0:T(8,128)} %get-tuple-element.88), channel_id=1, source_target_pairs={{1,0},{2,1},{3,2},{4,3},{5,4},{6,5},{7,6},{8,7},{9,8},{10,9},{11,1... | collective-permute-start | bytes 1572872 | tf_op jit(solution)/shard_map/ppermute | solution.py:26
  313.4 22.3 %all-to-all-start.2 = ((f32[128,8,128]{2,1,0:T(8,128)}), f32[128,8,128]{2,1,0:T(8,128)S(1)}, u32[]{:S(2)}, u32[]{:S(2)}) async-start(f32[128,8,128]{2,1,0:T(8,128)} %broadcast_in_dim.26), calls=%async_computation.2 | async-start | bytes 1048576 | tf_op jit(solution)/shard_map/all_to_all | solution.py:40
  449.3 16.3 %collective-permute-start.12 = (f32[1,512,512]{2,1,0:T(8,128)}, f32[1,512,512]{2,1,0:T(8,128)S(1)}, u32[]{:S(2)}, u32[]{:S(2)}) collective-permute-start(f32[1,512,512]{2,1,0:T(8,128)} %get-tuple-element.92), channel_id=1, source_target_pairs={{1,0},{2,1},{3,2},{4,3},{5,4},{6,5},{7,6},{8,7},{9,8},{10,9},{11,1... | collective-permute-start | bytes 3145736 | tf_op jit(solution)/shard_map/ppermute | solution.py:26
  452.1 14.8 %collective-permute-start.13 = (f32[1,512,512]{2,1,0:T(8,128)}, f32[1,512,512]{2,1,0:T(8,128)S(1)}, u32[]{:S(2)}, u32[]{:S(2)}) collective-permute-start(f32[1,512,512]{2,1,0:T(8,128)} %get-tuple-element.93), channel_id=1, source_target_pairs={{0,1},{1,2},{2,3},{3,4},{4,5},{5,6},{6,7},{7,8},{8,9},{9,10},{10,1... | collective-permute-start | bytes 3145736 | tf_op jit(solution)/shard_map/ppermute | solution.py:21
  479.4 28.5 %collective-permute-start.14 = (f32[1,512,512]{2,1,0:T(8,128)}, f32[1,512,512]{2,1,0:T(8,128)S(1)}, u32[]{:S(2)}, u32[]{:S(2)}) collective-permute-start(f32[1,512,512]{2,1,0:T(8,128)} %get-tuple-element.100), channel_id=1, source_target_pairs={{1,0},{2,1},{3,2},{4,3},{5,4},{6,5},{7,6},{8,7},{9,8},{10,9},{11,1... | collective-permute-start | bytes 3145736 | tf_op jit(solution)/shard_map/ppermute | solution.py:26
  481.4 26.6 %collective-permute-start.15 = (f32[1,512,512]{2,1,0:T(8,128)}, f32[1,512,512]{2,1,0:T(8,128)S(1)}, u32[]{:S(2)}, u32[]{:S(2)}) collective-permute-start(f32[1,512,512]{2,1,0:T(8,128)} %get-tuple-element.97), channel_id=1, source_target_pairs={{0,1},{1,2},{2,3},{3,4},{4,5},{5,6},{6,7},{7,8},{8,9},{9,10},{10,1... | collective-permute-start | bytes 3145736 | tf_op jit(solution)/shard_map/ppermute | solution.py:21
  486.3 19.3 %all-to-all-start.3 = ((f32[32,8,128]{2,1,0:T(8,128)}), f32[32,8,128]{2,1,0:T(8,128)S(1)}, u32[]{:S(2)}, u32[]{:S(2)}) async-start(f32[32,8,128]{2,1,0:T(8,128)} %broadcast_in_dim.31), calls=%async_computation.3 | async-start | bytes 262144 | tf_op jit(solution)/shard_map/all_to_all | solution.py:40
  520.6 16.3 %collective-permute-start.16 = (f32[1,512,512]{2,1,0:T(8,128)}, f32[1,512,512]{2,1,0:T(8,128)S(1)}, u32[]{:S(2)}, u32[]{:S(2)}) collective-permute-start(f32[1,512,512]{2,1,0:T(8,128)} %get-tuple-element.104), channel_id=1, source_target_pairs={{1,0},{2,1},{3,2},{4,3},{5,4},{6,5},{7,6},{8,7},{9,8},{10,9},{11,1... | collective-permute-start | bytes 3145736 | tf_op jit(solution)/shard_map/ppermute | solution.py:26
  523.1 15.0 %collective-permute-start.17 = (f32[1,512,512]{2,1,0:T(8,128)}, f32[1,512,512]{2,1,0:T(8,128)S(1)}, u32[]{:S(2)}, u32[]{:S(2)}) collective-permute-start(f32[1,512,512]{2,1,0:T(8,128)} %get-tuple-element.105), channel_id=1, source_target_pairs={{0,1},{1,2},{2,3},{3,4},{4,5},{5,6},{6,7},{7,8},{8,9},{9,10},{10,1... | collective-permute-start | bytes 3145736 | tf_op jit(solution)/shard_map/ppermute | solution.py:21
  546.9 11.4 %collective-permute-start.18 = (f32[1,512,128]{2,1,0:T(8,128)}, f32[1,512,128]{2,1,0:T(8,128)S(1)}, u32[]{:S(2)}, u32[]{:S(2)}) collective-permute-start(f32[1,512,128]{2,1,0:T(8,128)} %get-tuple-element.108), channel_id=1, source_target_pairs={{1,0},{2,1},{3,2},{4,3},{5,4},{6,5},{7,6},{8,7},{9,8},{10,9},{11,1... | collective-permute-start | bytes 786440 | tf_op jit(solution)/shard_map/ppermute | solution.py:26
  563.1 21.4 %all-to-all-start.4 = ((f32[128,8,128]{2,1,0:T(8,128)}), f32[128,8,128]{2,1,0:T(8,128)S(1)}, u32[]{:S(2)}, u32[]{:S(2)}) async-start(f32[128,8,128]{2,1,0:T(8,128)} %broadcast_in_dim.32), calls=%async_computation.4 | async-start | bytes 1048576 | tf_op jit(solution)/shard_map/all_to_all | solution.py:40
  (24 other events, 95.5 us)
Sparse Core Ops, SparseCore 0:
  10.2 42.9 all-gather.5
  54.9 57.2 all-gather.3

commit v7 on v6

--- a/solution.py
+++ b/solution.py
@@ -116,27 +116,95 @@
     )(x)
 
 
-def right_kernel(block_ref, stack_ref, up_ref, down_ref):
-    r0, r1, r2, r3, r4 = (block_ref[0, b] for b in range(5))
-    for k, value in enumerate((r0, r4 + r1, r4, r4 - r1, r1)):
-        stack_ref[k, 0], stack_ref[k, 1] = split(value)
+def turned_kernel(place_ref, own_ref, one_ref, two_ref, three_ref, up_ref, down_ref):
     half = ROOT_TWO / 2
-    up_ref[0], up_ref[1] = split(half * r2.T)
-    down_ref[0], down_ref[1] = split(half * r3.T)
-
-
-def right_parts(blocks):
-    count, _, size, width = blocks.shape
-    turned = pl.BlockSpec((2, width, size), lambda i: (0, i, 0))
+    for step, ref in enumerate((own_ref, one_ref, two_ref, three_ref)):
+        owner = lax.rem(place_ref[0] + step, 4)
+        width = ref.shape[1]
+        size = up_ref.shape[2]
+        rows = pl.ds(pl.multiple_of(owner * width, width), width)
+        up_ref[0, rows, :], up_ref[1, rows, :] = split(half * ref[0:size, :].T)
+        down_ref[0, rows, :], down_ref[1, rows, :] = split(half * ref[size : 2 * size, :].T)
+
+
+def turned_parts(place, own, received):
+    size = 4 * own.shape[1]
+    vmem = pl.BlockSpec(memory_space=pltpu.VMEM)
     pair = jax.ShapeDtypeStruct((2, size, size), BF16)
     return pl.pallas_call(
-        right_kernel,
-        grid=(count,),
-        in_specs=[pl.BlockSpec((1, 5, size, width), lambda i: (i, 0, 0, 0))],
-        out_specs=[pl.BlockSpec((5, 2, size, width), lambda i: (0, 0, 0, i)), turned, turned],
-        out_shape=[jax.ShapeDtypeStruct((5, 2, size, size), BF16), pair, pair],
-        compiler_params=params(),
-    )(blocks)
+        turned_kernel,
+        in_specs=[pl.BlockSpec(memory_space=pltpu.SMEM)] + [vmem] * 4,
+        out_specs=[vmem] * 2,
+        out_shape=[pair] * 2,
+        compiler_params=params(),
+    )(place, own, *received)
+
+
+PASSED = (1, 1, 2)
+
+
+def symmetric_kernel(place_ref, own_ref, one_ref, two_ref, three_ref, stack_ref):
+    width = own_ref.shape[2]
+
+    def at(index):
+        return pl.ds(pl.multiple_of(lax.rem(index, 4) * width, width), width)
+
+    def store(row, column, r0, r1, r4):
+        for k, value in enumerate((r0, r4 + r1, r4, r4 - r1, r1)):
+            high, low = split(value)
+            stack_ref[k, 0, at(row), at(column)] = high
+            stack_ref[k, 1, at(row), at(column)] = low
+
+    me = place_ref[0]
+    for step in range(4):
+        blocks = [own_ref[b, at(me + step), :] for b in range(3)]
+        store(me + step, me, *blocks)
+        if step > 0:
+            store(me, me + step, *[block.T for block in blocks])
+    for step, ref in ((1, one_ref), (2, two_ref), (3, three_ref)):
+        owner = me + step
+        other = owner + PASSED[step - 1]
+        first = 8 * width
+        parts = [ref[first + k * width : first + (k + 1) * width, :] for k in range(6)]
+        store(owner, owner, *parts[0::2])
+        blocks = parts[1::2]
+        store(other, owner, *blocks)
+        store(owner, other, *[block.T for block in blocks])
+
+
+def symmetric_parts(place, own, received):
+    size = own.shape[1]
+    vmem = pl.BlockSpec(memory_space=pltpu.VMEM)
+    return pl.pallas_call(
+        symmetric_kernel,
+        in_specs=[pl.BlockSpec(memory_space=pltpu.SMEM)] + [vmem] * 4,
+        out_specs=vmem,
+        out_shape=jax.ShapeDtypeStruct((5, 2, size, size), BF16),
+        compiler_params=params(),
+    )(place, own, *received)
+
+
+def gather_right(place, right):
+    width = right.shape[2]
+    me = place[0]
+    turned = right[2:4]
+    symmetric = jnp.stack([right[0], right[1], right[4]])
+
+    def rows(step):
+        start = ((me + step) % 4) * width
+        return lax.dynamic_slice_in_dim(symmetric, start, width, 1)
+
+    def back(block, step):
+        return lax.ppermute(block, "col", [(d, (d - step) % 4) for d in range(4)])
+
+    flat = turned.reshape(-1, width)
+    messages = [
+        jnp.concatenate([flat, jnp.stack([rows(0), rows(passed)], axis=1).reshape(-1, width)])
+        for passed in PASSED
+    ]
+    got = {step: back(messages[step - 1], step) for step in (1, 3, 2)}
+    received = [got[step] for step in (1, 2, 3)]
+    return flat, symmetric, received
 
 
 def left_kernel(flag_ref, left_ref, bsum_ref, bfour_ref, asum_ref, afour_ref, four_ref, mix_ref):
@@ -788,7 +856,8 @@
     left = left_env[0]
     site_block = site_tensor[:, 0]
     site_full = gather_col(site_block, 0)
-    right_blocks = gather_col(right_env, 0)
+    flat, symmetric, received = gather_right(place, right_env[0])
+    parts = {}
     site_nu = inverse_norm(exchange(norm_row(site_block), ("col", "sec")))
 
     below_four = to_next(left[4])
@@ -796,8 +865,8 @@
     below_sum = to_next(left[0] + left[1] + ANISOTROPY * left[4])
     above_sum = to_previous(left[0] - left[1] + ANISOTROPY * left[4])
     flags = jnp.stack([sector < last, sector > 0]).astype(jnp.int32)
+    flags, site_nu = lax.optimization_barrier((flags, site_nu))
     four, mix = left_parts(flags, left, below_sum, below_four, above_sum, above_four)
-    stack, up, down = right_parts(right_blocks)
     bond = bond_parts(bond_env[0])
 
     def send_sums(sums, after):
@@ -818,15 +887,18 @@
             d, u, z = quarter_call(
                 site_send_quarter,
                 place,
-                [(True, pair[0]), (False, four), (True, up), (True, down)],
+                [(True, pair[0]), (False, four), (True, parts["up"]), (True, parts["down"])],
                 [((2,), f32)] * 2 + [((3,), BF16)],
                 7,
             )
         elif stage == "first":
             zh, zl, ph, pl_part = first_products(pair, four, mix)
+            tied, zh = lax.optimization_barrier((place, zh))
+            parts["up"], parts["down"] = turned_parts(tied, flat, received)
+            parts["stack"] = symmetric_parts(tied, symmetric, received)
             d, u = full_call(
                 site_first_send,
-                [zh, zl, up, down],
+                [zh, zl, parts["up"], parts["down"]],
                 [doubles] * 2,
                 [thirds, thirds, pairs, pairs, doubles, doubles],
                 16,
@@ -835,7 +907,7 @@
         else:
             d, u, zh, zl = full_call(
                 site_send_kernel,
-                [pair[0], pair[1], four, up, down],
+                [pair[0], pair[1], four, parts["up"], parts["down"]],
                 [doubles] * 2 + [thirds] * 2,
                 [thirds, thirds, ((3, 2) + matrix, BF16), pairs, pairs, thirds, thirds]
                 + [doubles] * 2,
@@ -848,14 +920,14 @@
             (local,) = quarter_call(
                 site_local_quarter,
                 place,
-                [(True, pair[0]), (False, mix), (True, stack), (True, z)],
+                [(True, pair[0]), (False, mix), (True, parts["stack"]), (True, z)],
                 [((3,), f32)],
                 13,
             )
         elif stage == "first":
             (local,) = full_call(
                 site_first_local,
-                [ph, pl_part, stack, zh, zl],
+                [ph, pl_part, parts["stack"], zh, zl],
                 [((3,) + matrix, f32)],
                 [thirds, thirds, ((4, 2) + matrix, BF16), thirds, thirds, ((3,) + matrix, f32)],
                 24,
@@ -864,7 +936,7 @@
         else:
             (local,) = full_call(
                 site_local_kernel,
-                [pair[0], pair[1], mix, stack, zh, zl],
+                [pair[0], pair[1], mix, parts["stack"], zh, zl],
                 [((3,) + matrix, f32)],
                 [thirds, thirds, ((7, 2) + matrix, BF16), ((4, 2) + matrix, BF16), thirds, thirds]
                 + [((3,) + matrix, f32)],
@@ -891,14 +963,14 @@
             down_term, up_term = quarter_call(
                 bond_send_quarter,
                 place,
-                [(True, pair[0]), (False, bond), (True, up), (True, down)],
+                [(True, pair[0]), (False, bond), (True, parts["up"]), (True, parts["down"])],
                 [((1,), f32)] * 2,
                 4,
             )
         else:
             down_term, up_term = full_call(
                 bond_send_kernel,
-                [pair[0], pair[1], bond, up, down],
+                [pair[0], pair[1], bond, parts["up"], parts["down"]],
                 [((1,) + matrix, f32)] * 2,
                 [single, single, ((2, 2) + matrix, BF16), pairs, pairs] + [(matrix, f32)] * 2,
                 8,
@@ -910,14 +982,14 @@
             (local,) = quarter_call(
                 bond_local_quarter,
                 place,
-                [(True, pair[0]), (False, bond), (True, stack)],
+                [(True, pair[0]), (False, bond), (True, parts["stack"])],
                 [((1,), f32)],
                 6,
             )
         else:
             (local,) = full_call(
                 bond_local_kernel,
-                [pair[0], pair[1], bond, stack],
+                [pair[0], pair[1], bond, parts["stack"]],
                 [((1,) + matrix, f32)],
                 [single, single, ((3, 2) + matrix, BF16), ((3, 2) + matrix, BF16), (matrix, f32)],
                 9,

time: 608 us -> 581 us (0.956)
  blocking collectives: 35.8 us -> 0 us
  waiting for transfers between devices: 98.8 us -> 75.3 us
  starting transfers between devices: 86.3 us -> 109 us
    all_to_all x1 -> x0, blocking collectives: 35.8 us -> none  [exchange(): return lax.all_to_all(sent, axis, 0, 0)]
    all_gather x2 -> x1, waiting for transfers between devices: 35.2 us -> 18.1 us  [gather_col(): return lax.all_gather(block, 'col', axis=axis, tiled=True)]
    all_to_all x4 -> x5, starting transfers between devices: 28.5 us -> 43.3 us  [exchange(): return lax.all_to_all(sent, axis, 0, 0)]
    ppermute x10, waiting for transfers between devices: 18.2 us -> 5.41 us  [to_next(): return lax.ppermute(block, 'sec', [(i, i + 1) for i in range(count - 1)])]
    all_to_all x4 -> x5, waiting for transfers between devices: 24.5 us -> 32.4 us  [exchange(): return lax.all_to_all(sent, axis, 0, 0)]
    unnamed x47 -> x59, local copies, waits for them, and re-layouts: 18.1 us -> 21.6 us
  transfers between devices with their start and end apart: 26 -> 29, of which waited for: 15 -> 15; matrix products, arithmetic and copies ran while one was open for 2% -> 3% of each run, Pallas kernels for 20% -> 22%
where the time goes in v7:
time: 581 us; the launch traced here: 571 us
  Pallas kernels  240 us (41%)
  starting transfers between devices  109 us (19%)
  other arithmetic  86.4 us (15%)
  waiting for transfers between devices  75.3 us (13%)
  local copies, waits for them, and re-layouts  31 us (5%)
  between operations  18.4 us (3%)
  matrix products  10.2 us (2%)
    pallas_call x12, Pallas kernels, full_call(): pl.pallas_call(kernel, in_specs=[anywhere] * len(operands), out_specs=[an...  108 us
    another operation x14, other arithmetic, body(): factor = jnp.linalg.cholesky(gram[None])[0]  78.6 us
    all_to_all x5, starting transfers between devices, exchange(): return lax.all_to_all(sent, axis, 0, 0)  43.3 us
    ppermute x10, starting transfers between devices, to_next(): return lax.ppermute(block, 'sec', [(i, i + 1) for i in range(count - 1)])  37.3 us
    all_to_all x5, waiting for transfers between devices, exchange(): return lax.all_to_all(sent, axis, 0, 0)  32.4 us
    ppermute x10, starting transfers between devices, to_previous(): return lax.ppermute(block, 'sec', [(i + 1, i) for i in range(count - 1)])  24.8 us
    pallas_call x4, Pallas kernels, combine(): pl.pallas_call(functools.partial(combine_kernel, second, spins), grid=(si...  24.4 us
    unnamed x59, local copies, waits for them, and re-layouts  21.6 us
  transfers between devices with their start and end apart: 29, of which 15 were waited for; matrix products, arithmetic and copies ran while one was open for 3% of the time, Pallas kernels for 22%

profile of v7, /device:TPU:1, one launch (start us, length us, event | category | flops | bytes accessed | tf_op | source)
XLA Modules:
  0.0 570.6 jit_solution(15739153028880504767)
XLA Ops:
  28.8 9.2 %all-to-all-start = ((f32[128,8,128]{2,1,0:T(8,128)}), f32[128,8,128]{2,1,0:T(8,128)S(1)}, u32[]{:S(2)}, u32[]{:S(2)}) async-start(f32[128,8,128]{2,1,0:T(8,128)} %broadcast_in_dim.24), calls=%async_computation | async-start | bytes 1048576 | tf_op jit(solution)/shard_map/all_to_all | solution.py:40
  47.2 8.0 %all-to-all-done.parts_ref = f32[128,8,128]{2,1,0:T(8,128)S(1)} async-done(((f32[128,8,128]{2,1,0:T(8,128)}), f32[128,8,128]{2,1,0:T(8,128)S(1)}, u32[]{:S(2)}, u32[]{:S(2)}) %all-to-all-start) | async-done | bytes 524320 | tf_op jit(solution)/shard_map/all_to_all | solution.py:40
  57.8 9.1 %shard_map.71 = (bf16[3,2,512,512]{3,2,1,0:T(8,128)(2,1)}, bf16[7,2,512,512]{3,2,1,0:T(8,128)(2,1)}) custom-call(s32[2]{0:T(128)} %add_convert_fusion.flag_ref, f32[5,512,512]{2,1,0:T(8,128)} %bitcast.125, f32[512,512]{1,0:T(8,128)} %collective-permute-done.bsum_ref, f32[512,512]{1,0:T(8,128)} %collective-permute-done.1.bfour_ref, ...), custom_call_target="tpu_custom_call" | custom-call | tf_op jit(solution)/shard_map/pallas_call | solution.py:226
  66.9 18.1 %all-gather.3.cloned.1.call-done = f32[512,1,1536]{2,0,1:T(8,128)} async-done(((f32[128,1,1536]{2,0,1:T(8,128)}), f32[512,1,1536]{2,0,1:T(8,128)}) %all-gather.3.cloned.1.call-update) | async-done | bytes 3145744 | tf_op jit(solution)/shard_map/all_gather | solution.py:30
  89.2 13.1 %shard_map.72 = (bf16[3,512,512]{2,1,0:T(8,128)(2,1)}, bf16[3,512,512]{2,1,0:T(8,128)(2,1)}, bf16[3,512,512]{2,1,0:T(8,128)(2,1)}, bf16[3,512,512]{2,1,0:T(8,128)(2,1)}) custom-call(bf16[512,1536]{1,0:T(8,128)(2,1)} %get-tuple-element.60.high, bf16[512,1536]{1,0:T(8,128)(2,1)} %get-tuple-element.61.low, ...), custom_call_target="tpu_custom_call" | custom-call | flops 8053063680 | bytes 16777216 | tf_op jit(solution)/shard_map/pallas_call | solution.py:475
  128.0 8.3 %shard_map.74.refs_0_ = f32[3,512,512]{2,1,0:T(8,128)} custom-call(bf16[3,512,512]{2,1,0:T(8,128)(2,1)} %get-tuple-element.65.ph, bf16[3,512,512]{2,1,0:T(8,128)(2,1)} %get-tuple-element.66.pl_in, bf16[5,2,512,512]{3,2,1,0:T(8,128)(2,1)} %shard_map.73.stack.stack_ref, bf16[3,512,512]{2,1,0:T(8,128)(2,1)} %get-tuple-element.69.zh, ...), custom_call_target="tpu_custom_call" | custom-call | flops 4831838208 | bytes 16777216 | tf_op jit(solution)/shard_map/pallas_call | solution.py:564
  136.3 8.0 %collective-permute-done.7.refs_1_ = f32[2,512,512]{2,1,0:T(8,128)S(1)} collective-permute-done((f32[2,512,512]{2,1,0:T(8,128)}, f32[2,512,512]{2,1,0:T(8,128)S(1)}, u32[]{:S(2)}, u32[]{:S(2)}) %collective-permute-start.7) | collective-permute-done | bytes 2097184 | tf_op jit(solution)/shard_map/ppermute | solution.py:26
  154.6 9.4 %shard_map.78 = (f32[2,512,512]{2,1,0:T(8,128)}, f32[2,512,512]{2,1,0:T(8,128)}, bf16[3,512,512]{2,1,0:T(8,128)(2,1)}, bf16[3,512,512]{2,1,0:T(8,128)(2,1)}) custom-call(bf16[512,1536]{1,0:T(8,128)(2,1)} %get-tuple-element.76.high, bf16[512,1536]{1,0:T(8,128)(2,1)} %get-tuple-element.77.low, bf16[3,2,512,512]{3,2,1,0:T(8,128)(2,1)} %get-tuple-element.63.four_ref.four, ...), custom_call_target="tpu_custom_call" | custom-call | flops 5637144576 | bytes 16777216 | tf_op jit(solution)/shard_map/pallas_call | solution.py:564
  170.9 11.2 %all-to-all-start.1 = ((f32[32,8,128]{2,1,0:T(8,128)}), f32[32,8,128]{2,1,0:T(8,128)S(1)}, u32[]{:S(2)}, u32[]{:S(2)}) async-start(f32[32,8,128]{2,1,0:T(8,128)} %broadcast_in_dim.25), calls=%async_computation.1 | async-start | bytes 262144 | tf_op jit(solution)/shard_map/all_to_all | solution.py:40
  182.2 14.6 %shard_map.80.refs_1_ = f32[3,512,512]{2,1,0:T(8,128)} custom-call(bf16[512,1536]{1,0:T(8,128)(2,1)} %get-tuple-element.76.high, bf16[512,1536]{1,0:T(8,128)(2,1)} %get-tuple-element.77.low, bf16[7,2,512,512]{3,2,1,0:T(8,128)(2,1)} %get-tuple-element.64.mix_ref.mix, bf16[5,2,512,512]{3,2,1,0:T(8,128)(2,1)} %shard_map.73.stack.stack_ref, ...), custom_call_target="tpu_custom_call" | custom-call | flops 10468982784 | bytes 16777216 | tf_op jit(solution)/shard_map/pallas_call | solution.py:564
  207.9 8.4 %shard_map.81 = (f32[512,1536]{1,0:T(8,128)}, bf16[512,1536]{1,0:T(8,128)(2,1)}, bf16[512,1536]{1,0:T(8,128)(2,1)}) custom-call(f32[8,128]{1,0:T(8,128)} %shard_map.79.scale_ref, f32[512,1536]{1,0:T(8,128)} %get-tuple-element.80.w_ref.refs_3_.refs_4_.refs_5_.refs_1_, f32[512,1536]{1,0:T(8,128)} %bitcast.119, f32[3,512,512]{2,1,0:T(8,128)} %shard_map.80.refs_1_, ...), custom_call_target="tpu_custom_call" | custom-call | tf_op jit(solution)/shard_map/pallas_call | solution.py:664
  216.3 9.4 %shard_map.82 = (f32[2,512,512]{2,1,0:T(8,128)}, f32[2,512,512]{2,1,0:T(8,128)}, bf16[3,512,512]{2,1,0:T(8,128)(2,1)}, bf16[3,512,512]{2,1,0:T(8,128)(2,1)}) custom-call(bf16[512,1536]{1,0:T(8,128)(2,1)} %get-tuple-element.85.high, bf16[512,1536]{1,0:T(8,128)(2,1)} %get-tuple-element.86.low, bf16[3,2,512,512]{3,2,1,0:T(8,128)(2,1)} %get-tuple-element.63.four_ref.four, ...), custom_call_target="tpu_custom_call" | custom-call | flops 5637144576 | bytes 16777216 | tf_op jit(solution)/shard_map/pallas_call | solution.py:564
  231.5 14.6 %shard_map.83.refs_0_ = f32[3,512,512]{2,1,0:T(8,128)} custom-call(bf16[512,1536]{1,0:T(8,128)(2,1)} %get-tuple-element.85.high, bf16[512,1536]{1,0:T(8,128)(2,1)} %get-tuple-element.86.low, bf16[7,2,512,512]{3,2,1,0:T(8,128)(2,1)} %get-tuple-element.64.mix_ref.mix, bf16[5,2,512,512]{3,2,1,0:T(8,128)(2,1)} %shard_map.73.stack.stack_ref, ...), custom_call_target="tpu_custom_call" | custom-call | flops 10468982784 | bytes 16777216 | tf_op jit(solution)/shard_map/pallas_call | solution.py:564
  326.4 11.7 %custom-call.31 = f32[1,128,128]{2,1,0:T(8,128)S(1)} custom-call(f32[1,128,128]{2,1,0:T(8,128)S(1)} %cholesky.267), custom_call_target="Cholesky" | custom-call | tf_op jit(solution)/shard_map/jit(cholesky)/cholesky | solution.py:954
  338.3 9.8 %custom-call.32 = f32[1,1,128,128]{2,3,1,0:T(8,128)S(1)} custom-call(f32[1,1,128,128]{3,2,1,0:T(8,128)S(1)} %get-tuple-element.141), custom_call_target="InvertDiagBlocksLowerTriangular" | custom-call | tf_op jit(solution)/shard_map/jit(cholesky)/cholesky | solution.py:954
  349.2 11.7 %custom-call.33 = f32[1,128,128]{2,1,0:T(8,128)S(1)} custom-call(f32[1,128,128]{2,1,0:T(8,128)S(1)} %cholesky.271), custom_call_target="Cholesky" | custom-call | tf_op jit(solution)/shard_map/jit(cholesky)/cholesky | solution.py:954
  361.0 9.8 %custom-call.34 = f32[1,1,128,128]{2,3,1,0:T(8,128)S(1)} custom-call(f32[1,1,128,128]{3,2,1,0:T(8,128)S(1)} %get-tuple-element.138), custom_call_target="InvertDiagBlocksLowerTriangular" | custom-call | tf_op jit(solution)/shard_map/jit(cholesky)/cholesky | solution.py:954
  371.5 11.7 %custom-call.35 = f32[1,128,128]{2,1,0:T(8,128)S(1)} custom-call(f32[1,128,128]{2,1,0:T(8,128)S(1)} %cholesky.276), custom_call_target="Cholesky" | custom-call | tf_op jit(solution)/shard_map/jit(cholesky)/cholesky | solution.py:954
  383.2 10.0 %custom-call.36 = f32[1,1,128,128]{2,3,1,0:T(8,128)S(1)} custom-call(f32[1,1,128,128]{3,2,1,0:T(8,128)S(1)} %get-tuple-element.135), custom_call_target="InvertDiagBlocksLowerTriangular" | custom-call | tf_op jit(solution)/shard_map/jit(cholesky)/cholesky | solution.py:954
  393.8 11.7 %custom-call.37 = f32[1,128,128]{2,1,0:T(8,128)S(1)} custom-call(f32[1,128,128]{2,1,0:T(8,128)S(1)} %fusion.4), custom_call_target="Cholesky" | custom-call | tf_op jit(solution)/shard_map/jit(cholesky)/cholesky | solution.py:954
  427.5 8.3 %shard_map.93.refs_0_ = f32[1,512,512]{2,1,0:T(8,128)} custom-call(bf16[512,512]{1,0:T(8,128)(2,1)} %get-tuple-element.96.high, bf16[512,512]{1,0:T(8,128)(2,1)} %get-tuple-element.97.low, bf16[5,2,512,512]{3,2,1,0:T(8,128)(2,1)} %shard_map.92.bond.p_ref, bf16[5,2,512,512]{3,2,1,0:T(8,128)(2,1)} %shard_map.73.stack.stack_ref), custom_call_target="tpu_custom_call" | custom-call | flops 4831838208 | bytes 16777216 | tf_op jit(solution)/shard_map/pallas_call | solution.py:564
  458.3 8.0 %all-to-all-start.3 = ((f32[32,8,128]{2,1,0:T(8,128)}), f32[32,8,128]{2,1,0:T(8,128)S(1)}, u32[]{:S(2)}, u32[]{:S(2)}) async-start(f32[32,8,128]{2,1,0:T(8,128)} %broadcast_in_dim.31), calls=%async_computation.3 | async-start | bytes 262144 | tf_op jit(solution)/shard_map/all_to_all | solution.py:40
  466.3 8.3 %shard_map.98.refs_1_ = f32[1,512,512]{2,1,0:T(8,128)} custom-call(bf16[512,512]{1,0:T(8,128)(2,1)} %get-tuple-element.101.high, bf16[512,512]{1,0:T(8,128)(2,1)} %get-tuple-element.102.low, bf16[5,2,512,512]{3,2,1,0:T(8,128)(2,1)} %shard_map.92.bond.p_ref, bf16[5,2,512,512]{3,2,1,0:T(8,128)(2,1)} %shard_map.73.stack.stack_ref), custom_call_target="tpu_custom_call" | custom-call | flops 4831838208 | bytes 16777216 | tf_op jit(solution)/shard_map/pallas_call | solution.py:564
  498.0 8.3 %shard_map.100.refs_0_ = f32[1,512,512]{2,1,0:T(8,128)} custom-call(bf16[512,512]{1,0:T(8,128)(2,1)} %get-tuple-element.108.high, bf16[512,512]{1,0:T(8,128)(2,1)} %get-tuple-element.109.low, bf16[5,2,512,512]{3,2,1,0:T(8,128)(2,1)} %shard_map.92.bond.p_ref, bf16[5,2,512,512]{3,2,1,0:T(8,128)(2,1)} %shard_map.73.stack.stack_ref), custom_call_target="tpu_custom_call" | custom-call | flops 4831838208 | bytes 16777216 | tf_op jit(solution)/shard_map/pallas_call | solution.py:564
  (180 shorter events, 301.5 us)
Async XLA Ops:
  7.2 77.8 %all-gather.3.cloned.1.call-start = ((), (), s32[]{:S(2)}) async-start(), calls=%async_computation.5 | async-start | bytes 3932160 | tf_op jit(solution)/shard_map/all_gather | solution.py:30
  12.9 32.9 %collective-permute-start = (f32[512,512]{1,0:T(8,128)}, f32[512,512]{1,0:T(8,128)}, u32[]{:S(2)}, u32[]{:S(2)}) collective-permute-start(f32[512,512]{1,0:T(8,128)} %get-tuple-element.119), channel_id=1, source_target_pairs={{0,1},{1,2},{2,3},{3,4},{4,5},{5,6},{6,7},{7,8},{8,9},{9,10},{10,1... | collective-permute-start | bytes 3145736 | tf_op jit(solution)/shard_map/ppermute | solution.py:21
  19.9 26.0 %collective-permute-start.1 = (f32[512,512]{1,0:T(8,128)}, f32[512,512]{1,0:T(8,128)}, u32[]{:S(2)}, u32[]{:S(2)}) collective-permute-start(f32[512,512]{1,0:T(8,128)} %slice_bitcast_fusion), channel_id=1, source_target_pairs={{0,1},{1,2},{2,3},{3,4},{4,5},{5,6},{6,7},{7,8},{8,9},{9,10},{10,1... | collective-permute-start | bytes 3145736 | tf_op jit(solution)/shard_map/ppermute | solution.py:21
  21.8 36.0 %collective-permute-start.3 = (f32[512,512]{1,0:T(8,128)}, f32[512,512]{1,0:T(8,128)}, u32[]{:S(2)}, u32[]{:S(2)}) collective-permute-start(f32[512,512]{1,0:T(8,128)} %slice_bitcast_fusion), channel_id=1, source_target_pairs={{1,0},{2,1},{3,2},{4,3},{5,4},{6,5},{7,6},{8,7},{9,8},{10,9},{11,1... | collective-permute-start | bytes 3145736 | tf_op jit(solution)/shard_map/ppermute | solution.py:26
  28.8 26.5 %all-to-all-start = ((f32[128,8,128]{2,1,0:T(8,128)}), f32[128,8,128]{2,1,0:T(8,128)S(1)}, u32[]{:S(2)}, u32[]{:S(2)}) async-start(f32[128,8,128]{2,1,0:T(8,128)} %broadcast_in_dim.24), calls=%async_computation | async-start | bytes 1048576 | tf_op jit(solution)/shard_map/all_to_all | solution.py:40
  38.0 19.9 %collective-permute-start.2 = (f32[512,512]{1,0:T(8,128)}, f32[512,512]{1,0:T(8,128)}, u32[]{:S(2)}, u32[]{:S(2)}) collective-permute-start(f32[512,512]{1,0:T(8,128)} %get-tuple-element.118), channel_id=1, source_target_pairs={{1,0},{2,1},{3,2},{4,3},{5,4},{6,5},{7,6},{8,7},{9,8},{10,9},{11,1... | collective-permute-start | bytes 3145736 | tf_op jit(solution)/shard_map/ppermute | solution.py:26
  43.2 59.2 %collective-permute-start.4 = (f32[1792,128]{1,0:T(8,128)}, f32[1792,128]{1,0:T(8,128)S(1)}, u32[]{:S(2)}, u32[]{:S(2)}) collective-permute-start(f32[1792,128]{1,0:T(8,128)} %get-tuple-element.129), channel_id=1, source_target_pairs={{0,96},{32,0},{64,32},{96,64},{1,97},{33,1},{65,33},{97,65},{2,98}... | collective-permute-start | bytes 2752520 | tf_op jit(solution)/shard_map/ppermute | solution.py:198
  45.8 56.6 %collective-permute-start.5 = (f32[1792,128]{1,0:T(8,128)}, f32[1792,128]{1,0:T(8,128)S(1)}, u32[]{:S(2)}, u32[]{:S(2)}) collective-permute-start(f32[1792,128]{1,0:T(8,128)} %get-tuple-element.129), channel_id=1, source_target_pairs={{0,64},{32,96},{64,0},{96,32},{1,65},{33,97},{65,1},{97,33},{2,66}... | collective-permute-start | bytes 2752520 | tf_op jit(solution)/shard_map/ppermute | solution.py:198
  45.9 56.5 %collective-permute-start.6 = (f32[1792,128]{1,0:T(8,128)}, f32[1792,128]{1,0:T(8,128)S(1)}, u32[]{:S(2)}, u32[]{:S(2)}) collective-permute-start(f32[1792,128]{1,0:T(8,128)} %get-tuple-element.128), channel_id=1, source_target_pairs={{0,32},{32,64},{64,96},{96,0},{1,33},{33,65},{65,97},{97,1},{2,34}... | collective-permute-start | bytes 2752520 | tf_op jit(solution)/shard_map/ppermute | solution.py:198
  115.1 29.2 %collective-permute-start.7 = (f32[2,512,512]{2,1,0:T(8,128)}, f32[2,512,512]{2,1,0:T(8,128)S(1)}, u32[]{:S(2)}, u32[]{:S(2)}) collective-permute-start(f32[2,512,512]{2,1,0:T(8,128)} %get-tuple-element.73), channel_id=1, source_target_pairs={{1,0},{2,1},{3,2},{4,3},{5,4},{6,5},{7,6},{8,7},{9,8},{10,9},{11,1... | collective-permute-start | bytes 6291464 | tf_op jit(solution)/shard_map/ppermute | solution.py:26
  118.2 27.4 %collective-permute-start.8 = (f32[2,512,512]{2,1,0:T(8,128)}, f32[2,512,512]{2,1,0:T(8,128)S(1)}, u32[]{:S(2)}, u32[]{:S(2)}) collective-permute-start(f32[2,512,512]{2,1,0:T(8,128)} %get-tuple-element.74), channel_id=1, source_target_pairs={{0,1},{1,2},{2,3},{3,4},{4,5},{5,6},{6,7},{7,8},{8,9},{9,10},{10,1... | collective-permute-start | bytes 6291464 | tf_op jit(solution)/shard_map/ppermute | solution.py:21
  164.1 42.6 %collective-permute-start.9 = (f32[2,512,512]{2,1,0:T(8,128)}, f32[2,512,512]{2,1,0:T(8,128)S(1)}, u32[]{:S(2)}, u32[]{:S(2)}) collective-permute-start(f32[2,512,512]{2,1,0:T(8,128)} %get-tuple-element.83), channel_id=1, source_target_pairs={{1,0},{2,1},{3,2},{4,3},{5,4},{6,5},{7,6},{8,7},{9,8},{10,9},{11,1... | collective-permute-start | bytes 6291464 | tf_op jit(solution)/shard_map/ppermute | solution.py:26
  166.0 40.6 %collective-permute-start.10 = (f32[2,512,512]{2,1,0:T(8,128)}, f32[2,512,512]{2,1,0:T(8,128)}, u32[]{:S(2)}, u32[]{:S(2)}) collective-permute-start(f32[2,512,512]{2,1,0:T(8,128)} %get-tuple-element.78), channel_id=1, source_target_pairs={{0,1},{1,2},{2,3},{3,4},{4,5},{5,6},{6,7},{7,8},{8,9},{9,10},{10,1... | collective-permute-start | bytes 6291464 | tf_op jit(solution)/shard_map/ppermute | solution.py:21
  170.9 33.4 %all-to-all-start.1 = ((f32[32,8,128]{2,1,0:T(8,128)}), f32[32,8,128]{2,1,0:T(8,128)S(1)}, u32[]{:S(2)}, u32[]{:S(2)}) async-start(f32[32,8,128]{2,1,0:T(8,128)} %broadcast_in_dim.25), calls=%async_computation.1 | async-start | bytes 262144 | tf_op jit(solution)/shard_map/all_to_all | solution.py:40
  225.8 27.6 %collective-permute-start.11 = (f32[2,512,512]{2,1,0:T(8,128)}, f32[2,512,512]{2,1,0:T(8,128)S(1)}, u32[]{:S(2)}, u32[]{:S(2)}) collective-permute-start(f32[2,512,512]{2,1,0:T(8,128)} %get-tuple-element.89), channel_id=1, source_target_pairs={{1,0},{2,1},{3,2},{4,3},{5,4},{6,5},{7,6},{8,7},{9,8},{10,9},{11,1... | collective-permute-start | bytes 6291464 | tf_op jit(solution)/shard_map/ppermute | solution.py:26
  228.1 26.5 %collective-permute-start.12 = (f32[2,512,512]{2,1,0:T(8,128)}, f32[2,512,512]{2,1,0:T(8,128)S(1)}, u32[]{:S(2)}, u32[]{:S(2)}) collective-permute-start(f32[2,512,512]{2,1,0:T(8,128)} %get-tuple-element.90), channel_id=1, source_target_pairs={{0,1},{1,2},{2,3},{3,4},{4,5},{5,6},{6,7},{7,8},{8,9},{9,10},{10,1... | collective-permute-start | bytes 6291464 | tf_op jit(solution)/shard_map/ppermute | solution.py:21
  286.6 20.9 %all-to-all-start.2 = ((f32[128,8,128]{2,1,0:T(8,128)}), f32[128,8,128]{2,1,0:T(8,128)S(1)}, u32[]{:S(2)}, u32[]{:S(2)}) async-start(f32[128,8,128]{2,1,0:T(8,128)} %broadcast_in_dim.26), calls=%async_computation.2 | async-start | bytes 1048576 | tf_op jit(solution)/shard_map/all_to_all | solution.py:40
  421.3 16.3 %collective-permute-start.15 = (f32[1,512,512]{2,1,0:T(8,128)}, f32[1,512,512]{2,1,0:T(8,128)S(1)}, u32[]{:S(2)}, u32[]{:S(2)}) collective-permute-start(f32[1,512,512]{2,1,0:T(8,128)} %get-tuple-element.98), channel_id=1, source_target_pairs={{1,0},{2,1},{3,2},{4,3},{5,4},{6,5},{7,6},{8,7},{9,8},{10,9},{11,1... | collective-permute-start | bytes 3145736 | tf_op jit(solution)/shard_map/ppermute | solution.py:26
  451.4 28.5 %collective-permute-start.17 = (f32[1,512,512]{2,1,0:T(8,128)}, f32[1,512,512]{2,1,0:T(8,128)S(1)}, u32[]{:S(2)}, u32[]{:S(2)}) collective-permute-start(f32[1,512,512]{2,1,0:T(8,128)} %get-tuple-element.106), channel_id=1, source_target_pairs={{1,0},{2,1},{3,2},{4,3},{5,4},{6,5},{7,6},{8,7},{9,8},{10,9},{11,1... | collective-permute-start | bytes 3145736 | tf_op jit(solution)/shard_map/ppermute | solution.py:26
  453.3 26.6 %collective-permute-start.18 = (f32[1,512,512]{2,1,0:T(8,128)}, f32[1,512,512]{2,1,0:T(8,128)S(1)}, u32[]{:S(2)}, u32[]{:S(2)}) collective-permute-start(f32[1,512,512]{2,1,0:T(8,128)} %get-tuple-element.103), channel_id=1, source_target_pairs={{0,1},{1,2},{2,3},{3,4},{4,5},{5,6},{6,7},{7,8},{8,9},{9,10},{10,1... | collective-permute-start | bytes 3145736 | tf_op jit(solution)/shard_map/ppermute | solution.py:21
  458.3 19.3 %all-to-all-start.3 = ((f32[32,8,128]{2,1,0:T(8,128)}), f32[32,8,128]{2,1,0:T(8,128)S(1)}, u32[]{:S(2)}, u32[]{:S(2)}) async-start(f32[32,8,128]{2,1,0:T(8,128)} %broadcast_in_dim.31), calls=%async_computation.3 | async-start | bytes 262144 | tf_op jit(solution)/shard_map/all_to_all | solution.py:40
  492.4 16.3 %collective-permute-start.19 = (f32[1,512,512]{2,1,0:T(8,128)}, f32[1,512,512]{2,1,0:T(8,128)S(1)}, u32[]{:S(2)}, u32[]{:S(2)}) collective-permute-start(f32[1,512,512]{2,1,0:T(8,128)} %get-tuple-element.110), channel_id=1, source_target_pairs={{1,0},{2,1},{3,2},{4,3},{5,4},{6,5},{7,6},{8,7},{9,8},{10,9},{11,1... | collective-permute-start | bytes 3145736 | tf_op jit(solution)/shard_map/ppermute | solution.py:26
  495.0 15.0 %collective-permute-start.20 = (f32[1,512,512]{2,1,0:T(8,128)}, f32[1,512,512]{2,1,0:T(8,128)S(1)}, u32[]{:S(2)}, u32[]{:S(2)}) collective-permute-start(f32[1,512,512]{2,1,0:T(8,128)} %get-tuple-element.111), channel_id=1, source_target_pairs={{0,1},{1,2},{2,3},{3,4},{4,5},{5,6},{6,7},{7,8},{8,9},{9,10},{10,1... | collective-permute-start | bytes 3145736 | tf_op jit(solution)/shard_map/ppermute | solution.py:21
  535.1 21.4 %all-to-all-start.4 = ((f32[128,8,128]{2,1,0:T(8,128)}), f32[128,8,128]{2,1,0:T(8,128)S(1)}, u32[]{:S(2)}, u32[]{:S(2)}) async-start(f32[128,8,128]{2,1,0:T(8,128)} %broadcast_in_dim.32), calls=%async_computation.4 | async-start | bytes 1048576 | tf_op jit(solution)/shard_map/all_to_all | solution.py:40
  (33 other events, 142.4 us)
Sparse Core Ops, SparseCore 0:
  10.2 74.6 all-gather.2
